TPU v7x, 32 devices: a whole 2x2x4 slice. The times are simulated.
32 devices in a mesh: tok: 8 (over z, y), mp: 4 (over x, core).
Axes of the slice: x: 2, y: 2, z: 4, core: 2. Of those that a mesh axis runs over, the one named last changes fastest.
Arguments:
- inputs: bfloat16 [8192, 2560], P(('tok', 'mp')), may hold values from -40 to 40
- grad_output: bfloat16 [8192, 2560], P(('tok', 'mp')), may hold values from -6 to 6
- segments: int32 [8192], replicated, may hold values from 0 to 4, as said below
- attention_gain: bfloat16 [2560], P('tok'), may hold values from 0.25 to 1.75
- query_weight: bfloat16 [2560, 2560], P('tok', 'mp'), may hold values from -0.125 to 0.125
- key_matrix: bfloat16 [2560, 640], P('tok', 'mp'), may hold values from -0.15625 to 0.15625
- value_matrix: bfloat16 [2560, 640], P('tok', 'mp'), may hold values from -0.125 to 0.125
- output_weight: bfloat16 [2560, 2560], P('mp', 'tok'), may hold values from -1 to 1
- feedforward_gain: bfloat16 [2560], P('tok'), may hold values from 0.25 to 1.75
- gate_weight: bfloat16 [2560, 7168], P('tok', 'mp'), may hold values from -0.125 to 0.125
- up_weight: bfloat16 [2560, 7168], P('tok', 'mp'), may hold values from -0.125 to 0.125
- down_weight: bfloat16 [7168, 2560], P('mp', 'tok'), may hold values from -0.09375 to 0.09375
Outputs:
- layer_output: bfloat16 [8192, 2560], P(('tok', 'mp'))
- input_gradient: float32 [8192, 2560], P(('tok', 'mp'))
- attention_gain_gradient: float32 [2560], P('tok')
- query_weight_gradient: float32 [2560, 2560], P('tok', 'mp')
- key_weight_gradient: float32 [2560, 640], P('tok', 'mp')
- value_weight_gradient: float32 [2560, 640], P('tok', 'mp')
- output_weight_gradient: float32 [2560, 2560], P('mp', 'tok')
- feedforward_gain_gradient: float32 [2560], P('tok')
- gate_weight_gradient: float32 [2560, 7168], P('tok', 'mp')
- up_weight_gradient: float32 [2560, 7168], P('tok', 'mp')
- down_weight_gradient: float32 [7168, 2560], P('mp', 'tok')
Inputs may be any that keep to these rules, and one draw needn't show every extreme that they name: `segments`: document numbers never fall along the tokens and start at 0; document 2 begins within the first 512 tokens and ends within the last 512 tokens; the other documents lie in those ends.
All inputs are finite; a program needn't handle non-finite values.
Results may differ from a plain program's by a relative error of at most 0.025.
Values may be sent and summed in bfloat16 or wider, within the bound.
A program may use at most 256 MiB of HBM per device.

v0:
```python
import jax
import jax.numpy as jnp
from jax import lax
from jax.sharding import PartitionSpec as P

HEAD_SIZE = 80
WINDOW_LENGTH = 512


EPS = 1e-05
THETA = 1000000.0
FLOOR = -1e30


def passed_along(value, axis, steps):
    count = lax.axis_size(axis)
    leading, last = (max(0, -steps), min(count, count - steps))
    return lax.ppermute(value, axis, [(source, source + steps) for source in range(leading, last)])


def rope_tables(count, first, width):
    places = (first + jnp.arange(count, dtype=jnp.int32)).astype(jnp.float32)
    freqs = THETA ** (-(jnp.arange(width // 2, dtype=jnp.int32).astype(jnp.float32) * 2.0 / width))
    angles = places[:, None] * freqs[None, :]
    angles = jnp.concatenate([angles, angles], axis=1)
    return (jnp.cos(angles), jnp.sin(angles))


def turn(value_states, cosine, sine):
    half = value_states.shape[-1] // 2
    swapped = jnp.concatenate([-value_states[..., half:], value_states[..., :half]], axis=-1)
    return value_states * cosine[:, None, :] + swapped * sine[:, None, :]


def turn_back(grads, cosine, sine):
    half = grads.shape[-1] // 2
    scaled = grads * sine[:, None, :]
    return grads * cosine[:, None, :] + jnp.concatenate(
        [scaled[..., half:], -scaled[..., :half]], axis=-1
    )


def normalize(value_states, gain):
    inverse = lax.rsqrt(jnp.mean(value_states * value_states, axis=-1, keepdims=True) + EPS)
    return (value_states * inverse * gain.astype(jnp.float32), inverse)


def norm_back(grads, value_states, inverse, gain):
    normalized_input = value_states * inverse
    dnormed = grads * gain.astype(jnp.float32)
    back = inverse * (
        dnormed - normalized_input * jnp.mean(dnormed * normalized_input, axis=-1, keepdims=True)
    )
    return (back, jnp.sum(grads * normalized_input, axis=0))


def outer_product(left, right):
    return lax.dot_general(
        left, right, (((0,), (0,)), ((), ())), preferred_element_type=jnp.float32
    )


def times_transposed(left, right):
    return lax.dot_general(
        left, right, (((1,), (1,)), ((), ())), preferred_element_type=jnp.float32
    )


def block_scores(query_states, key_states, key_ids, start_index, head, block_rows):
    head_group = query_states.shape[2]
    width = query_states.shape[3]
    query_tile_rows = lax.dynamic_slice(
        query_states, (start_index, head, 0, 0), (block_rows, 1, head_group, width)
    )[:, 0]
    key_block = lax.dynamic_slice(
        key_states, (start_index, head, 0), (block_rows + WINDOW_LENGTH, 1, width)
    )[:, 0]
    ids = lax.dynamic_slice_in_dim(key_ids, start_index, block_rows + WINDOW_LENGTH, 0)
    query_ids = lax.dynamic_slice_in_dim(key_ids, start_index + WINDOW_LENGTH, block_rows, 0)
    scores = jnp.einsum(
        "qrd,kd->rqk", query_tile_rows, key_block, preferred_element_type=jnp.float32
    ) * HEAD_SIZE ** (-0.5)
    distance = (
        jnp.arange(block_rows)[:, None]
        + WINDOW_LENGTH
        - jnp.arange(block_rows + WINDOW_LENGTH)[None, :]
    )
    allowed = (distance >= 0) & (distance < WINDOW_LENGTH) & (query_ids[:, None] == ids[None, :])
    return (jnp.where(allowed, scores, FLOOR), query_tile_rows, key_block)


def attend(query_states, key_states, value_states, key_ids):
    length, kheads, head_group, width = query_states.shape
    block_rows = min(length, 512)
    turns = length // block_rows * kheads

    def advance(turn_index, carry):
        out_buffer, lse_buffer = carry
        start_index = turn_index // kheads * block_rows
        head = turn_index % kheads
        scores, query_tile_rows, key_block = block_scores(
            query_states, key_states, key_ids, start_index, head, block_rows
        )
        value_block = lax.dynamic_slice(
            value_states, (start_index, head, 0), (block_rows + WINDOW_LENGTH, 1, width)
        )[:, 0]
        peak = jnp.max(scores, axis=-1, keepdims=True)
        lse = peak + jnp.log(jnp.sum(jnp.exp(scores - peak), axis=-1, keepdims=True))
        probs = jnp.exp(scores - lse).astype(jnp.bfloat16)
        result = jnp.einsum("rqk,kd->qrd", probs, value_block, preferred_element_type=jnp.float32)
        out_buffer = lax.dynamic_update_slice(
            out_buffer, result.astype(jnp.bfloat16)[:, None], (start_index, head, 0, 0)
        )
        lse_buffer = lax.dynamic_update_slice(
            lse_buffer, lse[None, :, :, 0], (head, 0, start_index)
        )
        return (out_buffer, lse_buffer)

    initial = (
        jnp.zeros(query_states.shape, jnp.bfloat16),
        jnp.zeros((kheads, head_group, length), jnp.float32),
    )
    return lax.fori_loop(0, turns, advance, initial)


def attend_back(query_states, key_states, value_states, key_ids, lses, dattended):
    length, kheads, head_group, width = query_states.shape
    block_rows = min(length, 512)
    turns = length // block_rows * kheads

    def advance(turn_index, carry):
        dquery_buffer, dkey_buffer, dvalue_buffer = carry
        start_index = turn_index // kheads * block_rows
        head = turn_index % kheads
        scores, query_tile_rows, key_block = block_scores(
            query_states, key_states, key_ids, start_index, head, block_rows
        )
        value_block = lax.dynamic_slice(
            value_states, (start_index, head, 0), (block_rows + WINDOW_LENGTH, 1, width)
        )[:, 0]
        lse = lax.dynamic_slice(lses, (head, 0, start_index), (1, head_group, block_rows))[0]
        probs = jnp.exp(scores - lse[:, :, None])
        dout_block = lax.dynamic_slice(
            dattended, (start_index, head, 0, 0), (block_rows, 1, head_group, width)
        )[:, 0]
        dprobs = jnp.einsum(
            "qrd,kd->rqk", dout_block, value_block, preferred_element_type=jnp.float32
        )
        dvalue_part = jnp.einsum(
            "rqk,qrd->kd",
            probs.astype(jnp.bfloat16),
            dout_block,
            preferred_element_type=jnp.float32,
        )
        inner = jnp.sum(probs * dprobs, axis=-1, keepdims=True)
        dscores = (probs * (dprobs - inner)).astype(jnp.bfloat16)
        dquery_part = jnp.einsum(
            "rqk,kd->qrd", dscores, key_block, preferred_element_type=jnp.float32
        ) * HEAD_SIZE ** (-0.5)
        dkey_part = jnp.einsum(
            "rqk,qrd->kd", dscores, query_tile_rows, preferred_element_type=jnp.float32
        ) * HEAD_SIZE ** (-0.5)
        dquery_buffer = lax.dynamic_update_slice(
            dquery_buffer, dquery_part[:, None], (start_index, head, 0, 0)
        )
        old_keys = lax.dynamic_slice(
            dkey_buffer, (start_index, head, 0), (block_rows + WINDOW_LENGTH, 1, width)
        )
        dkey_buffer = lax.dynamic_update_slice(
            dkey_buffer, old_keys + dkey_part[:, None], (start_index, head, 0)
        )
        old_values = lax.dynamic_slice(
            dvalue_buffer, (start_index, head, 0), (block_rows + WINDOW_LENGTH, 1, width)
        )
        dvalue_buffer = lax.dynamic_update_slice(
            dvalue_buffer, old_values + dvalue_part[:, None], (start_index, head, 0)
        )
        return (dquery_buffer, dkey_buffer, dvalue_buffer)

    initial = (
        jnp.zeros(query_states.shape, jnp.float32),
        jnp.zeros(key_states.shape, jnp.float32),
        jnp.zeros(value_states.shape, jnp.float32),
    )
    return lax.fori_loop(0, turns, advance, initial)


def forward(weights, inputs, segments, finish):
    (
        attention_gain,
        query_weight,
        key_matrix,
        value_matrix,
        output_weight,
        feedforward_gain,
        gate_weight,
        up_weight,
        down_weight,
    ) = weights
    position = lax.axis_index("tok")
    inwide = inputs.astype(jnp.float32)
    normalized_input, inverse_one = normalize(inwide, attention_gain)
    normed_all = lax.all_gather(normalized_input.astype(jnp.bfloat16), "mp", axis=0, tiled=True)
    length = normed_all.shape[0]
    qheads = query_weight.shape[1] // HEAD_SIZE
    kheads = key_matrix.shape[1] // HEAD_SIZE
    query_lin = jnp.dot(normed_all, query_weight, preferred_element_type=jnp.float32)
    key_linear = jnp.dot(normed_all, key_matrix, preferred_element_type=jnp.float32)
    value_states = jnp.dot(normed_all, value_matrix, preferred_element_type=jnp.float32).astype(
        jnp.bfloat16
    )
    value_states = value_states.reshape(length, kheads, HEAD_SIZE)
    cosine, sine = rope_tables(length, position * length, HEAD_SIZE)
    query_states = turn(query_lin.reshape(length, qheads, HEAD_SIZE), cosine, sine).astype(
        jnp.bfloat16
    )
    query_states = query_states.reshape(length, kheads, qheads // kheads, HEAD_SIZE)
    key_states = turn(key_linear.reshape(length, kheads, HEAD_SIZE), cosine, sine).astype(
        jnp.bfloat16
    )
    edge_keys, edge_values = passed_along(
        (key_states[length - WINDOW_LENGTH :], value_states[length - WINDOW_LENGTH :]), "tok", 1
    )
    all_keys = jnp.concatenate([edge_keys, key_states], 0)
    all_values = jnp.concatenate([edge_values, value_states], 0)
    padded_ids = jnp.concatenate([jnp.full((WINDOW_LENGTH,), -1, jnp.int32), segments])
    key_ids = lax.dynamic_slice_in_dim(padded_ids, position * length, length + WINDOW_LENGTH, 0)
    attended, lses = attend(query_states, all_keys, all_values, key_ids)
    attended_flat = attended.reshape(length, qheads * HEAD_SIZE)
    residual = inwide + lax.psum_scatter(
        jnp.dot(attended_flat, output_weight, preferred_element_type=jnp.float32).astype(
            jnp.bfloat16
        ),
        "mp",
        scatter_dimension=0,
        tiled=True,
    ).astype(jnp.float32)
    normed_two, inverse_two = normalize(residual, feedforward_gain)
    normed_two_all = lax.all_gather(normed_two.astype(jnp.bfloat16), "mp", axis=0, tiled=True)
    gate = jnp.dot(normed_two_all, gate_weight, preferred_element_type=jnp.float32)
    up = jnp.dot(normed_two_all, up_weight, preferred_element_type=jnp.float32)
    mixed = (jax.nn.silu(gate) * up).astype(jnp.bfloat16)
    result = None
    if finish:
        result = residual + lax.psum_scatter(
            jnp.dot(mixed, down_weight, preferred_element_type=jnp.float32).astype(jnp.bfloat16),
            "mp",
            scatter_dimension=0,
            tiled=True,
        ).astype(jnp.float32)
    saved = (
        inwide,
        inverse_one,
        normed_all,
        query_states,
        all_keys,
        all_values,
        key_ids,
        cosine,
        sine,
        lses,
        attended_flat,
        residual,
        inverse_two,
        normed_two_all,
        gate,
        up,
        mixed,
    )
    return (result, saved)


def fetch(
    attention_gain,
    query_weight,
    key_matrix,
    value_matrix,
    output_weight,
    feedforward_gain,
    gate_weight,
    up_weight,
    down_weight,
):
    return (
        lax.all_gather(attention_gain, "tok", axis=0, tiled=True),
        lax.all_gather(query_weight, "tok", axis=0, tiled=True),
        lax.all_gather(key_matrix, "tok", axis=0, tiled=True),
        lax.all_gather(value_matrix, "tok", axis=0, tiled=True),
        lax.all_gather(output_weight, "tok", axis=1, tiled=True),
        lax.all_gather(feedforward_gain, "tok", axis=0, tiled=True),
        lax.all_gather(gate_weight, "tok", axis=0, tiled=True),
        lax.all_gather(up_weight, "tok", axis=0, tiled=True),
        lax.all_gather(down_weight, "tok", axis=1, tiled=True),
    )


def body(
    inputs,
    grad_output,
    segments,
    attention_gain,
    query_weight,
    key_matrix,
    value_matrix,
    output_weight,
    feedforward_gain,
    gate_weight,
    up_weight,
    down_weight,
):
    shards = (
        attention_gain,
        query_weight,
        key_matrix,
        value_matrix,
        output_weight,
        feedforward_gain,
        gate_weight,
        up_weight,
        down_weight,
    )
    weights = fetch(*shards)
    result, saved = forward(weights, inputs, segments, True)
    weights = fetch(*shards)
    unused, saved = forward(weights, inputs, segments, False)
    (
        gain_one,
        query_full,
        key_full,
        value_full,
        output_full,
        gain_two,
        gate_full,
        up_full,
        down_full,
    ) = weights
    (
        inwide,
        inverse_one,
        normed_all,
        query_states,
        all_keys,
        all_values,
        key_ids,
        cosine,
        sine,
        lses,
        attended_flat,
        residual,
        inverse_two,
        normed_two_all,
        gate,
        up,
        mixed,
    ) = saved
    length = normed_all.shape[0]
    qheads = query_states.shape[1] * query_states.shape[2]
    dout_all = lax.all_gather(grad_output, "mp", axis=0, tiled=True)
    down_grad = outer_product(mixed, dout_all)
    dmixed = times_transposed(dout_all, down_full)
    sigma = jax.nn.sigmoid(gate)
    dup = (dmixed * (gate * sigma)).astype(jnp.bfloat16)
    dgate = (dmixed * up * sigma * (1.0 + gate * (1.0 - sigma))).astype(jnp.bfloat16)
    gate_grad = outer_product(normed_two_all, dgate)
    up_grad = outer_product(normed_two_all, dup)
    dnormed_two = lax.psum_scatter(
        (times_transposed(dgate, gate_full) + times_transposed(dup, up_full)).astype(jnp.bfloat16),
        "mp",
        scatter_dimension=0,
        tiled=True,
    ).astype(jnp.float32)
    dresidual_norm, gain_two_part = norm_back(dnormed_two, residual, inverse_two, gain_two)
    dresidual = grad_output.astype(jnp.float32) + dresidual_norm
    dresidual_all = lax.all_gather(dresidual.astype(jnp.bfloat16), "mp", axis=0, tiled=True)
    output_grad = outer_product(attended_flat, dresidual_all)
    dattended = (
        times_transposed(dresidual_all, output_full)
        .astype(jnp.bfloat16)
        .reshape(query_states.shape)
    )
    dquery_rot, dkey_all, dvalue_all = attend_back(
        query_states, all_keys, all_values, key_ids, lses, dattended
    )
    back_keys, back_values = (
        passed_along(dkey_all[:WINDOW_LENGTH].astype(jnp.bfloat16), "tok", -1).astype(jnp.float32),
        passed_along(dvalue_all[:WINDOW_LENGTH].astype(jnp.bfloat16), "tok", -1).astype(
            jnp.float32
        ),
    )
    own_keys = dkey_all[WINDOW_LENGTH:]
    own_values = dvalue_all[WINDOW_LENGTH:]
    boundary = length - WINDOW_LENGTH
    dkey_rot = jnp.concatenate([own_keys[:boundary], own_keys[boundary:] + back_keys], 0)
    dvalue_sum = jnp.concatenate([own_values[:boundary], own_values[boundary:] + back_values], 0)
    dquery = (
        turn_back(dquery_rot.reshape(length, qheads, HEAD_SIZE), cosine, sine)
        .reshape(length, qheads * HEAD_SIZE)
        .astype(jnp.bfloat16)
    )
    dkey = turn_back(dkey_rot, cosine, sine).reshape(length, -1).astype(jnp.bfloat16)
    dvalue = dvalue_sum.reshape(length, -1).astype(jnp.bfloat16)
    query_grad = outer_product(normed_all, dquery)
    key_grad = outer_product(normed_all, dkey)
    value_grad = outer_product(normed_all, dvalue)
    total_length = times_transposed(dquery, query_full) + times_transposed(dkey, key_full)
    dnormed_one = lax.psum_scatter(
        (total_length + times_transposed(dvalue, value_full)).astype(jnp.bfloat16),
        "mp",
        scatter_dimension=0,
        tiled=True,
    ).astype(jnp.float32)
    dinput_norm, gain_one_part = norm_back(dnormed_one, inwide, inverse_one, gain_one)
    input_gradient = dresidual + dinput_norm
    gain_totals = lax.psum((gain_one_part, gain_two_part), "mp")
    grads = (
        lax.psum_scatter(
            gain_totals[0].astype(jnp.bfloat16), "tok", scatter_dimension=0, tiled=True
        ).astype(jnp.float32),
        lax.psum_scatter(
            query_grad.astype(jnp.bfloat16), "tok", scatter_dimension=0, tiled=True
        ).astype(jnp.float32),
        lax.psum_scatter(
            key_grad.astype(jnp.bfloat16), "tok", scatter_dimension=0, tiled=True
        ).astype(jnp.float32),
        lax.psum_scatter(
            value_grad.astype(jnp.bfloat16), "tok", scatter_dimension=0, tiled=True
        ).astype(jnp.float32),
        lax.psum_scatter(
            output_grad.astype(jnp.bfloat16), "tok", scatter_dimension=1, tiled=True
        ).astype(jnp.float32),
        lax.psum_scatter(
            gain_totals[1].astype(jnp.bfloat16), "tok", scatter_dimension=0, tiled=True
        ).astype(jnp.float32),
        lax.psum_scatter(
            gate_grad.astype(jnp.bfloat16), "tok", scatter_dimension=0, tiled=True
        ).astype(jnp.float32),
        lax.psum_scatter(
            up_grad.astype(jnp.bfloat16), "tok", scatter_dimension=0, tiled=True
        ).astype(jnp.float32),
        lax.psum_scatter(
            down_grad.astype(jnp.bfloat16), "tok", scatter_dimension=1, tiled=True
        ).astype(jnp.float32),
    )
    return (
        result.astype(jnp.bfloat16),
        input_gradient,
        grads[0],
        grads[1],
        grads[2],
        grads[3],
        grads[4],
        grads[5],
        grads[6],
        grads[7],
        grads[8],
    )


def solution(mesh):
    in_specs = (
        P(("tok", "mp"), None),
        P(("tok", "mp"), None),
        P(),
        P("tok"),
        P("tok", "mp"),
        P("tok", "mp"),
        P("tok", "mp"),
        P("mp", "tok"),
        P("tok"),
        P("tok", "mp"),
        P("tok", "mp"),
        P("mp", "tok"),
    )
    out_specs = (
        P(("tok", "mp"), None),
        P(("tok", "mp"), None),
        P("tok"),
        P("tok", "mp"),
        P("tok", "mp"),
        P("tok", "mp"),
        P("mp", "tok"),
        P("tok"),
        P("tok", "mp"),
        P("tok", "mp"),
        P("mp", "tok"),
    )
    return jax.shard_map(body, mesh=mesh, in_specs=in_specs, out_specs=out_specs, check_vma=False)
```

profile of v0, /device:TPU:0, one launch (start us, length us, event | category | flops | bytes accessed | tf_op | source)
XLA Modules:
  0.0 1982.7 jit_solution(13480963268365953518)
XLA Ops:
  12.8 38.8 %all-reduce.7 = (bf16[2560]{0:T(1024)(128)(2,1)S(1)}, bf16[2560]{0:T(1024)(128)(2,1)S(1)}) all-reduce(bf16[2560]{0:T(1024)(128)(2,1)S(1)} %dynamic-update-slice, bf16[2560]{0:T(1024)(128)(2,1)S(1)} %dynamic-update-slice.1), channel_id=1, replica_groups=mesh['tok'=8,'mp'=4] {'tok'}, use_global_device_ids=true, to_apply=%add.1 | all-reduce | flops 5120 | bytes 20480
  57.3 32.7 %all-gather.1 = bf16[8,320,160]{1,2,0:T(8,128)(2,1)S(1)} all-gather(bf16[1,320,160]{1,2,0:T(8,128)(2,1)S(1)} %bitcast.328), channel_id=1, replica_groups=mesh['tok'=8,'mp'=4] {'tok'}, dimensions={0}, use_global_device_ids=true | all-gather | bytes 921600 | tf_op jit(solution)/shard_map/all_gather | solution.py:287
  91.0 33.8 %all-gather = bf16[8,320,160]{1,2,0:T(8,128)(2,1)S(1)} all-gather(bf16[1,320,160]{1,2,0:T(8,128)(2,1)S(1)} %bitcast.329), channel_id=1, replica_groups=mesh['tok'=8,'mp'=4] {'tok'}, dimensions={0}, use_global_device_ids=true | all-gather | bytes 921600 | tf_op jit(solution)/shard_map/all_gather | solution.py:288
  126.8 5.1 convolution_convert_fusion.11
  139.2 24.9 %all-gather.15.cloned.1.call-done = bf16[2560,640]{1,0:T(8,128)(2,1)} async-done(((bf16[320,640]{1,0:T(8,128)(2,1)}), bf16[2560,640]{1,0:T(8,128)(2,1)}) %all-gather.15.cloned.1.call-update) | async-done | bytes 3276816 | tf_op jit(solution)/shard_map/all_gather | solution.py:286
  164.0 6.6 fusion.132
  173.8 29.8 %while.52 = (s32[]{:T(128)}, bf16[1024,2,4,80]{0,3,2,1:T(8,128)(2,1)}, f32[2,4,1024]{2,1,0:T(4,128)S(1)}, bf16[1536,2,80]{0,2,1:T(8,128)(2,1)S(1)}, s32[1536]{0:...) while((s32[]{:T(128)}, ...), condition=%wide.region_11.12_spmd, body=%wide.region_8.11_spmd.sunk | while | flops 697465344 | bytes 28338608 | solution.py:123
  203.6 23.2 %all-gather.17.cloned.1.call-done = bf16[640,2560]{0,1:T(8,128)(2,1)} async-done(((bf16[640,320]{0,1:T(8,128)(2,1)}), bf16[640,2560]{0,1:T(8,128)(2,1)}) %all-gather.17.cloned.1.call-update) | async-done | bytes 3276816 | tf_op jit(solution)/shard_map/all_gather | solution.py:289
  226.8 8.9 convolution_convert_fusion.3
  236.4 49.5 %reduce-scatter.21.cloned.1.call-done = bf16[256,2560]{1,0:T(8,128)(2,1)} async-done(((bf16[1024,2560]{1,0:T(8,128)(2,1)}), bf16[256,2560]{1,0:T(8,128)(2,1)}) %reduce-scatter.21.cloned.1.call-update) | async-done | bytes 1310736 | tf_op jit(solution)/shard_map/reduce_scatter | solution.py:230
  293.1 33.5 %while.51 = (s32[]{:T(128)}, bf16[1024,2,4,80]{0,3,2,1:T(8,128)(2,1)}, bf16[1536,2,80]{0,2,1:T(8,128)(2,1)}, s32[1536]{0:T(1024)S(1)}, bf16[1536,2,80]{0,2,1:T(8...) while((s32[]{:T(128)}, ...), condition=%wide.region_4.5_spmd, body=%wide.region_1.4_spmd.sunk | while | flops 697465344 | bytes 28330400 | solution.py:123
  326.5 9.0 convolution_convert_fusion.4
  335.6 87.5 %all-gather.21.cloned.1.call-done = bf16[2560,1792]{1,0:T(8,128)(2,1)} async-done(((bf16[320,1792]{1,0:T(8,128)(2,1)}), bf16[2560,1792]{1,0:T(8,128)(2,1)}) %all-gather.21.cloned.1.call-update) | async-done | bytes 9175056 | tf_op jit(solution)/shard_map/all_gather | solution.py:291
  423.1 40.7 %all-gather.29.cloned.1.call-done = bf16[1024,2560]{1,0:T(8,128)(2,1)} async-done(((bf16[256,2560]{1,0:T(8,128)(2,1)}), bf16[1024,2560]{1,0:T(8,128)(2,1)}) %all-gather.29.cloned.1.call-update) | async-done | bytes 5242896 | tf_op jit(solution)/shard_map/all_gather | solution.py:239
  463.8 16.4 fusion.135
  480.2 120.9 %all-gather.23.cloned.1.call-done = bf16[2560,1792]{1,0:T(8,128)(2,1)} async-done(((bf16[320,1792]{1,0:T(8,128)(2,1)}), bf16[2560,1792]{1,0:T(8,128)(2,1)}) %all-gather.23.cloned.1.call-update) | async-done | bytes 9175056 | tf_op jit(solution)/shard_map/all_gather | solution.py:292
  601.1 16.0 fusion.134
  617.1 24.3 %all-gather.27.cloned.1.call-done = bf16[1024,2560]{1,0:T(8,128)(2,1)} async-done(((bf16[256,2560]{1,0:T(8,128)(2,1)}), bf16[1024,2560]{1,0:T(8,128)(2,1)}) %all-gather.27.cloned.1.call-update) | async-done | bytes 5242896 | tf_op jit(solution)/shard_map/all_gather | solution.py:358
  641.4 137.3 %all-gather.25.cloned.1.call-done = bf16[1792,2560]{0,1:T(8,128)(2,1)} async-done(((bf16[1792,320]{0,1:T(8,128)(2,1)}), bf16[1792,2560]{0,1:T(8,128)(2,1)}) %all-gather.25.cloned.1.call-update) | async-done | bytes 9175056 | tf_op jit(solution)/shard_map/all_gather | solution.py:293
  778.7 21.8 %multiply_convert_fusion.1 = (bf16[1024,1792]{1,0:T(8,128)(2,1)}, bf16[1024,1792]{1,0:T(8,128)(2,1)}) fusion(f32[1024,1792]{1,0:T(8,128)} %fusion.135, f32[1024,1792]{1,0:T(8,128)} %fusion.134, bf16[1024,2560]{1,0:T(8,128)(2,1)} %all-gather.27.cloned.1.call-done, bf16[1792,2560]{0,1:T(8,128)(2,1)} %all-gather.25.cloned.1.call-done), kind=kOutput, calls=%fused_computation.113 | convolution fusion | flops 9419096064 | bytes 36438016 | tf_op jit(solution)/shard_map/dot_general | solution.py:64
  800.5 15.9 fusion.136
  816.5 15.1 add_convert_fusion.1
  831.7 53.2 %reduce-scatter.23.cloned.1.call-done = bf16[256,2560]{1,0:T(8,128)(2,1)} async-done(((bf16[1024,2560]{1,0:T(8,128)(2,1)}), bf16[256,2560]{1,0:T(8,128)(2,1)}) %reduce-scatter.23.cloned.1.call-update) | async-done | bytes 1310736 | tf_op jit(solution)/shard_map/reduce_scatter | solution.py:366
  884.9 4.6 fusion.107
  891.7 40.5 %all-gather.31.cloned.1.call-done = bf16[1024,2560]{1,0:T(8,128)(2,1)} async-done(((bf16[256,2560]{1,0:T(8,128)(2,1)}), bf16[1024,2560]{1,0:T(8,128)(2,1)}) %all-gather.31.cloned.1.call-update) | async-done | bytes 5242896 | tf_op jit(solution)/shard_map/all_gather | solution.py:374
  932.2 8.1 convolution_convert_fusion.10
  944.3 61.5 %while.53 = (s32[]{:T(128)}, f32[1024,2,4,80]{0,3,2,1:T(8,128)}, f32[1536,2,80]{0,2,1:T(8,128)}, f32[1536,2,80]{0,2,1:T(8,128)}, bf16[1536,2,80]{0,2,1:T(8,128)(...) while((s32[]{:T(128)}, f32[1024,2,4,80]{0,3,2,1:T(8,128)}, ...), condition=%wide.region_18.19_spmd, body=%wide.region_16.18_spmd.sunk | while | flops 1712732672 | bytes 89842256 | solution.py:185
  1016.6 7.3 fusion.137
  1027.8 8.3 add_convert_fusion
  1036.2 54.7 %reduce-scatter.25.cloned.1.call-done = bf16[256,2560]{1,0:T(8,128)(2,1)} async-done(((bf16[1024,2560]{1,0:T(8,128)(2,1)}), bf16[256,2560]{1,0:T(8,128)(2,1)}) %reduce-scatter.25.cloned.1.call-update) | async-done | bytes 1310736 | tf_op jit(solution)/shard_map/reduce_scatter | solution.py:406
  1094.0 4.7 fusion.103
  1098.8 18.6 convolution_convert_fusion
  1117.4 15.0 convolution_convert_fusion.1
  1132.5 15.3 convolution_convert_fusion.2
  1158.3 8.5 convolution_convert_fusion.6
  1168.1 8.5 convolution_convert_fusion.7
  1176.8 16.2 fusion.133
  1192.9 30.8 %convolution_convert_fusion.5 = bf16[1024,2560]{1,0:T(8,128)(2,1)} fusion(bf16[1792,2560]{0,1:T(8,128)(2,1)} %all-gather.25.cloned.1.call-done, f32[1024,1792]{1,0:T(8,128)} %fusion.133, bf16[1024,2560]{1,0:T(8,128)(2,1)} %all-gather.19.cloned.1.call-done, bf16[2560,1792]{1,0:T(8,128)(2,1)} %all-gather.23.cloned.1.call-done), kind=kOutput, calls=%fused_computation.120 | convolution fusion | flops 18804113408 | bytes 36175872 | tf_op jit(solution)/shard_map/dot_general | solution.py:246
  1224.4 78.3 %reduce-scatter.35.cloned.1.call-done = bf16[1792,320]{0,1:T(8,128)(2,1)} async-done(((bf16[1792,2560]{0,1:T(8,128)(2,1)}), bf16[1792,320]{0,1:T(8,128)(2,1)}) %reduce-scatter.35.cloned.1.call-update) | async-done | bytes 1146896 | tf_op jit(solution)/shard_map/reduce_scatter | solution.py:440
  1305.5 160.1 %reduce-scatter.33.cloned.1.call-done = bf16[320,1792]{1,0:T(8,128)(2,1)} async-done(((bf16[2560,1792]{1,0:T(8,128)(2,1)}), bf16[320,1792]{1,0:T(8,128)(2,1)}) %reduce-scatter.33.cloned.1.call-update) | async-done | bytes 1146896 | tf_op jit(solution)/shard_map/reduce_scatter | solution.py:437
  1468.4 159.5 %reduce-scatter.31.cloned.1.call-done = bf16[320,1792]{1,0:T(8,128)(2,1)} async-done(((bf16[2560,1792]{1,0:T(8,128)(2,1)}), bf16[320,1792]{1,0:T(8,128)(2,1)}) %reduce-scatter.31.cloned.1.call-update) | async-done | bytes 1146896 | tf_op jit(solution)/shard_map/reduce_scatter | solution.py:434
  1630.7 64.2 %reduce-scatter.37.cloned.1.call-done = bf16[320,160]{1,0:T(8,128)(2,1)} async-done(((bf16[2560,160]{1,0:T(8,128)(2,1)}), bf16[320,160]{1,0:T(8,128)(2,1)}) %reduce-scatter.37.cloned.1.call-update) | async-done | bytes 102416
  1696.7 65.3 %reduce-scatter.39.cloned.1.call-done = bf16[320,160]{1,0:T(8,128)(2,1)} async-done(((bf16[2560,160]{1,0:T(8,128)(2,1)}), bf16[320,160]{1,0:T(8,128)(2,1)}) %reduce-scatter.39.cloned.1.call-update) | async-done | bytes 102416
  1763.8 77.2 %reduce-scatter.29.cloned.1.call-done = bf16[640,320]{0,1:T(8,128)(2,1)} async-done(((bf16[640,2560]{0,1:T(8,128)(2,1)}), bf16[640,320]{0,1:T(8,128)(2,1)}) %reduce-scatter.29.cloned.1.call-update) | async-done | bytes 409616 | tf_op jit(solution)/shard_map/reduce_scatter | solution.py:428
  1843.0 76.8 %reduce-scatter.27.cloned.1.call-done = bf16[320,640]{1,0:T(8,128)(2,1)} async-done(((bf16[2560,640]{1,0:T(8,128)(2,1)}), bf16[320,640]{1,0:T(8,128)(2,1)}) %reduce-scatter.27.cloned.1.call-update) | async-done | bytes 409616 | tf_op jit(solution)/shard_map/reduce_scatter | solution.py:419
  1921.7 10.5 all-reduce.5
  1932.2 35.3 %all-reduce.6 = (bf16[2560]{0:T(1024)(128)(2,1)S(1)}, bf16[2560]{0:T(1024)(128)(2,1)S(1)}) all-reduce(bf16[2560]{0:T(1024)(128)(2,1)S(1)} %get-tuple-element.655, bf16[2560]{0:T(1024)(128)(2,1)S(1)} %get-tuple-element.656), channel_id=7, replica_groups=mesh['tok'=8,'mp'=4] {'tok'}, use_global_device_ids=true, to_apply=%region_23.24.clone | all-reduce | flops 5120 | bytes 20480
  1968.2 4.7 reduce-scatter.19.cloned.1.call-done
  (352 shorter events, 210.4 us)
Async XLA Ops:
  7.2 119.6 %all-gather.13.cloned.1.call-start = ((), (), s32[]{:S(2)}) async-start(), calls=%async_computation.12 | async-start | bytes 6553600 | tf_op jit(solution)/shard_map/all_gather | solution.py:203
  7.2 50.0 %copy-start.32 = (bf16[320,160]{0,1:T(8,128)(2,1)S(1)}, bf16[320,160]{0,1:T(8,128)(2,1)}, u32[]{:S(2)}) copy-start(bf16[320,160]{0,1:T(8,128)(2,1)} %param.23) | copy-start | bytes 307204
  8.9 48.3 %copy-start.37 = (f32[256]{0:T(256)}, f32[256]{0:T(256)S(1)}, u32[]{:S(2)}) copy-start(f32[256]{0:T(256)S(1)} %add_rsqrt_fusion.2) | copy-start | bytes 3076
  54.4 36.6 %copy-start.33 = (bf16[320,160]{0,1:T(8,128)(2,1)S(1)}, bf16[320,160]{0,1:T(8,128)(2,1)}, u32[]{:S(2)}) copy-start(bf16[320,160]{0,1:T(8,128)(2,1)} %param.24) | copy-start | bytes 307204
  54.4 109.6 %all-gather.15.cloned.1.call-start = ((), (), s32[]{:S(2)}) async-start(), calls=%async_computation.13 | async-start | bytes 3686400 | tf_op jit(solution)/shard_map/all_gather | solution.py:286
  55.1 171.6 %all-gather.17.cloned.1.call-start = ((), (), s32[]{:S(2)}) async-start(), calls=%async_computation.14 | async-start | bytes 3686400 | tf_op jit(solution)/shard_map/all_gather | solution.py:289
  55.9 230.0 %reduce-scatter.21.cloned.1.call-start = ((), (), s32[]{:S(2)}) async-start(), calls=%async_computation.21 | async-start | bytes 6553600 | tf_op jit(solution)/shard_map/reduce_scatter | solution.py:230
  57.2 113.5 %copy-start.15 = (f32[1024,80]{0,1:T(8,128)}, f32[1024,80]{0,1:T(8,128)S(1)}, u32[]{:S(2)}) copy-start(f32[1024,80]{0,1:T(8,128)S(1)} %get-tuple-element.686) | copy-start | bytes 983044
  57.3 113.5 %copy-start.17 = (f32[1024,80]{0,1:T(8,128)}, f32[1024,80]{0,1:T(8,128)S(1)}, u32[]{:S(2)}) copy-start(f32[1024,80]{0,1:T(8,128)S(1)} %get-tuple-element.685) | copy-start | bytes 983044
  90.3 36.4 %copy-start.36 = (s32[8192]{0:T(1024)S(1)}, s32[8192]{0:T(1024)}, u32[]{:S(2)}) copy-start(s32[8192]{0:T(1024)} %param.20) | copy-start | bytes 98308
  91.0 42.9 %copy-start.22 = (bf16[2560,160]{0,1:T(8,128)(2,1)}, bf16[2560,160]{0,1:T(8,128)(2,1)S(1)}, u32[]{:S(2)}) copy-start(bf16[2560,160]{0,1:T(8,128)(2,1)S(1)} %reshape.260) | copy-start | bytes 2457604
  132.0 39.7 %collective-permute-start = (bf16[512,2,80]{0,2,1:T(8,128)(2,1)S(1)}, bf16[512,2,80]{0,2,1:T(8,128)(2,1)}, u32[]{:S(2)}, u32[]{:S(2)}) collective-permute-start(bf16[512,2,80]{0,2,1:T(8,128)(2,1)S(1)} %bitcast.327), channel_id=1, source_target_pairs={{0,4},{4,8},{8,12},{12,16},{16,20},{20,24},{24,28},{1,5},{5,9},{9,... | collective-permute-start | bytes 491528 | tf_op jit(solution)/shard_map/ppermute | solution.py:18
  136.0 35.5 %collective-permute-start.1 = (bf16[512,2,80]{0,2,1:T(8,128)(2,1)S(1)}, bf16[512,2,80]{0,2,1:T(8,128)(2,1)S(1)}, u32[]{:S(2)}, u32[]{:S(2)}) collective-permute-start(bf16[512,2,80]{0,2,1:T(8,128)(2,1)S(1)} %slice.86), channel_id=1, source_target_pairs={{0,4},{4,8},{8,12},{12,16},{16,20},{20,24},{24,28},{1,5},{5,9},{9,... | collective-permute-start | bytes 491528 | tf_op jit(solution)/shard_map/ppermute | solution.py:18
  203.6 23.2 %copy-start.21 = (bf16[1536,2,80]{0,2,1:T(8,128)(2,1)}, bf16[1536,2,80]{0,2,1:T(8,128)(2,1)S(1)}, u32[]{:S(2)}) copy-start(bf16[1536,2,80]{0,2,1:T(8,128)(2,1)S(1)} %get-tuple-element.1050) | copy-start | bytes 1474564
  203.6 23.2 %copy-start.31 = (f32[2,4,1024]{2,1,0:T(4,128)}, f32[2,4,1024]{2,1,0:T(4,128)S(1)}, u32[]{:S(2)}) copy-start(f32[2,4,1024]{2,1,0:T(4,128)S(1)} %get-tuple-element.942) | copy-start | bytes 98308
  235.7 50.2 %copy-start = (bf16[256,2560]{1,0:T(8,128)(2,1)S(1)}, bf16[256,2560]{1,0:T(8,128)(2,1)}, u32[]{:S(2)}) copy-start(bf16[256,2560]{1,0:T(8,128)(2,1)} %param.18) | copy-start | bytes 3932164
  235.8 187.3 %all-gather.21.cloned.1.call-start = ((), (), s32[]{:S(2)}) async-start(), calls=%async_computation.17 | async-start | bytes 10321920 | tf_op jit(solution)/shard_map/all_gather | solution.py:291
  236.4 227.4 %all-gather.29.cloned.1.call-start = ((), (), s32[]{:S(2)}) async-start(), calls=%async_computation.23 | async-start | bytes 6553600 | tf_op jit(solution)/shard_map/all_gather | solution.py:239
  289.6 311.6 %all-gather.23.cloned.1.call-start = ((), (), s32[]{:S(2)}) async-start(), calls=%async_computation.18 | async-start | bytes 10321920 | tf_op jit(solution)/shard_map/all_gather | solution.py:292
  290.3 351.1 %all-gather.27.cloned.1.call-start = ((), (), s32[]{:S(2)}) async-start(), calls=%async_computation.22 | async-start | bytes 6553600 | tf_op jit(solution)/shard_map/all_gather | solution.py:358
  291.1 487.7 %all-gather.25.cloned.1.call-start = ((), (), s32[]{:S(2)}) async-start(), calls=%async_computation.19 | async-start | bytes 10321920 | tf_op jit(solution)/shard_map/all_gather | solution.py:293
  291.8 539.9 %reduce-scatter.17.cloned.1.call-start = ((), (), s32[]{:S(2)}) async-start(), calls=%async_computation.15 | async-start | bytes 6553600 | tf_op jit(solution)/shard_map/reduce_scatter | solution.py:230
  335.5 549.3 %reduce-scatter.23.cloned.1.call-start = ((), (), s32[]{:S(2)}) async-start(), calls=%async_computation.24 | async-start | bytes 6553600 | tf_op jit(solution)/shard_map/reduce_scatter | solution.py:366
  778.7 37.7 %slice-start = ((s8[9175040]{0:T(1024)(128)(4,1)}), s8[4194304]{0:T(1024)(128)(4,1)S(1)}, s32[]{:S(2)}) async-start(s8[9175040]{0:T(1024)(128)(4,1)} %bitcast.330), calls=%async_computation.34 | async-start | bytes 8388608
  778.7 37.7 %slice-start.1 = ((s8[9175040]{0:T(1024)(128)(4,1)}), s8[4194304]{0:T(1024)(128)(4,1)S(1)}, s32[]{:S(2)}) async-start(s8[9175040]{0:T(1024)(128)(4,1)} %bitcast.330), calls=%async_computation.35 | async-start | bytes 8388608
  800.5 15.9 slice-start.2
  831.6 100.6 %all-gather.31.cloned.1.call-start = ((), (), s32[]{:S(2)}) async-start(), calls=%async_computation.25 | async-start | bytes 6553600 | tf_op jit(solution)/shard_map/all_gather | solution.py:374
  891.6 199.3 %reduce-scatter.25.cloned.1.call-start = ((), (), s32[]{:S(2)}) async-start(), calls=%async_computation.26 | async-start | bytes 6553600 | tf_op jit(solution)/shard_map/reduce_scatter | solution.py:406
  944.3 66.4 %copy-start.16 = (f32[1024,80]{0,1:T(8,128)S(1)}, f32[1024,80]{0,1:T(8,128)}, u32[]{:S(2)}) copy-start(f32[1024,80]{0,1:T(8,128)} %copy-done.15) | copy-start | bytes 983044
  1006.8 17.2 collective-permute-start.2
  1009.3 17.4 collective-permute-start.3
  1016.6 7.3 copy-start.9
  1036.1 54.8 %copy-start.30 = (f32[2560]{0:T(1024)S(1)}, f32[2560]{0:T(1024)}, u32[]{:S(2)}) copy-start(f32[2560]{0:T(1024)} %copy-done.29) | copy-start | bytes 30724
  1036.1 54.8 %copy-start.38 = (f32[256]{0:T(256)S(1)}, f32[256]{0:T(256)}, u32[]{:S(2)}) copy-start(f32[256]{0:T(256)} %copy-done.37) | copy-start | bytes 3076
  1036.1 57.9 %copy-start.4 = (bf16[256,2560]{1,0:T(8,128)(2,1)S(1)}, bf16[256,2560]{1,0:T(8,128)(2,1)}, u32[]{:S(2)}) copy-start(bf16[256,2560]{1,0:T(8,128)(2,1)} %reduce-scatter.21.cloned.1.call-done) | copy-start | bytes 3932164
  1036.1 140.6 %all-gather.19.cloned.1.call-start = ((), (), s32[]{:S(2)}) async-start(), calls=%async_computation.16 | async-start | bytes 6553600 | tf_op jit(solution)/shard_map/all_gather | solution.py:239
  1098.7 204.0 %reduce-scatter.35.cloned.1.call-start = ((), (), s32[]{:S(2)}) async-start(), calls=%async_computation.31 | async-start | bytes 10321920 | tf_op jit(solution)/shard_map/reduce_scatter | solution.py:440
  1117.4 348.2 %reduce-scatter.33.cloned.1.call-start = ((), (), s32[]{:S(2)}) async-start(), calls=%async_computation.30 | async-start | bytes 10321920 | tf_op jit(solution)/shard_map/reduce_scatter | solution.py:437
  1132.4 495.5 %reduce-scatter.31.cloned.1.call-start = ((), (), s32[]{:S(2)}) async-start(), calls=%async_computation.29 | async-start | bytes 10321920 | tf_op jit(solution)/shard_map/reduce_scatter | solution.py:434
  1147.8 547.1 %reduce-scatter.37.cloned.1.call-start = ((), (), s32[]{:S(2)}) async-start(), calls=%async_computation.32 | async-start | bytes 1474560
  1153.2 608.8 %reduce-scatter.39.cloned.1.call-start = ((), (), s32[]{:S(2)}) async-start(), calls=%async_computation.33 | async-start | bytes 1474560
  1158.2 682.8 %reduce-scatter.29.cloned.1.call-start = ((), (), s32[]{:S(2)}) async-start(), calls=%async_computation.28 | async-start | bytes 3686400 | tf_op jit(solution)/shard_map/reduce_scatter | solution.py:428
  1166.8 752.9 %reduce-scatter.27.cloned.1.call-start = ((), (), s32[]{:S(2)}) async-start(), calls=%async_computation.27 | async-start | bytes 3686400 | tf_op jit(solution)/shard_map/reduce_scatter | solution.py:419
  1176.7 796.2 %reduce-scatter.19.cloned.1.call-start = ((), (), s32[]{:S(2)}) async-start(), calls=%async_computation.20 | async-start | bytes 6553600 | tf_op jit(solution)/shard_map/reduce_scatter | solution.py:245
  1468.4 453.3 %copy-start.34 = (f32[2560]{0:T(1024)S(1)}, f32[2560]{0:T(1024)}, u32[]{:S(2)}) copy-start(f32[2560]{0:T(1024)} %get-tuple-element.606) | copy-start | bytes 30724
  1468.4 453.3 %copy-start.35 = (f32[2560]{0:T(1024)S(1)}, f32[2560]{0:T(1024)}, u32[]{:S(2)}) copy-start(f32[2560]{0:T(1024)} %get-tuple-element.604) | copy-start | bytes 30724
  1468.4 504.4 %copy-start.1 = (bf16[256,2560]{1,0:T(8,128)(2,1)S(1)}, bf16[256,2560]{1,0:T(8,128)(2,1)}, u32[]{:S(2)}) copy-start(bf16[256,2560]{1,0:T(8,128)(2,1)} %param.18) | copy-start | bytes 3932164
  1468.4 504.4 %copy-start.11 = (bf16[256,2560]{1,0:T(8,128)(2,1)S(1)}, bf16[256,2560]{1,0:T(8,128)(2,1)}, u32[]{:S(2)}) copy-start(bf16[256,2560]{1,0:T(8,128)(2,1)} %reduce-scatter.17.cloned.1.call-done) | copy-start | bytes 3932164
  (36 other events, 98.9 us)
Sparse Core Ops, SparseCore 0:
  54.5 37.6 all-gather.12
  94.4 69.5 all-gather.14
  166.2 60.5 all-gather.16
  235.9 49.9 reduce-scatter.20
  288.2 134.8 all-gather.20
  425.1 38.6 all-gather.28
  466.2 134.8 all-gather.22
  602.7 38.6 all-gather.26
  643.8 134.8 all-gather.24
  781.3 49.5 reduce-scatter.16
  833.4 51.3 reduce-scatter.22
  891.8 40.4 all-gather.30
  1036.2 54.6 reduce-scatter.24
  1098.9 40.4 all-gather.18
  1142.9 159.8 reduce-scatter.34
  1306.7 158.8 reduce-scatter.32
  1469.1 158.7 reduce-scatter.30
  1631.5 63.3 reduce-scatter.36
  1698.7 63.2 reduce-scatter.38
  1765.9 75.0 reduce-scatter.28
  1844.6 75.0 reduce-scatter.26
  1922.4 50.3 reduce-scatter.18
where the time goes:
time: 1990 us; the launch traced here: 1980 us
  waiting for transfers between devices  1350 us (68%)
  matrix products  346 us (17%)
  blocking collectives  151 us (8%)
  other arithmetic  82.8 us (4%)
  local copies, waits for them, and re-layouts  29.1 us (1%)
    reduce_scatter x1, waiting for transfers between devices, body(): lax.psum_scatter(up_grad.astype(jnp.bfloat16), 'tok', scatter_dimension=0...  160 us
    reduce_scatter x1, waiting for transfers between devices, body(): lax.psum_scatter(gate_grad.astype(jnp.bfloat16), 'tok', scatter_dimension...  159 us
    all_gather x1, waiting for transfers between devices, fetch(): lax.all_gather(down_weight, 'tok', axis=1, tiled=True)  137 us
    unnamed x24, waiting for transfers between devices  134 us
    all_gather x1, waiting for transfers between devices, fetch(): lax.all_gather(up_weight, 'tok', axis=0, tiled=True)  121 us
    all_gather x1, waiting for transfers between devices, fetch(): lax.all_gather(gate_weight, 'tok', axis=0, tiled=True)  87.5 us
    reduce_scatter x1, waiting for transfers between devices, body(): lax.psum_scatter(down_grad.astype(jnp.bfloat16), 'tok', scatter_dimension...  78.3 us
    dot_general x7, matrix products, times_transposed(): lax.dot_general(left, right, (((1,), (1,)), ((), ())), preferred_element_...  78.1 us
  transfers between devices with their start and end apart: 26, of which 19 were waited for; matrix products, arithmetic and copies ran while one was open for 17% of the time, Pallas kernels for 0%

commit v1 on v0

v1 whole, which is shorter than its diff:
```python
import functools

import jax
import jax.numpy as jnp
from jax import lax
from jax.experimental import pallas as pl
from jax.experimental.pallas import tpu as pltpu
from jax.sharding import PartitionSpec as P

HEAD_SIZE = 80
WINDOW_LENGTH = 512
EPS = 1e-05
THETA = 1000000.0
FLOOR = -1e30
AXES = ("tok", "mp")
FF_CHUNKS = (512, 384)


class Grid:
    def __init__(self):
        self.nz = lax.axis_size("tok") // 2
        tok = lax.axis_index("tok")
        mp = lax.axis_index("mp")
        self.z, self.y = tok // 2, tok % 2
        self.x, self.c = mp // 2, mp % 2
        self.me = self.y * 4 + self.x * 2 + self.c

    def pairs(self, move):
        out = []
        for z in range(self.nz):
            for g in range(8):
                target = move(z, g)
                if target is not None:
                    out.append((z * 8 + g, target[0] * 8 + target[1]))
        return out

    def swap(self, value, bit):
        return lax.ppermute(value, AXES, self.pairs(lambda z, g: (z, g ^ bit)))

    def ring(self, value):
        return lax.ppermute(value, AXES, self.pairs(lambda z, g: ((z + 1) % self.nz, g)))

    def step(self, value, d):
        def move(z, g):
            return (z + d, g) if 0 <= z + d < self.nz else None

        return lax.ppermute(value, AXES, self.pairs(move))


Y, X, C = 4, 2, 1


def rotated(grid, value, back=False):
    width = value.shape[-1] // grid.nz
    parts = []
    for s in range(grid.nz):
        block = lax.rem(grid.z - s + grid.nz, grid.nz)
        parts.append(lax.dynamic_slice_in_dim(value, block * width, width, value.ndim - 1))
    return jnp.concatenate(parts, -1)


def natural(grid, value):
    blocks = value.reshape((8, value.shape[0] // 8) + value.shape[1:])
    parts = [lax.dynamic_index_in_dim(blocks, grid.me ^ b, 0, False) for b in range(8)]
    return jnp.concatenate(parts, 0)


def gather_tokens(grid, block):
    half = block.shape[0] // 2
    bx = grid.swap(block, X)
    by = grid.swap(block, Y)
    bc = grid.swap(block, C)
    top = grid.swap(by[:half], X)
    bottom = grid.swap(bx[half:], Y)
    both = jnp.concatenate([bx, by], 0)
    cboth = grid.swap(both, C)
    bxy = jnp.concatenate([top, bottom], 0)
    bxyc = grid.swap(bxy, C)
    n = block.shape[0]
    return jnp.concatenate([block, bc, bx, cboth[:n], by, cboth[n:], bxy, bxyc], 0)


def scatter_tokens(grid, partial):
    n = partial.shape[0] // 8
    half = n // 2
    p = partial.reshape(4, 2, n, partial.shape[1])
    got = grid.swap(p[:, 1], C)
    q = (p[:, 0].astype(jnp.float32) + got.astype(jnp.float32)).astype(jnp.bfloat16)
    top, bottom = q[:, :half], q[:, half:]
    gx = grid.swap(jnp.stack([top[1], top[3]]), X)
    gy = grid.swap(jnp.stack([bottom[2], bottom[3]]), Y)
    tx = (top[2].astype(jnp.float32) + gx[1].astype(jnp.float32)).astype(jnp.bfloat16)
    by = (bottom[1].astype(jnp.float32) + gy[1].astype(jnp.float32)).astype(jnp.bfloat16)
    gt = grid.swap(tx, Y)
    gb = grid.swap(by, X)
    top = top[0].astype(jnp.float32) + gx[0].astype(jnp.float32) + gt.astype(jnp.float32)
    bottom = bottom[0].astype(jnp.float32) + gy[0].astype(jnp.float32) + gb.astype(jnp.float32)
    return jnp.concatenate([top, bottom], 0)


def halves(value):
    return value.reshape(value.shape[0], 2, value.shape[1] // 2)


def slot_zero(grid, pieces):
    packed = jnp.concatenate(pieces, -1)
    mine = lax.dynamic_index_in_dim(packed, grid.y, 1, False)
    other = lax.dynamic_index_in_dim(packed, 1 - grid.y, 1, False)
    got = grid.swap(other, Y)
    first = jnp.where(grid.y == 0, mine, got)
    second = jnp.where(grid.y == 0, got, mine)
    return jnp.concatenate([first, second], 0)


def gather_weight(grid, slot):
    slots = [slot]
    for _ in range(grid.nz - 1):
        slots.append(grid.ring(slots[-1]))
    return jnp.concatenate(slots, 0)


def scatter_weight(grid, partial):
    rows = partial.shape[0] // grid.nz
    p = partial.reshape(grid.nz, rows, partial.shape[1])
    acc = p[1]
    for s in range(2, grid.nz + 1):
        got = grid.ring(acc)
        acc = (got.astype(jnp.float32) + p[s % grid.nz].astype(jnp.float32)).astype(jnp.bfloat16)
    both = acc.reshape(2, rows // 2, acc.shape[1])
    mine = lax.dynamic_index_in_dim(both, grid.y, 0, False)
    other = lax.dynamic_index_in_dim(both, 1 - grid.y, 0, False)
    got = grid.swap(other, Y)
    first = jnp.where(grid.y == 0, mine, got)
    second = jnp.where(grid.y == 0, got, mine)
    return jnp.stack([first, second], 1).astype(jnp.float32)


LANES = 128
SCALE = HEAD_SIZE ** (-0.5)
LOG2E = 1.4426950408889634
MIB = 1024 * 1024
BF16 = jnp.bfloat16
F32 = jnp.float32
HBM = pl.BlockSpec(memory_space=pl.ANY)
WHOLE = pl.BlockSpec(memory_space=pltpu.VMEM)
MESH = pl.DeviceIdType.MESH


def light(**kwargs):
    return dict(
        cost_estimate=pl.CostEstimate(flops=1000000, bytes_accessed=100000, transcendentals=0),
        **kwargs,
    )


def params(mib, **kwargs):
    return pltpu.CompilerParams(vmem_limit_bytes=mib * MIB, **kwargs)


def rope_tables(count, first, width):
    half = width // 2
    places = (first + jnp.arange(count, dtype=jnp.int32)).astype(F32)
    freqs = THETA ** (-(jnp.arange(half, dtype=jnp.int32).astype(F32) * 2.0 / width))
    angles = places[:, None] * freqs[None, :]
    cosine, sine = jnp.cos(angles), jnp.sin(angles)
    blank = jnp.zeros((count, LANES // 2 - half), F32)
    return (
        jnp.concatenate([cosine, blank, cosine, blank], 1),
        jnp.concatenate([-sine, blank, sine, blank], 1),
    )


def spread_matrix(turned, plain):
    half = HEAD_SIZE // 2
    f = jnp.arange((turned + plain) * HEAD_SIZE, dtype=jnp.int32)
    head, place = f // HEAD_SIZE, f % HEAD_SIZE
    gap = jnp.where((head < turned) & (place >= half), LANES // 2 - half, 0)
    target = head * LANES + place + gap
    lanes = jnp.arange((turned + plain) * LANES, dtype=jnp.int32)
    return (target[:, None] == lanes[None, :]).astype(BF16)


def nt(left, right):
    return lax.dot_general(left, right, (((1,), (1,)), ((), ())), preferred_element_type=F32)


def nn(left, right):
    return lax.dot_general(left, right, (((1,), (0,)), ((), ())), preferred_element_type=F32)


def qkv_kernel(me_ref, a_ref, w_ref, cos_ref, sin_ref, q_ref, k_ref, v_ref):
    acc = nn(a_ref[...], w_ref[...])
    cosine, sine = cos_ref[...], sin_ref[...]
    heads = q_ref.shape[1] // LANES
    for h in range(heads + 1):
        u = acc[:, h * LANES : (h + 1) * LANES]
        turned = (u * cosine + pltpu.roll(u, LANES // 2, 1) * sine).astype(BF16)
        if h < heads:
            q_ref[:, h * LANES : (h + 1) * LANES] = turned
        else:
            k_ref[...] = turned
    v_ref[...] = acc[:, (heads + 1) * LANES :].astype(BF16)


def project_qkv(me, a1, w_pad, cosine, sine):
    length, model = a1.shape
    rows = length // 8
    wide = w_pad.shape[1] - 2 * LANES
    own = lambda b, me_ref: (b, 0)
    return pl.pallas_call(
        qkv_kernel,
        grid_spec=pltpu.PrefetchScalarGridSpec(
            num_scalar_prefetch=1,
            grid=(8,),
            in_specs=[
                pl.BlockSpec((rows, model), lambda b, me_ref: (b ^ me_ref[0], 0)),
                pl.BlockSpec(w_pad.shape, lambda b, me_ref: (0, 0)),
                pl.BlockSpec((rows, LANES), own),
                pl.BlockSpec((rows, LANES), own),
            ],
            out_specs=[
                pl.BlockSpec((rows, wide), own),
                pl.BlockSpec((rows, LANES), own),
                pl.BlockSpec((rows, LANES), own),
            ],
        ),
        out_shape=[
            jax.ShapeDtypeStruct((length, wide), BF16),
            jax.ShapeDtypeStruct((length, LANES), BF16),
            jax.ShapeDtypeStruct((length, LANES), BF16),
        ],
        compiler_params=params(40),
        name="project_qkv",
        **light(),
    )(me, a1, w_pad, cosine, sine)


def mask_bias(kid, qid, keys, rows):
    kk = lax.broadcasted_iota(jnp.int32, (keys, rows), 0)
    qq = lax.broadcasted_iota(jnp.int32, (keys, rows), 1)
    d = qq + WINDOW_LENGTH - kk
    allowed = (d >= 0) & (d < WINDOW_LENGTH) & (kid == qid)
    return jnp.where(allowed, 0.0, FLOOR)


def attend_kernel(me_ref, q_ref, k_ref, v_ref, kid_ref, qid_ref, o_ref, lse_ref):
    rows = q_ref.shape[0]
    keys = rows + WINDOW_LENGTH
    start = pl.multiple_of(pl.program_id(0) * rows, rows)
    span = pl.ds(start, keys)
    kb = k_ref[span, :]
    vt = v_ref[span, :].T
    bias = mask_bias(kid_ref[span, :], qid_ref[...], keys, rows)
    for h in range(q_ref.shape[1] // LANES):
        lanes = slice(h * LANES, (h + 1) * LANES)
        s = nt(kb, q_ref[:, lanes]) * (SCALE * LOG2E) + bias
        peak = jnp.max(s, axis=0, keepdims=True)
        p = jnp.exp2(s - peak)
        total = jnp.sum(p, axis=0, keepdims=True)
        ot = nn(vt, p.astype(BF16)) / total
        o_ref[:, lanes] = ot.T.astype(BF16)
        lse_ref[0, h : h + 1, :] = peak + jnp.log2(total)


def attend(me, q, k_all, v_all, kid, qid):
    length, wide = q.shape
    rows = length // 8
    heads = wide // LANES
    own = lambda b, me_ref: (b, 0)
    full = lambda b, me_ref: (0, 0)
    return pl.pallas_call(
        attend_kernel,
        grid_spec=pltpu.PrefetchScalarGridSpec(
            num_scalar_prefetch=1,
            grid=(8,),
            in_specs=[
                pl.BlockSpec((rows, wide), own),
                pl.BlockSpec(k_all.shape, full),
                pl.BlockSpec(v_all.shape, full),
                pl.BlockSpec(kid.shape, full),
                pl.BlockSpec((1, rows), lambda b, me_ref: (0, b)),
            ],
            out_specs=[
                pl.BlockSpec((rows, wide), lambda b, me_ref: (b ^ me_ref[0], 0)),
                pl.BlockSpec((1, heads, rows), lambda b, me_ref: (b, 0, 0)),
            ],
        ),
        out_shape=[
            jax.ShapeDtypeStruct((length, wide), BF16),
            jax.ShapeDtypeStruct((8, heads, rows), F32),
        ],
        compiler_params=params(40),
        name="attend",
        **light(),
    )(me, q, k_all, v_all, kid, qid)


def attend_back_kernel(
    me_ref, q_ref, do_ref, k_ref, v_ref, kid_ref, qid_ref, lse_ref, cos_ref, sin_ref,
    dq_ref, dk_ref, dv_ref,
):
    rows = q_ref.shape[0]
    keys = rows + WINDOW_LENGTH
    start = pl.multiple_of(pl.program_id(0) * rows, rows)
    span = pl.ds(start, keys)

    @pl.when(pl.program_id(0) == 0)
    def _():
        dk_ref[...] = jnp.zeros_like(dk_ref)
        dv_ref[...] = jnp.zeros_like(dv_ref)

    kb = k_ref[span, :]
    vb = v_ref[span, :]
    kt = kb.T
    bias = mask_bias(kid_ref[span, :], qid_ref[...], keys, rows)
    cosine, sine = cos_ref[...], sin_ref[...]
    dk = None
    for h in range(q_ref.shape[1] // LANES):
        lanes = slice(h * LANES, (h + 1) * LANES)
        qh = q_ref[:, lanes]
        doh = do_ref[:, lanes]
        p = jnp.exp2(nt(kb, qh) * (SCALE * LOG2E) + (bias - lse_ref[0, h : h + 1, :]))
        t = p * nt(vb, doh)
        inner = jnp.sum(t, axis=0, keepdims=True)
        ds = (t - p * inner).astype(BF16)
        dq = nn(kt, ds).T * SCALE
        dq_ref[:, lanes] = (dq * cosine - pltpu.roll(dq, LANES // 2, 1) * sine).astype(BF16)
        dk_h = nn(ds, qh)
        dv_h = nn(p.astype(BF16), doh)
        dk = dk_h if dk is None else dk + dk_h
        dv = dv_h if h == 0 else dv + dv_h
    dk_ref[span, :] += dk
    dv_ref[span, :] += dv


def attend_back(me, q, do, k_all, v_all, kid, qid, lse, cosine, sine):
    length, wide = q.shape
    rows = length // 8
    heads = wide // LANES
    own = lambda b, me_ref: (b, 0)
    mixed = lambda b, me_ref: (b ^ me_ref[0], 0)
    full = lambda b, me_ref: (0, 0)
    return pl.pallas_call(
        attend_back_kernel,
        grid_spec=pltpu.PrefetchScalarGridSpec(
            num_scalar_prefetch=1,
            grid=(8,),
            in_specs=[
                pl.BlockSpec((rows, wide), own),
                pl.BlockSpec((rows, wide), mixed),
                pl.BlockSpec(k_all.shape, full),
                pl.BlockSpec(v_all.shape, full),
                pl.BlockSpec(kid.shape, full),
                pl.BlockSpec((1, rows), lambda b, me_ref: (0, b)),
                pl.BlockSpec((1, heads, rows), lambda b, me_ref: (b, 0, 0)),
                pl.BlockSpec((rows, LANES), own),
                pl.BlockSpec((rows, LANES), own),
            ],
            out_specs=[
                pl.BlockSpec((rows, wide), mixed),
                pl.BlockSpec(k_all.shape, full),
                pl.BlockSpec(k_all.shape, full),
            ],
        ),
        out_shape=[
            jax.ShapeDtypeStruct((length, wide), BF16),
            jax.ShapeDtypeStruct(k_all.shape, F32),
            jax.ShapeDtypeStruct(k_all.shape, F32),
        ],
        compiler_params=params(40),
        name="attend_back",
        **light(),
    )(me, q, do, k_all, v_all, kid, qid, lse, cosine, sine)


def hidden_kernel(a_ref, d_ref, w_ref, m_ref, g_ref):
    n = m_ref.shape[1]
    gate = nn(a_ref[...], w_ref[:, :n])
    up = nn(a_ref[...], w_ref[:, n : 2 * n])
    dmixed = nn(d_ref[...], w_ref[:, 2 * n :])
    sigma = jax.nn.sigmoid(gate)
    silu = gate * sigma
    m_ref[...] = (silu * up).astype(BF16)
    g_ref[:, n:] = (dmixed * silu).astype(BF16)
    g_ref[:, :n] = (dmixed * up * sigma * (1.0 + gate * (1.0 - sigma))).astype(BF16)


def hidden_units(a2, dout, w):
    length, model = a2.shape
    n = w.shape[1] // 3
    rows = length // 4
    block = pl.BlockSpec((rows, model), lambda b: (b, 0))
    return pl.pallas_call(
        hidden_kernel,
        grid=(length // rows,),
        in_specs=[block, block, pl.BlockSpec(w.shape, lambda b: (0, 0))],
        out_specs=[
            pl.BlockSpec((rows, n), lambda b: (b, 0)),
            pl.BlockSpec((rows, 2 * n), lambda b: (b, 0)),
        ],
        out_shape=[
            jax.ShapeDtypeStruct((length, n), BF16),
            jax.ShapeDtypeStruct((length, 2 * n), BF16),
        ],
        compiler_params=params(56),
        name="hidden_units",
        **light(),
    )(a2, dout, w)


def peers():
    tok, mp = lax.axis_index("tok"), lax.axis_index("mp")
    tok_other = tok + 1 - 2 * (tok % 2)
    mp_x = lax.rem(mp + 2, 4)
    mp_c = mp + 1 - 2 * (mp % 2)
    return (tok, mp_x), (tok_other, mp), (tok, mp_c)


class Wires:
    def __init__(self, send, recv):
        self.send, self.recv, self.count = send, recv, 0
        self.copies = []
        self.x, self.y, self.c = peers()

    def greet(self):
        barrier = pltpu.get_barrier_semaphore()
        for peer in (self.x, self.y, self.c):
            pl.semaphore_signal(barrier, inc=1, device_id=peer, device_id_type=MESH)
        pl.semaphore_wait(barrier, 3)

    def start(self, source, target, peer):
        i = self.count
        self.count += 1
        copy = pltpu.make_async_remote_copy(
            src_ref=source,
            dst_ref=target,
            send_sem=self.send.at[i],
            recv_sem=self.recv.at[i],
            device_id=peer,
            device_id_type=MESH,
        )
        copy.start()
        self.copies.append(copy)
        return copy

    def finish(self):
        for copy in self.copies:
            copy.wait_send()


RS_COPIES, AG_COPIES = 10, 13


def reduce_phase(wires, pairs, cs, cr, q, xr, yr, tr, br, emit):
    n = q.shape[1]
    half = n // 2
    top, bottom = pl.ds(0, half), pl.ds(half, half)
    model = q.shape[2]
    tile = 512 if model % 512 == 0 else model

    def product(place, target):
        @pl.loop(0, model // tile)
        def _(t):
            cols = pl.ds(pl.multiple_of(t * tile, tile), tile)
            total = None
            for a, w in pairs:
                part = nt(a[place], w[cols, :])
                total = part if total is None else total + part
            target[:, cols] = total.astype(BF16)

    waits = {}
    for j in (3, 1, 2, 0):
        product(2 * j + 1, cs.at[j])
        got = wires.start(cs.at[j], cr.at[j], wires.c)
        product(2 * j, q.at[j])
        got.wait_recv()
        q[j] = (q[j].astype(F32) + cr[j].astype(F32)).astype(BF16)
        if j == 3:
            waits["x1"] = wires.start(q.at[3, top], xr.at[1], wires.x)
            waits["y1"] = wires.start(q.at[3, bottom], yr.at[1], wires.y)
        if j == 1:
            waits["x0"] = wires.start(q.at[1, top], xr.at[0], wires.x)
        if j == 2:
            waits["y0"] = wires.start(q.at[2, bottom], yr.at[0], wires.y)
    waits["x1"].wait_recv()
    q[2, top] = (q[2, top].astype(F32) + xr[1].astype(F32)).astype(BF16)
    waits["t"] = wires.start(q.at[2, top], tr, wires.y)
    waits["y1"].wait_recv()
    q[1, bottom] = (q[1, bottom].astype(F32) + yr[1].astype(F32)).astype(BF16)
    waits["b"] = wires.start(q.at[1, bottom], br, wires.x)
    waits["x0"].wait_recv()
    waits["t"].wait_recv()
    emit(top, q[0, top].astype(F32) + xr[0].astype(F32) + tr[...].astype(F32))
    waits["y0"].wait_recv()
    waits["b"].wait_recv()
    emit(bottom, q[0, bottom].astype(F32) + yr[0].astype(F32) + br[...].astype(F32))


def reduce_scratch(n, model):
    half = n // 2
    return [
        pltpu.VMEM((4, n, model), BF16),
        pltpu.VMEM((4, n, model), BF16),
        pltpu.VMEM((4, n, model), BF16),
        pltpu.VMEM((2, half, model), BF16),
        pltpu.VMEM((2, half, model), BF16),
        pltpu.VMEM((half, model), BF16),
        pltpu.VMEM((half, model), BF16),
    ]


def gather_phase(wires, block, out, local):
    n = block.shape[0]
    half = n // 2
    top, bottom = pl.ds(0, half), pl.ds(half, half)
    mine = pltpu.make_async_copy(block, out.at[0], local)
    mine.start()
    xb = wires.start(block.at[bottom], out.at[2, bottom], wires.x)
    yt = wires.start(block.at[top], out.at[4, top], wires.y)
    c = [wires.start(block, out.at[1], wires.c)]
    xt = wires.start(block.at[top], out.at[2, top], wires.x)
    yb = wires.start(block.at[bottom], out.at[4, bottom], wires.y)
    xb.wait_recv()
    db = wires.start(out.at[2, bottom], out.at[6, bottom], wires.y)
    c.append(wires.start(out.at[2, bottom], out.at[3, bottom], wires.c))
    yt.wait_recv()
    dt = wires.start(out.at[4, top], out.at[6, top], wires.x)
    c.append(wires.start(out.at[4, top], out.at[5, top], wires.c))
    xt.wait_recv()
    c.append(wires.start(out.at[2, top], out.at[3, top], wires.c))
    yb.wait_recv()
    c.append(wires.start(out.at[4, bottom], out.at[5, bottom], wires.c))
    dt.wait_recv()
    c.append(wires.start(out.at[6, top], out.at[7, top], wires.c))
    db.wait_recv()
    c.append(wires.start(out.at[6, bottom], out.at[7, bottom], wires.c))
    for copy in c:
        copy.wait_recv()
    mine.wait()


def gather_kernel(block, out, send, recv, local):
    wires = Wires(send, recv)
    wires.greet()
    gather_phase(wires, block, out, local)
    wires.finish()


def gather_block(block, number):
    n, model = block.shape
    return pl.pallas_call(
        gather_kernel,
        in_specs=[WHOLE],
        out_specs=HBM,
        out_shape=jax.ShapeDtypeStruct((8, n, model), BF16),
        scratch_shapes=[
            pltpu.SemaphoreType.DMA((AG_COPIES,)),
            pltpu.SemaphoreType.DMA((AG_COPIES,)),
            pltpu.SemaphoreType.DMA(()),
        ],
        compiler_params=params(16, collective_id=number, has_side_effects=True),
        name="gather_block",
        **light(),
    )(block).reshape(8 * n, model)


def forward_kernel(
    a_ref, w_ref, x_ref, gain_ref, res_ref, inv_ref, out_ref,
    block, cs, cr, q, xr, yr, tr, br, send, recv, local,
):
    wires = Wires(send, recv)
    wires.greet()

    def emit(rows, total):
        residual = x_ref[rows, :].astype(F32) + total
        inverse = lax.rsqrt(jnp.mean(residual * residual, axis=1, keepdims=True) + EPS)
        res_ref[rows, :] = residual
        inv_ref[rows, :] = inverse
        block[rows, :] = (residual * inverse * gain_ref[...]).astype(BF16)

    reduce_phase(wires, [(a_ref, w_ref)], cs, cr, q, xr, yr, tr, br, emit)
    gather_phase(wires, block, out_ref, local)
    wires.finish()


def project_out(o, w_out, inputs, gain):
    n, model = inputs.shape
    copies = RS_COPIES + AG_COPIES
    residual, inverse, gathered = pl.pallas_call(
        forward_kernel,
        in_specs=[WHOLE] * 4,
        out_specs=[WHOLE, WHOLE, HBM],
        out_shape=[
            jax.ShapeDtypeStruct((n, model), F32),
            jax.ShapeDtypeStruct((n, 1), F32),
            jax.ShapeDtypeStruct((8, n, model), BF16),
        ],
        scratch_shapes=[pltpu.VMEM((n, model), BF16)]
        + reduce_scratch(n, model)
        + [
            pltpu.SemaphoreType.DMA((copies,)),
            pltpu.SemaphoreType.DMA((copies,)),
            pltpu.SemaphoreType.DMA(()),
        ],
        compiler_params=params(52, collective_id=2, has_side_effects=True),
        name="project_out",
        **light(),
    )(o.reshape(8, n, -1), w_out, inputs, gain)
    return residual, inverse, gathered.reshape(8 * n, model)


def middle_kernel(count, *refs):
    pairs = [(refs[2 * i], refs[2 * i + 1]) for i in range(count)]
    (dout_ref, res_ref, inv_ref, gain_ref, dres_ref, out_ref,
     block, cs, cr, q, xr, yr, tr, br, send, recv, local) = refs[2 * count :]
    wires = Wires(send, recv)
    wires.greet()

    def emit(rows, total):
        inverse = inv_ref[rows, :]
        normed = res_ref[rows, :] * inverse
        e = total * gain_ref[...]
        back = inverse * (e - normed * jnp.mean(e * normed, axis=1, keepdims=True))
        dres = dout_ref[rows, :].astype(F32) + back
        dres_ref[rows, :] = dres
        block[rows, :] = dres.astype(BF16)

    reduce_phase(wires, pairs, cs, cr, q, xr, yr, tr, br, emit)
    gather_phase(wires, block, out_ref, local)
    wires.finish()


def feed_back(pairs, dout, residual, inverse, gain):
    n, model = dout.shape
    copies = RS_COPIES + AG_COPIES
    args, specs = [], []
    for a, w in pairs:
        k = a.shape[1]
        args += [a.reshape(8, n, k), w]
        specs += [WHOLE, pl.BlockSpec((model, k), lambda i: (0, 0))]
    specs[0::2] = [pl.BlockSpec((8, n, a.shape[1]), lambda i: (0, 0, 0)) for a, w in pairs]
    flat = pl.BlockSpec((n, model), lambda i: (0, 0))
    thin = pl.BlockSpec((n, 1), lambda i: (0, 0))
    dres, gathered = pl.pallas_call(
        functools.partial(middle_kernel, len(pairs)),
        grid=(1,),
        in_specs=specs + [flat, flat, thin, pl.BlockSpec((1, model), lambda i: (0, 0))],
        out_specs=[flat, HBM],
        out_shape=[
            jax.ShapeDtypeStruct((n, model), F32),
            jax.ShapeDtypeStruct((8, n, model), BF16),
        ],
        scratch_shapes=[pltpu.VMEM((n, model), BF16)]
        + reduce_scratch(n, model)
        + [
            pltpu.SemaphoreType.DMA((copies,)),
            pltpu.SemaphoreType.DMA((copies,)),
            pltpu.SemaphoreType.DMA(()),
        ],
        compiler_params=params(60, collective_id=3, has_side_effects=True),
        name="feed_back",
        **light(),
    )(*args, dout, residual, inverse, gain)
    return dres, gathered.reshape(8 * n, model)


def last_kernel(
    a_ref, w_ref, x_ref, inv_ref, gain_ref, dres_ref, out_ref,
    cs, cr, q, xr, yr, tr, br, send, recv,
):
    wires = Wires(send, recv)
    wires.greet()

    def emit(rows, total):
        inverse = inv_ref[rows, :]
        normed = x_ref[rows, :].astype(F32) * inverse
        e = total * gain_ref[...]
        back = inverse * (e - normed * jnp.mean(e * normed, axis=1, keepdims=True))
        out_ref[rows, :] = dres_ref[rows, :] + back

    reduce_phase(wires, [(a_ref, w_ref)], cs, cr, q, xr, yr, tr, br, emit)
    wires.finish()


def input_back(dqkv, w, inputs, inverse, gain, dres):
    n, model = inputs.shape
    return pl.pallas_call(
        last_kernel,
        in_specs=[WHOLE] * 6,
        out_specs=WHOLE,
        out_shape=jax.ShapeDtypeStruct((n, model), F32),
        scratch_shapes=reduce_scratch(n, model)
        + [
            pltpu.SemaphoreType.DMA((RS_COPIES,)),
            pltpu.SemaphoreType.DMA((RS_COPIES,)),
        ],
        compiler_params=params(52, collective_id=4, has_side_effects=True),
        name="input_back",
        **light(),
    )(dqkv.reshape(8, n, -1), w, inputs, inverse, gain, dres)


def normalize(value_states, gain):
    inverse = lax.rsqrt(jnp.mean(value_states * value_states, axis=-1, keepdims=True) + EPS)
    return (value_states * inverse * gain.astype(jnp.float32), inverse)


def dot(left, right):
    return jnp.dot(left, right, preferred_element_type=jnp.float32)


def outer_product(left, right):
    return lax.dot_general(
        left, right, (((0,), (0,)), ((), ())), preferred_element_type=jnp.float32
    )


def times_transposed(left, right):
    return lax.dot_general(
        left, right, (((1,), (1,)), ((), ())), preferred_element_type=jnp.float32
    )


def body(
    inputs,
    grad_output,
    segments,
    attention_gain,
    query_weight,
    key_matrix,
    value_matrix,
    output_weight,
    feedforward_gain,
    gate_weight,
    up_weight,
    down_weight,
):
    grid = Grid()
    bf16 = jnp.bfloat16
    model = inputs.shape[1]
    length = inputs.shape[0] * 8
    hidden = gate_weight.shape[1] // 2
    qdim = query_weight.shape[1] // 2
    kdim = key_matrix.shape[1] // 2
    cuts = []
    at = 0
    for n in FF_CHUNKS:
        cuts.append((at, at + n))
        at += n

    gains = slot_zero(
        grid,
        [
            jnp.broadcast_to(
                jnp.stack([attention_gain, feedforward_gain], -1)[:, None, :],
                (attention_gain.shape[0], 2, 2),
            )
        ],
    )
    gains = gather_weight(grid, gains)
    gain_one, gain_two = gains[:, 0], gains[:, 1]
    w_attn = gather_weight(
        grid,
        slot_zero(grid, [halves(query_weight), halves(key_matrix), halves(value_matrix)]),
    )
    w_out = gather_weight(grid, slot_zero(grid, [halves(output_weight.T)]))
    gate_h, up_h, down_h = halves(gate_weight), halves(up_weight), halves(down_weight.T)
    w_ff = [
        gather_weight(grid, slot_zero(grid, [v[:, :, a:b] for v in (gate_h, up_h, down_h)]))
        for a, b in cuts
    ]

    me = jnp.reshape(grid.me, (1,)).astype(jnp.int32)
    heads = qdim // HEAD_SIZE
    spread = spread_matrix(heads + kdim // HEAD_SIZE, kdim // HEAD_SIZE)
    spread_out = spread_matrix(0, heads)
    gain_one = gain_one.astype(F32)[None, :]
    gain_two = gain_two.astype(F32)[None, :]
    own = rotated(grid, inputs)
    normed_one, inverse_one = normalize(own.astype(F32), gain_one)
    a1 = gather_block(normed_one.astype(bf16), 0)
    dout = rotated(grid, grad_output)
    dout_all = gather_tokens(grid, dout)
    cosine, sine = rope_tables(length, grid.z * length, HEAD_SIZE)
    padded_ids = jnp.concatenate([jnp.full((WINDOW_LENGTH,), -1, jnp.int32), segments])
    key_ids = lax.dynamic_slice_in_dim(padded_ids, grid.z * length, length + WINDOW_LENGTH, 0)
    kid, qid = key_ids[:, None], key_ids[None, WINDOW_LENGTH:]
    w_pad = dot(w_attn, spread).astype(bf16)
    w_out_pad = dot(w_out, spread_out).astype(bf16)
    q, k, v = project_qkv(me, a1, w_pad, cosine, sine)
    edge = grid.step(
        jnp.concatenate([k[length - WINDOW_LENGTH :], v[length - WINDOW_LENGTH :]], 1), 1
    )
    k_all = jnp.concatenate([edge[:, :LANES], k], 0)
    v_all = jnp.concatenate([edge[:, LANES:], v], 0)
    o, lse = attend(me, q, k_all, v_all, kid, qid)
    residual, inverse_two, a2 = project_out(o, w_out_pad, own, gain_two)

    result = jnp.zeros((length, model), F32)
    ff_grads, back_pairs = [], []
    for (a, b), w in zip(cuts, w_ff):
        n = b - a
        mixed, dgu = hidden_units(a2, dout_all, w)
        back_pairs.append((dgu, w))
        result = result + times_transposed(mixed, w[:, 2 * n :])
        partial = jnp.concatenate(
            [outer_product(a2, dgu), outer_product(dout_all, mixed)], 1
        ).astype(bf16)
        ff_grads.append(scatter_weight(grid, partial))
    dresidual, da_all = feed_back(back_pairs, dout, residual, inverse_two, gain_two)
    result = residual + scatter_tokens(grid, result.astype(bf16))
    layer_output = rotated(grid, result.astype(bf16))

    do = dot(da_all, w_out_pad).astype(bf16)
    dq, dk, dv = attend_back(me, q, do, k_all, v_all, kid, qid, lse, cosine, sine)
    back = grid.step(
        jnp.concatenate([dk[:WINDOW_LENGTH], dv[:WINDOW_LENGTH]], 1).astype(bf16), -1
    ).astype(F32)
    back = jnp.concatenate([jnp.zeros((length - WINDOW_LENGTH, 2 * LANES), F32), back], 0)
    dk = (dk[WINDOW_LENGTH:] + back[:, :LANES]) * SCALE
    dv = dv[WINDOW_LENGTH:] + back[:, LANES:]
    dk = dk * cosine - jnp.roll(dk, LANES // 2, 1) * sine
    dkv = natural(grid, jnp.concatenate([dk, dv], 1).astype(bf16))
    dqkv = jnp.concatenate([dq, dkv], 1)
    attn_grad = scatter_weight(
        grid, outer_product(a1, times_transposed(dqkv, spread).astype(bf16)).astype(bf16)
    )
    input_gradient = rotated(
        grid, input_back(dqkv, w_pad, own, inverse_one, gain_one, dresidual)
    )
    out_grad = scatter_weight(
        grid, times_transposed(outer_product(da_all, o).astype(bf16), spread_out).astype(bf16)
    )

    def whole(part):
        return part.reshape(part.shape[0], -1)

    query_grad = whole(attn_grad[:, :, :qdim])
    key_grad = whole(attn_grad[:, :, qdim : qdim + kdim])
    value_grad = whole(attn_grad[:, :, qdim + kdim :])
    output_grad = whole(out_grad).T
    parts = []
    for k in range(3):
        parts.append(
            whole(
                jnp.concatenate(
                    [g[:, :, k * (b - a) : (k + 1) * (b - a)] for (a, b), g in zip(cuts, ff_grads)],
                    2,
                )
            )
        )
    gate_grad, up_grad, down_grad = parts[0], parts[1], parts[2].T

    def row_sum(*both):
        return sum(
            jnp.sum(w.astype(jnp.float32) * g, axis=1) for w, g in both
        )

    sums = jnp.stack(
        [
            row_sum((query_weight, query_grad), (key_matrix, key_grad), (value_matrix, value_grad)),
            row_sum((gate_weight, gate_grad), (up_weight, up_grad)),
        ]
    )
    sums = sums + grid.swap(sums, C)
    sums = sums + grid.swap(sums, X)
    return (
        layer_output,
        input_gradient,
        sums[0] / attention_gain.astype(jnp.float32),
        query_grad,
        key_grad,
        value_grad,
        output_grad,
        sums[1] / feedforward_gain.astype(jnp.float32),
        gate_grad,
        up_grad,
        down_grad,
    )


def solution(mesh):
    in_specs = (
        P(("tok", "mp"), None),
        P(("tok", "mp"), None),
        P(),
        P("tok"),
        P("tok", "mp"),
        P("tok", "mp"),
        P("tok", "mp"),
        P("mp", "tok"),
        P("tok"),
        P("tok", "mp"),
        P("tok", "mp"),
        P("mp", "tok"),
    )
    out_specs = (
        P(("tok", "mp"), None),
        P(("tok", "mp"), None),
        P("tok"),
        P("tok", "mp"),
        P("tok", "mp"),
        P("tok", "mp"),
        P("mp", "tok"),
        P("tok"),
        P("tok", "mp"),
        P("tok", "mp"),
        P("mp", "tok"),
    )
    return jax.shard_map(body, mesh=mesh, in_specs=in_specs, out_specs=out_specs, check_vma=False)
```

time: 1990 us -> 1170 us (0.59)
  waiting for transfers between devices: 1350 us -> 370 us
  Pallas kernels: 0 us -> 421 us
  matrix products: 346 us -> 113 us
  blocking collectives: 151 us -> 0 us
  local copies, waits for them, and re-layouts: 29.1 us -> 127 us
  starting transfers between devices: 8.74 us -> 42.9 us
    reduce_scatter x10 -> x0, waiting for transfers between devices: 714 us -> none  [the longest x1 160 us: body(): lax.psum_scatter(up_grad.astype(jnp.bfloat16), 'tok', scatter_dimension=0...]
    all_gather x10 -> x0, waiting for transfers between devices: 499 us -> none  [the longest x1 137 us: fetch(): lax.all_gather(down_weight, 'tok', axis=1, tiled=True)]
    pallas_call x0 -> x9, Pallas kernels: none -> 421 us  [the longest x1 108 us: feed_back(): pl.pallas_call(functools.partial(middle_kernel, len(pairs)), grid=(1,), i...]
    ppermute x4 -> x52, waiting for transfers between devices: 0.01 us -> 370 us  [the longest x27 298 us: ring(): lax.ppermute(value, AXES, self.pairs(lambda z, g: ((z + 1) % self.nz, g)))]
    dot_general x45 -> x3, matrix products: 195 us -> 17.3 us  [dot(): return jnp.dot(left, right, preferred_element_type=jnp.float32)]
    unnamed x24 -> x0, waiting for transfers between devices: 134 us -> none
    unnamed x2 -> x0, blocking collectives: 74.1 us -> none
    all_gather x2 -> x0, blocking collectives: 66.6 us -> none  [the longest x1 33.8 us: fetch(): lax.all_gather(value_matrix, 'tok', axis=0, tiled=True)]
  transfers between devices with their start and end apart: 26 -> 52, of which waited for: 19 -> 23; matrix products, arithmetic and copies ran while one was open for 17% -> 25% of each run, Pallas kernels for 0% -> 36%
where the time goes in v1:
time: 1170 us; the launch traced here: 1160 us
  Pallas kernels  421 us (36%)
  waiting for transfers between devices  370 us (32%)
  local copies, waits for them, and re-layouts  127 us (11%)
  matrix products  113 us (10%)
  other arithmetic  84.9 us (7%)
  starting transfers between devices  42.9 us (4%)
    ppermute x27, waiting for transfers between devices, ring(): lax.ppermute(value, AXES, self.pairs(lambda z, g: ((z + 1) % self.nz, g)))  298 us
    pallas_call x1, Pallas kernels, feed_back(): pl.pallas_call(functools.partial(middle_kernel, len(pairs)), grid=(1,), i...  108 us
    pallas_call x1, Pallas kernels, project_out(): pl.pallas_call(forward_kernel, in_specs=[WHOLE] * 4, out_specs=[WHOLE, WH...  103 us
    ppermute x23, waiting for transfers between devices, swap(): return lax.ppermute(value, AXES, self.pairs(lambda z, g: (z, g ^ bit)))  66.7 us
    dot_general x5, matrix products, outer_product(): lax.dot_general(left, right, (((0,), (0,)), ((), ())), preferred_element_...  60 us
    pallas_call x1, Pallas kernels, input_back(): pl.pallas_call(last_kernel, in_specs=[WHOLE] * 6, out_specs=WHOLE, out_sh...  57.8 us
    unnamed x202, local copies, waits for them, and re-layouts  52.6 us
    pallas_call x1, Pallas kernels, gather_block(): pl.pallas_call(gather_kernel, in_specs=[WHOLE], out_specs=HBM, out_shape=...  49 us
  transfers between devices with their start and end apart: 52, of which 23 were waited for; matrix products, arithmetic and copies ran while one was open for 25% of the time, Pallas kernels for 36%

profile of v1, /device:TPU:0, one launch (start us, length us, event | category | flops | bytes accessed | tf_op | source)
XLA Modules:
  0.0 1161.8 jit_solution(2154925153120322274)
XLA Ops:
  30.0 3.7 fusion.29
  45.1 4.8 collective-permute-done.2
  52.1 3.3 collective-permute-done.3
  63.8 49.0 %gather_block.1 = bf16[8,256,2560]{2,1,0:T(8,128)(2,1)S(1)} custom-call(bf16[256,2560]{1,0:T(8,128)(2,1)S(1)} %fusion.3.block), custom_call_target="tpu_custom_call" | custom-call | flops 1000000 | bytes 100000 | tf_op jit(solution)/shard_map/gather_block/pallas_call | solution.py:551
  112.9 3.8 copy-done
  136.3 14.7 %collective-permute-done.20 = bf16[320,1536]{1,0:T(8,128)(2,1)S(1)} collective-permute-done((bf16[320,1536]{1,0:T(8,128)(2,1)}, bf16[320,1536]{1,0:T(8,128)(2,1)S(1)}, u32[]{:S(2)}, u32[]{:S(2)}) %collective-permute-start.20) | collective-permute-done | bytes 983072 | tf_op jit(solution)/shard_map/ppermute | solution.py:38
  155.5 11.7 %collective-permute-done.11 = bf16[640,320]{1,0:T(8,128)(2,1)S(1)} collective-permute-done((bf16[640,320]{1,0:T(8,128)(2,1)}, bf16[640,320]{1,0:T(8,128)(2,1)S(1)}, u32[]{:S(2)}, u32[]{:S(2)}) %collective-permute-start.11) | collective-permute-done | bytes 409632 | tf_op jit(solution)/shard_map/ppermute | solution.py:41
  171.3 3.4 pad_maximum_fusion.1
  181.2 39.5 %collective-permute-done.12 = bf16[640,320]{1,0:T(8,128)(2,1)S(1)} collective-permute-done((bf16[640,320]{1,0:T(8,128)(2,1)S(1)}, bf16[640,320]{1,0:T(8,128)(2,1)S(1)}, u32[]{:S(2)}, u32[]{:S(2)}) %collective-permute-start.12) | collective-permute-done | bytes 409632 | tf_op jit(solution)/shard_map/ppermute | solution.py:41
  226.2 52.9 %collective-permute-done.7 = bf16[640,480]{0,1:T(8,128)(2,1)} collective-permute-done((bf16[640,480]{0,1:T(8,128)(2,1)S(1)}, bf16[640,480]{0,1:T(8,128)(2,1)}, u32[]{:S(2)}, u32[]{:S(2)}) %collective-permute-start.7) | collective-permute-done | bytes 614432 | tf_op jit(solution)/shard_map/ppermute | solution.py:41
  279.1 4.9 concatenate.137
  284.0 4.0 convolution_convert_fusion.2.w_ref
  288.1 12.8 %project_qkv.1 = (bf16[2048,512]{1,0:T(8,128)(2,1)S(1)}, bf16[2048,128]{1,0:T(8,128)(2,1)S(1)}, bf16[2048,128]{1,0:T(8,128)(2,1)S(1)}) custom-call(s32[1]{0:T(128)} %bitcast.me_ref, bf16[2048,2560]{1,0:T(8,128)(2,1)} %bitcast.175, bf16[2560,768]{1,0:T(8,128)(2,1)S(1)} %convolution_convert_fusion.2.w_ref, f32[2048,128]{1,0:T(8,128)S(1)} %get-tuple-element.100.cos_ref, ...), custom_call_target="tpu_custom_call" | custom-call | flops 1000000 | bytes 100000 | tf_op jit(solution)/shard_map/project_qkv/pallas_call | solution.py:210
  305.1 3.9 collective-permute-done.8
  309.2 18.8 %attend.1 = (bf16[2048,512]{1,0:T(8,128)(2,1)S(1)}, f32[8,4,256]{2,1,0:T(4,128)S(1)}) custom-call(s32[1]{0:T(128)} %bitcast.me_ref, bf16[2048,512]{1,0:T(8,128)(2,1)S(1)} %get-tuple-element.28.q_ref, bf16[2560,128]{1,0:T(8,128)(2,1)S(1)} %pad_maximum_fusion.18.k_ref, bf16[2560,128]{1,0:T(8,128)(2,1)S(1)} %pad_maximum_fusion.19.v_ref, ...), custom_call_target="tpu_custom_call" | custom-call | flops 1000000 | bytes 100000 | tf_op jit(solution)/shard_map/attend/pallas_call | solution.py:271
  330.0 103.2 %project_out.1 = (f32[256,2560]{1,0:T(8,128)}, f32[256,1]{1,0:T(8,128)S(1)}, bf16[8,256,2560]{2,1,0:T(8,128)(2,1)}) custom-call(bf16[8,256,512]{2,1,0:T(8,128)(2,1)} %bitcast.177, bf16[2560,512]{1,0:T(8,128)(2,1)} %convolution_convert_fusion.5.w_ref, bf16[256,2560]{1,0:T(8,128)(2,1)S(1)} %get-tuple-element.60.x_ref, ...), custom_call_target="tpu_custom_call" | custom-call | flops 1000000 | bytes 100000 | tf_op jit(solution)/shard_map/project_out/pallas_call | solution.py:589
  451.9 29.1 %collective-permute-done.22 = bf16[640,1536]{1,0:T(8,128)(2,1)} collective-permute-done((bf16[640,1536]{1,0:T(8,128)(2,1)}, bf16[640,1536]{1,0:T(8,128)(2,1)}, u32[]{:S(2)}, u32[]{:S(2)}) %collective-permute-start.22) | collective-permute-done | bytes 1966112 | tf_op jit(solution)/shard_map/ppermute | solution.py:41
  484.9 27.6 %collective-permute-done.27 = bf16[640,1152]{1,0:T(8,128)(2,1)S(1)} collective-permute-done((bf16[640,1152]{1,0:T(8,128)(2,1)S(1)}, bf16[640,1152]{1,0:T(8,128)(2,1)S(1)}, u32[]{:S(2)}, u32[]{:S(2)}) %collective-permute-start.27) | collective-permute-done | bytes 1474592 | tf_op jit(solution)/shard_map/ppermute | solution.py:41
  513.8 22.6 %hidden_units.3 = (bf16[2048,384]{1,0:T(8,128)(2,1)}, bf16[2048,768]{1,0:T(8,128)(2,1)}) custom-call(bf16[2048,2560]{1,0:T(8,128)(2,1)} %bitcast.198, bf16[2048,2560]{1,0:T(8,128)(2,1)} %constant_dynamic-update-slice_fusion.5.d_ref, bf16[2560,1152]{1,0:T(8,128)(2,1)} %constant_dynamic-update-slice_fusion.17.w_ref.refs_3_), custom_call_target="tpu_custom_call" | custom-call | flops 1000000 | bytes 100000 | tf_op jit(solution)/shard_map/hidden_units/pallas_call | solution.py:393
  536.3 8.8 convolution_convert_fusion.7
  545.2 11.8 %convolution_convert_fusion.1 = bf16[2560,768]{0,1:T(8,128)(2,1)S(1)} fusion(bf16[2048,2560]{1,0:T(8,128)(2,1)} %bitcast.199, bf16[2048,768]{1,0:T(8,128)(2,1)S(1)} %copy-done.50), kind=kOutput, calls=%fused_computation.18 | convolution fusion | flops 8055029760 | bytes 17563648 | tf_op jit(solution)/shard_map/dot_general | solution.py:713
  559.5 11.5 fusion.9
  571.0 21.3 %collective-permute-done.42 = bf16[640,1152]{0,1:T(8,128)(2,1)S(1)} collective-permute-done((bf16[640,1152]{0,1:T(8,128)(2,1)S(1)}, bf16[640,1152]{0,1:T(8,128)(2,1)S(1)}, u32[]{:S(2)}, u32[]{:S(2)}) %collective-permute-start.42) | collective-permute-done | bytes 1474592 | tf_op jit(solution)/shard_map/ppermute | solution.py:41
  597.3 23.6 %hidden_units.2 = (bf16[2048,512]{1,0:T(8,128)(2,1)}, bf16[2048,1024]{1,0:T(8,128)(2,1)}) custom-call(bf16[2048,2560]{1,0:T(8,128)(2,1)} %bitcast.200, bf16[2048,2560]{1,0:T(8,128)(2,1)} %constant_dynamic-update-slice_fusion.5.d_ref, bf16[2560,1536]{1,0:T(8,128)(2,1)} %constant_dynamic-update-slice_fusion.12.w_ref.refs_1_), custom_call_target="tpu_custom_call" | custom-call | flops 1000000 | bytes 100000 | tf_op jit(solution)/shard_map/hidden_units/pallas_call | solution.py:393
  620.9 16.7 %convolution_convert_fusion = bf16[2560,1024]{0,1:T(8,128)(2,1)} fusion(bf16[2048,2560]{1,0:T(8,128)(2,1)} %bitcast.201, bf16[2048,1024]{1,0:T(8,128)(2,1)} %get-tuple-element.36), kind=kOutput, calls=%fused_computation.15 | convolution fusion | flops 10740039680 | bytes 19922944 | tf_op jit(solution)/shard_map/dot_general | solution.py:713
  637.6 108.2 %feed_back.1 = (f32[256,2560]{1,0:T(8,128)}, bf16[8,256,2560]{2,1,0:T(8,128)(2,1)}) custom-call(bf16[8,256,1024]{2,1,0:T(8,128)(2,1)} %bitcast.215, bf16[2560,1536]{1,0:T(8,128)(2,1)} %constant_dynamic-update-slice_fusion.12.w_ref.refs_1_, bf16[8,256,768]{2,1,0:T(8,128)(2,1)} %bitcast.216, ...), custom_call_target="tpu_custom_call" | custom-call | flops 1000000 | bytes 100000 | tf_op jit(solution)/shard_map/feed_back/pallas_call | solution.py:644
  745.8 10.1 convolution_convert_fusion.9.do_ref
  755.9 10.8 convolution_convert_fusion.8
  766.7 10.2 convolution_convert_fusion.4
  777.0 3.7 fusion.7
  782.0 24.5 %attend_back.1 = (bf16[2048,512]{1,0:T(8,128)(2,1)S(1)}, f32[2560,128]{1,0:T(8,128)S(1)}, f32[2560,128]{1,0:T(8,128)S(1)}) custom-call(s32[1]{0:T(128)} %bitcast.me_ref, bf16[2048,512]{1,0:T(8,128)(2,1)S(1)} %copy-done.5, bf16[2048,512]{1,0:T(8,128)(2,1)S(1)} %copy-done.13, bf16[2560,128]{1,0:T(8,128)(2,1)S(1)} %copy-done.9, ...), custom_call_target="tpu_custom_call" | custom-call | flops 1000000 | bytes 100000 | tf_op jit(solution)/shard_map/attend_back/pallas_call | solution.py:343
  813.7 13.7 %add_convert_fusion = bf16[2048,2560]{1,0:T(8,128)(2,1)} fusion(f32[2048,2560]{1,0:T(8,128)} %fusion.9, bf16[2048,512]{1,0:T(8,128)(2,1)} %get-tuple-element.34, bf16[2560,1536]{1,0:T(8,128)(2,1)} %constant_dynamic-update-slice_fusion.12.w_ref.refs_1_), kind=kOutput, calls=%fused_computation | convolution fusion | flops 5379194880 | bytes 36175872 | tf_op jit(solution)/shard_map/dot_general | solution.py:719
  827.4 5.1 slice_bitcast_fusion
  839.2 12.6 %convolution_convert_fusion.6 = bf16[2560,480]{0,1:T(8,128)(2,1)} fusion(bf16[2048,2560]{1,0:T(8,128)(2,1)} %bitcast.176, s32[480]{0:T(512)S(1)} %copy-done.85, bf16[2048,256]{1,0:T(8,128)(2,1)} %copy-done.61, bf16[2048,512]{1,0:T(8,128)(2,1)S(1)} %copy-done.11), kind=kOutput, calls=%fused_computation.23 | convolution fusion | flops 6551986176 | bytes 16091008 | tf_op jit(solution)/shard_map/dot_general | solution.py:713
  858.5 57.8 %input_back.1 = f32[256,2560]{1,0:T(8,128)} custom-call(bf16[8,256,768]{2,1,0:T(8,128)(2,1)} %bitcast.204, bf16[2560,768]{1,0:T(8,128)(2,1)} %copy-done.1, bf16[256,2560]{1,0:T(8,128)(2,1)S(1)} %get-tuple-element.60.x_ref, f32[256,1]{1,0:T(8,128)S(1)} %copy.133.inv_ref, f32[1,2560]{1,0:T(1,128)S(1)} %copy-done.18, f32[256,2560]{1,0:T(8,128)} %get-tuple-element.44.dres_ref), custom_call_target="tpu_custom_call" | custom-call | flops 1000000 | bytes 100000 | tf_op jit(solution)/shard_map/input_back/pallas_call | solution.py:687
  924.2 8.6 collective-permute-done.50
  934.3 10.9 collective-permute-done.35
  953.7 12.6 %collective-permute-done.36 = bf16[640,480]{0,1:T(8,128)(2,1)S(1)} collective-permute-done((bf16[640,480]{0,1:T(8,128)(2,1)}, bf16[640,480]{0,1:T(8,128)(2,1)S(1)}, u32[]{:S(2)}, u32[]{:S(2)}) %collective-permute-start.36) | collective-permute-done | bytes 614432 | tf_op jit(solution)/shard_map/ppermute | solution.py:41
  970.8 3.7 add_convert_fusion.3
  989.9 8.1 collective-permute-done.44
  1001.2 3.6 copy.139
  1007.0 31.3 %collective-permute-done.39 = bf16[640,1536]{0,1:T(8,128)(2,1)} collective-permute-done((bf16[640,1536]{0,1:T(8,128)(2,1)}, bf16[640,1536]{0,1:T(8,128)(2,1)}, u32[]{:S(2)}, u32[]{:S(2)}) %collective-permute-start.39) | collective-permute-done | bytes 1966112 | tf_op jit(solution)/shard_map/ppermute | solution.py:41
  1038.4 3.7 add_convert_fusion.2
  1044.1 6.2 fusion
  1053.7 33.6 %collective-permute-done.40 = bf16[640,1536]{0,1:T(8,128)(2,1)} collective-permute-done((bf16[640,1536]{0,1:T(8,128)(2,1)}, bf16[640,1536]{0,1:T(8,128)(2,1)}, u32[]{:S(2)}, u32[]{:S(2)}) %collective-permute-start.40) | collective-permute-done | bytes 1966112 | tf_op jit(solution)/shard_map/ppermute | solution.py:41
  1098.1 20.1 %collective-permute-done.41 = bf16[320,1536]{1,0:T(8,128)(2,1)S(1)} collective-permute-done((bf16[320,1536]{1,0:T(8,128)(2,1)S(1)}, bf16[320,1536]{1,0:T(8,128)(2,1)S(1)}, u32[]{:S(2)}, u32[]{:S(2)}) %collective-permute-start.41) | collective-permute-done | bytes 983072 | tf_op jit(solution)/shard_map/ppermute | solution.py:38
  1124.5 18.5 %collective-permute-done.31 = bf16[2,128,2560]{2,1,0:T(8,128)(2,1)S(1)} collective-permute-done((bf16[2,128,2560]{2,1,0:T(8,128)(2,1)S(1)}, bf16[2,128,2560]{2,1,0:T(8,128)(2,1)S(1)}, u32[]{:S(2)}, u32[]{:S(2)}) %collective-permute-start.31) | collective-permute-done | bytes 1310752 | tf_op jit(solution)/shard_map/ppermute | solution.py:38
  1148.3 8.7 collective-permute-done.47
  (449 shorter events, 225.6 us)
Async XLA Ops:
  5.4 161.9 %collective-permute-start.15 = (bf16[256,2560]{1,0:T(8,128)(2,1)}, bf16[256,2560]{1,0:T(8,128)(2,1)}, u32[]{:S(2)}, u32[]{:S(2)}) collective-permute-start(bf16[256,2560]{1,0:T(8,128)(2,1)} %get-tuple-element.87.refs_4_), channel_id=1, source_target_pairs={{0,4},{1,5},{2,6},{3,7},{4,0},{5,1},{6,2},{7,3},{8,12},{9,13},{10,... | collective-permute-start | bytes 3932168 | tf_op jit(solution)/shard_map/ppermute | solution.py:38
  8.3 160.1 %collective-permute-start.14 = (bf16[256,2560]{1,0:T(8,128)(2,1)}, bf16[256,2560]{1,0:T(8,128)(2,1)}, u32[]{:S(2)}, u32[]{:S(2)}) collective-permute-start(bf16[256,2560]{1,0:T(8,128)(2,1)} %get-tuple-element.87.refs_4_), channel_id=1, source_target_pairs={{0,2},{1,3},{2,0},{3,1},{4,6},{5,7},{6,4},{7,5},{8,10},{9,11},{10,... | collective-permute-start | bytes 3932168 | tf_op jit(solution)/shard_map/ppermute | solution.py:38
  9.9 28.4 %collective-permute-start = (bf16[320,2]{0,1:T(2,128)(2,1)S(1)}, bf16[320,2]{0,1:T(2,128)(2,1)S(1)}, u32[]{:S(2)}, u32[]{:S(2)}) collective-permute-start(bf16[320,2]{0,1:T(2,128)(2,1)S(1)} %pad_maximum_fusion.25), channel_id=1, source_target_pairs={{0,4},{1,5},{2,6},{3,7},{4,0},{5,1},{6,2},{7,3},{8,12},{9,13},{10,... | collective-permute-start | bytes 3848 | tf_op jit(solution)/shard_map/ppermute | solution.py:38
  13.1 103.6 %collective-permute-start.4 = (bf16[320,480]{1,0:T(8,128)(2,1)}, bf16[320,480]{1,0:T(8,128)(2,1)}, u32[]{:S(2)}, u32[]{:S(2)}) collective-permute-start(bf16[320,480]{1,0:T(8,128)(2,1)} %dynamic-slice_bitcast_fusion.5), channel_id=1, source_target_pairs={{0,4},{1,5},{2,6},{3,7},{4,0},{5,1},{6,2},{7,3},{8,12},{9,13},{10,... | collective-permute-start | bytes 921608 | tf_op jit(solution)/shard_map/ppermute | solution.py:38
  17.6 41.4 %collective-permute-start.9 = (bf16[320,320]{1,0:T(8,128)(2,1)}, bf16[320,320]{1,0:T(8,128)(2,1)}, u32[]{:S(2)}, u32[]{:S(2)}) collective-permute-start(bf16[320,320]{1,0:T(8,128)(2,1)} %bitcast.174), channel_id=1, source_target_pairs={{0,4},{1,5},{2,6},{3,7},{4,0},{5,1},{6,2},{7,3},{8,12},{9,13},{10,... | collective-permute-start | bytes 614408 | tf_op jit(solution)/shard_map/ppermute | solution.py:38
  55.4 75.1 %collective-permute-start.24 = (bf16[320,1152]{1,0:T(8,128)(2,1)}, bf16[320,1152]{1,0:T(8,128)(2,1)}, u32[]{:S(2)}, u32[]{:S(2)}) collective-permute-start(bf16[320,1152]{1,0:T(8,128)(2,1)} %dynamic-slice_bitcast_fusion.3), channel_id=1, source_target_pairs={{0,4},{1,5},{2,6},{3,7},{4,0},{5,1},{6,2},{7,3},{8,12},{9,13},{10,... | collective-permute-start | bytes 2211848 | tf_op jit(solution)/shard_map/ppermute | solution.py:38
  62.4 64.6 %collective-permute-start.10 = (bf16[640,320]{1,0:T(8,128)(2,1)}, bf16[640,320]{1,0:T(8,128)(2,1)}, u32[]{:S(2)}, u32[]{:S(2)}) collective-permute-start(bf16[640,320]{1,0:T(8,128)(2,1)} %pad_maximum_fusion.20), channel_id=1, source_target_pairs={{0,8},{1,9},{2,10},{3,11},{4,12},{5,13},{6,14},{7,15},{8,16},{9,17... | collective-permute-start | bytes 1228808 | tf_op jit(solution)/shard_map/ppermute | solution.py:41
  116.7 58.0 %collective-permute-start.13 = (bf16[256,2560]{1,0:T(8,128)(2,1)}, bf16[256,2560]{1,0:T(8,128)(2,1)}, u32[]{:S(2)}, u32[]{:S(2)}) collective-permute-start(bf16[256,2560]{1,0:T(8,128)(2,1)} %get-tuple-element.87.refs_4_), channel_id=1, source_target_pairs={{0,1},{1,0},{2,3},{3,2},{4,5},{5,4},{6,7},{7,6},{8,9},{9,8},{10,11... | collective-permute-start | bytes 3932168 | tf_op jit(solution)/shard_map/ppermute | solution.py:38
  127.0 24.0 %collective-permute-start.20 = (bf16[320,1536]{1,0:T(8,128)(2,1)}, bf16[320,1536]{1,0:T(8,128)(2,1)S(1)}, u32[]{:S(2)}, u32[]{:S(2)}) collective-permute-start(bf16[320,1536]{1,0:T(8,128)(2,1)} %dynamic-slice_bitcast_fusion.1), channel_id=1, source_target_pairs={{0,4},{1,5},{2,6},{3,7},{4,0},{5,1},{6,2},{7,3},{8,12},{9,13},{10,... | collective-permute-start | bytes 2949128 | tf_op jit(solution)/shard_map/ppermute | solution.py:38
  130.5 24.3 %collective-permute-start.5 = (bf16[640,480]{0,1:T(8,128)(2,1)}, bf16[640,480]{0,1:T(8,128)(2,1)S(1)}, u32[]{:S(2)}, u32[]{:S(2)}) collective-permute-start(bf16[640,480]{0,1:T(8,128)(2,1)} %copy.119), channel_id=1, source_target_pairs={{0,8},{1,9},{2,10},{3,11},{4,12},{5,13},{6,14},{7,15},{8,16},{9,17... | collective-permute-start | bytes 1843208 | tf_op jit(solution)/shard_map/ppermute | solution.py:41
  151.0 16.2 %collective-permute-start.11 = (bf16[640,320]{1,0:T(8,128)(2,1)}, bf16[640,320]{1,0:T(8,128)(2,1)S(1)}, u32[]{:S(2)}, u32[]{:S(2)}) collective-permute-start(bf16[640,320]{1,0:T(8,128)(2,1)} %collective-permute-done.10), channel_id=1, source_target_pairs={{0,8},{1,9},{2,10},{3,11},{4,12},{5,13},{6,14},{7,15},{8,16},{9,17... | collective-permute-start | bytes 1228808 | tf_op jit(solution)/shard_map/ppermute | solution.py:41
  154.9 147.4 %collective-permute-start.25 = (bf16[640,1152]{1,0:T(8,128)(2,1)}, bf16[640,1152]{1,0:T(8,128)(2,1)}, u32[]{:S(2)}, u32[]{:S(2)}) collective-permute-start(bf16[640,1152]{1,0:T(8,128)(2,1)} %pad_maximum_fusion.10), channel_id=1, source_target_pairs={{0,8},{1,9},{2,10},{3,11},{4,12},{5,13},{6,14},{7,15},{8,16},{9,17... | collective-permute-start | bytes 4423688 | tf_op jit(solution)/shard_map/ppermute | solution.py:41
  167.2 53.6 %collective-permute-start.6 = (bf16[640,480]{0,1:T(8,128)(2,1)S(1)}, bf16[640,480]{0,1:T(8,128)(2,1)S(1)}, u32[]{:S(2)}, u32[]{:S(2)}) collective-permute-start(bf16[640,480]{0,1:T(8,128)(2,1)S(1)} %collective-permute-done.5), channel_id=1, source_target_pairs={{0,8},{1,9},{2,10},{3,11},{4,12},{5,13},{6,14},{7,15},{8,16},{9,17... | collective-permute-start | bytes 1843208 | tf_op jit(solution)/shard_map/ppermute | solution.py:41
  167.3 53.4 %collective-permute-start.12 = (bf16[640,320]{1,0:T(8,128)(2,1)S(1)}, bf16[640,320]{1,0:T(8,128)(2,1)S(1)}, u32[]{:S(2)}, u32[]{:S(2)}) collective-permute-start(bf16[640,320]{1,0:T(8,128)(2,1)S(1)} %collective-permute-done.11), channel_id=1, source_target_pairs={{0,8},{1,9},{2,10},{3,11},{4,12},{5,13},{6,14},{7,15},{8,16},{9,17... | collective-permute-start | bytes 1228808 | tf_op jit(solution)/shard_map/ppermute | solution.py:41
  168.5 55.6 %collective-permute-start.17 = (bf16[128,2560]{1,0:T(8,128)(2,1)S(1)}, bf16[128,2560]{1,0:T(8,128)(2,1)S(1)}, u32[]{:S(2)}, u32[]{:S(2)}) collective-permute-start(bf16[128,2560]{1,0:T(8,128)(2,1)S(1)} %slice.303), channel_id=1, source_target_pairs={{0,2},{1,3},{2,0},{3,1},{4,6},{5,7},{6,4},{7,5},{8,10},{9,11},{10,... | collective-permute-start | bytes 1966088 | tf_op jit(solution)/shard_map/ppermute | solution.py:38
  174.7 49.5 %collective-permute-start.18 = (bf16[128,2560]{1,0:T(8,128)(2,1)S(1)}, bf16[128,2560]{1,0:T(8,128)(2,1)S(1)}, u32[]{:S(2)}, u32[]{:S(2)}) collective-permute-start(bf16[128,2560]{1,0:T(8,128)(2,1)S(1)} %slice.304), channel_id=1, source_target_pairs={{0,4},{1,5},{2,6},{3,7},{4,0},{5,1},{6,2},{7,3},{8,12},{9,13},{10,... | collective-permute-start | bytes 1966088 | tf_op jit(solution)/shard_map/ppermute | solution.py:38
  220.7 212.5 %collective-permute-start.21 = (bf16[640,1536]{1,0:T(8,128)(2,1)}, bf16[640,1536]{1,0:T(8,128)(2,1)}, u32[]{:S(2)}, u32[]{:S(2)}) collective-permute-start(bf16[640,1536]{1,0:T(8,128)(2,1)} %pad_maximum_fusion.4), channel_id=1, source_target_pairs={{0,8},{1,9},{2,10},{3,11},{4,12},{5,13},{6,14},{7,15},{8,16},{9,17... | collective-permute-start | bytes 5898248 | tf_op jit(solution)/shard_map/ppermute | solution.py:41
  220.8 58.3 %collective-permute-start.7 = (bf16[640,480]{0,1:T(8,128)(2,1)S(1)}, bf16[640,480]{0,1:T(8,128)(2,1)}, u32[]{:S(2)}, u32[]{:S(2)}) collective-permute-start(bf16[640,480]{0,1:T(8,128)(2,1)S(1)} %collective-permute-done.6), channel_id=1, source_target_pairs={{0,8},{1,9},{2,10},{3,11},{4,12},{5,13},{6,14},{7,15},{8,16},{9,17... | collective-permute-start | bytes 1843208 | tf_op jit(solution)/shard_map/ppermute | solution.py:41
  224.1 216.0 %collective-permute-start.16 = (bf16[512,2560]{1,0:T(8,128)(2,1)}, bf16[512,2560]{1,0:T(8,128)(2,1)}, u32[]{:S(2)}, u32[]{:S(2)}) collective-permute-start(bf16[512,2560]{1,0:T(8,128)(2,1)} %pad_maximum_fusion.1), channel_id=1, source_target_pairs={{0,1},{1,0},{2,3},{3,2},{4,5},{5,4},{6,7},{7,6},{8,9},{9,8},{10,11... | collective-permute-start | bytes 7864328 | tf_op jit(solution)/shard_map/ppermute | solution.py:38
  226.2 223.2 %collective-permute-start.19 = (bf16[256,2560]{1,0:T(8,128)(2,1)}, bf16[256,2560]{1,0:T(8,128)(2,1)}, u32[]{:S(2)}, u32[]{:S(2)}) collective-permute-start(bf16[256,2560]{1,0:T(8,128)(2,1)} %pad_maximum_fusion.12), channel_id=1, source_target_pairs={{0,1},{1,0},{2,3},{3,2},{4,5},{5,4},{6,7},{7,6},{8,9},{9,8},{10,11... | collective-permute-start | bytes 3932168 | tf_op jit(solution)/shard_map/ppermute | solution.py:38
  301.0 8.0 collective-permute-start.8
  302.3 136.5 %collective-permute-start.26 = (bf16[640,1152]{1,0:T(8,128)(2,1)}, bf16[640,1152]{1,0:T(8,128)(2,1)S(1)}, u32[]{:S(2)}, u32[]{:S(2)}) collective-permute-start(bf16[640,1152]{1,0:T(8,128)(2,1)} %collective-permute-done.25), channel_id=1, source_target_pairs={{0,8},{1,9},{2,10},{3,11},{4,12},{5,13},{6,14},{7,15},{8,16},{9,17... | collective-permute-start | bytes 4423688 | tf_op jit(solution)/shard_map/ppermute | solution.py:41
  433.2 47.8 %collective-permute-start.22 = (bf16[640,1536]{1,0:T(8,128)(2,1)}, bf16[640,1536]{1,0:T(8,128)(2,1)}, u32[]{:S(2)}, u32[]{:S(2)}) collective-permute-start(bf16[640,1536]{1,0:T(8,128)(2,1)} %collective-permute-done.21), channel_id=1, source_target_pairs={{0,8},{1,9},{2,10},{3,11},{4,12},{5,13},{6,14},{7,15},{8,16},{9,17... | collective-permute-start | bytes 5898248 | tf_op jit(solution)/shard_map/ppermute | solution.py:41
  438.8 73.7 %collective-permute-start.27 = (bf16[640,1152]{1,0:T(8,128)(2,1)S(1)}, bf16[640,1152]{1,0:T(8,128)(2,1)S(1)}, u32[]{:S(2)}, u32[]{:S(2)}) collective-permute-start(bf16[640,1152]{1,0:T(8,128)(2,1)S(1)} %collective-permute-done.26), channel_id=1, source_target_pairs={{0,8},{1,9},{2,10},{3,11},{4,12},{5,13},{6,14},{7,15},{8,16},{9,17... | collective-permute-start | bytes 4423688 | tf_op jit(solution)/shard_map/ppermute | solution.py:41
  481.0 113.4 %collective-permute-start.23 = (bf16[640,1536]{1,0:T(8,128)(2,1)}, bf16[640,1536]{1,0:T(8,128)(2,1)}, u32[]{:S(2)}, u32[]{:S(2)}) collective-permute-start(bf16[640,1536]{1,0:T(8,128)(2,1)} %collective-permute-done.22), channel_id=1, source_target_pairs={{0,8},{1,9},{2,10},{3,11},{4,12},{5,13},{6,14},{7,15},{8,16},{9,17... | collective-permute-start | bytes 5898248 | tf_op jit(solution)/shard_map/ppermute | solution.py:41
  557.1 35.2 %collective-permute-start.42 = (bf16[640,1152]{0,1:T(8,128)(2,1)S(1)}, bf16[640,1152]{0,1:T(8,128)(2,1)S(1)}, u32[]{:S(2)}, u32[]{:S(2)}) collective-permute-start(bf16[640,1152]{0,1:T(8,128)(2,1)S(1)} %fusion.12), channel_id=1, source_target_pairs={{0,8},{1,9},{2,10},{3,11},{4,12},{5,13},{6,14},{7,15},{8,16},{9,17... | collective-permute-start | bytes 4423688 | tf_op jit(solution)/shard_map/ppermute | solution.py:41
  593.9 353.6 %collective-permute-start.43 = (bf16[640,1152]{0,1:T(8,128)(2,1)}, bf16[640,1152]{0,1:T(8,128)(2,1)}, u32[]{:S(2)}, u32[]{:S(2)}) collective-permute-start(bf16[640,1152]{0,1:T(8,128)(2,1)} %add_convert_fusion.6), channel_id=1, source_target_pairs={{0,8},{1,9},{2,10},{3,11},{4,12},{5,13},{6,14},{7,15},{8,16},{9,17... | collective-permute-start | bytes 4423688 | tf_op jit(solution)/shard_map/ppermute | solution.py:41
  780.7 190.1 %collective-permute-start.38 = (bf16[640,1536]{0,1:T(8,128)(2,1)}, bf16[640,1536]{0,1:T(8,128)(2,1)}, u32[]{:S(2)}, u32[]{:S(2)}) collective-permute-start(bf16[640,1536]{0,1:T(8,128)(2,1)} %fusion.7), channel_id=1, source_target_pairs={{0,8},{1,9},{2,10},{3,11},{4,12},{5,13},{6,14},{7,15},{8,16},{9,17... | collective-permute-start | bytes 5898248 | tf_op jit(solution)/shard_map/ppermute | solution.py:41
  807.9 26.1 %collective-permute-start.33 = (bf16[512,256]{1,0:T(8,128)(2,1)S(1)}, bf16[512,256]{1,0:T(8,128)(2,1)S(1)}, u32[]{:S(2)}, u32[]{:S(2)}) collective-permute-start(bf16[512,256]{1,0:T(8,128)(2,1)S(1)} %pad_maximum_fusion.22), channel_id=1, source_target_pairs={{8,0},{9,1},{10,2},{11,3},{12,4},{13,5},{14,6},{15,7},{16,8},{17,9... | collective-permute-start | bytes 786440 | tf_op jit(solution)/shard_map/ppermute | solution.py:47
  811.0 42.6 %collective-permute-start.48 = (bf16[640,320]{0,1:T(8,128)(2,1)}, bf16[640,320]{0,1:T(8,128)(2,1)}, u32[]{:S(2)}, u32[]{:S(2)}) collective-permute-start(bf16[640,320]{0,1:T(8,128)(2,1)} %slice.353), channel_id=1, source_target_pairs={{0,8},{1,9},{2,10},{3,11},{4,12},{5,13},{6,14},{7,15},{8,16},{9,17... | collective-permute-start | bytes 1228808 | tf_op jit(solution)/shard_map/ppermute | solution.py:41
  832.5 211.6 %collective-permute-start.28 = (bf16[4,256,2560]{2,1,0:T(8,128)(2,1)}, bf16[4,256,2560]{2,1,0:T(8,128)(2,1)}, u32[]{:S(2)}, u32[]{:S(2)}) collective-permute-start(bf16[4,256,2560]{2,1,0:T(8,128)(2,1)} %slice_bitcast_fusion), channel_id=1, source_target_pairs={{0,1},{1,0},{2,3},{3,2},{4,5},{5,4},{6,7},{7,6},{8,9},{9,8},{10,11... | collective-permute-start | bytes 15728648 | tf_op jit(solution)/shard_map/ppermute | solution.py:38
  853.0 66.1 %collective-permute-start.34 = (bf16[640,480]{0,1:T(8,128)(2,1)S(1)}, bf16[640,480]{0,1:T(8,128)(2,1)S(1)}, u32[]{:S(2)}, u32[]{:S(2)}) collective-permute-start(bf16[640,480]{0,1:T(8,128)(2,1)S(1)} %slice.331), channel_id=1, source_target_pairs={{0,8},{1,9},{2,10},{3,11},{4,12},{5,13},{6,14},{7,15},{8,16},{9,17... | collective-permute-start | bytes 1843208 | tf_op jit(solution)/shard_map/ppermute | solution.py:41
  854.8 63.5 %collective-permute-start.49 = (bf16[640,320]{0,1:T(8,128)(2,1)S(1)}, bf16[640,320]{0,1:T(8,128)(2,1)S(1)}, u32[]{:S(2)}, u32[]{:S(2)}) collective-permute-start(bf16[640,320]{0,1:T(8,128)(2,1)S(1)} %add_convert_fusion.14), channel_id=1, source_target_pairs={{0,8},{1,9},{2,10},{3,11},{4,12},{5,13},{6,14},{7,15},{8,16},{9,17... | collective-permute-start | bytes 1228808 | tf_op jit(solution)/shard_map/ppermute | solution.py:41
  918.7 14.2 %collective-permute-start.50 = (bf16[640,320]{0,1:T(8,128)(2,1)S(1)}, bf16[640,320]{0,1:T(8,128)(2,1)S(1)}, u32[]{:S(2)}, u32[]{:S(2)}) collective-permute-start(bf16[640,320]{0,1:T(8,128)(2,1)S(1)} %add_convert_fusion.13), channel_id=1, source_target_pairs={{0,8},{1,9},{2,10},{3,11},{4,12},{5,13},{6,14},{7,15},{8,16},{9,17... | collective-permute-start | bytes 1228808 | tf_op jit(solution)/shard_map/ppermute | solution.py:41
  920.3 25.0 %collective-permute-start.35 = (bf16[640,480]{0,1:T(8,128)(2,1)S(1)}, bf16[640,480]{0,1:T(8,128)(2,1)}, u32[]{:S(2)}, u32[]{:S(2)}) collective-permute-start(bf16[640,480]{0,1:T(8,128)(2,1)S(1)} %add_convert_fusion.11), channel_id=1, source_target_pairs={{0,8},{1,9},{2,10},{3,11},{4,12},{5,13},{6,14},{7,15},{8,16},{9,17... | collective-permute-start | bytes 1843208 | tf_op jit(solution)/shard_map/ppermute | solution.py:41
  933.2 18.0 %collective-permute-start.51 = (bf16[320,320]{1,0:T(8,128)(2,1)S(1)}, bf16[320,320]{1,0:T(8,128)(2,1)S(1)}, u32[]{:S(2)}, u32[]{:S(2)}) collective-permute-start(bf16[320,320]{1,0:T(8,128)(2,1)S(1)} %dynamic-slice_bitcast_fusion.6), channel_id=1, source_target_pairs={{0,4},{1,5},{2,6},{3,7},{4,0},{5,1},{6,2},{7,3},{8,12},{9,13},{10,... | collective-permute-start | bytes 614408 | tf_op jit(solution)/shard_map/ppermute | solution.py:38
  947.5 18.8 %collective-permute-start.36 = (bf16[640,480]{0,1:T(8,128)(2,1)}, bf16[640,480]{0,1:T(8,128)(2,1)S(1)}, u32[]{:S(2)}, u32[]{:S(2)}) collective-permute-start(bf16[640,480]{0,1:T(8,128)(2,1)} %add_convert_fusion.10), channel_id=1, source_target_pairs={{0,8},{1,9},{2,10},{3,11},{4,12},{5,13},{6,14},{7,15},{8,16},{9,17... | collective-permute-start | bytes 1843208 | tf_op jit(solution)/shard_map/ppermute | solution.py:41
  950.6 47.4 %collective-permute-start.44 = (bf16[640,1152]{0,1:T(8,128)(2,1)}, bf16[640,1152]{0,1:T(8,128)(2,1)}, u32[]{:S(2)}, u32[]{:S(2)}) collective-permute-start(bf16[640,1152]{0,1:T(8,128)(2,1)} %add_convert_fusion.5), channel_id=1, source_target_pairs={{0,8},{1,9},{2,10},{3,11},{4,12},{5,13},{6,14},{7,15},{8,16},{9,17... | collective-permute-start | bytes 4423688 | tf_op jit(solution)/shard_map/ppermute | solution.py:41
  974.5 63.9 %collective-permute-start.39 = (bf16[640,1536]{0,1:T(8,128)(2,1)}, bf16[640,1536]{0,1:T(8,128)(2,1)}, u32[]{:S(2)}, u32[]{:S(2)}) collective-permute-start(bf16[640,1536]{0,1:T(8,128)(2,1)} %add_convert_fusion.3), channel_id=1, source_target_pairs={{0,8},{1,9},{2,10},{3,11},{4,12},{5,13},{6,14},{7,15},{8,16},{9,17... | collective-permute-start | bytes 5898248 | tf_op jit(solution)/shard_map/ppermute | solution.py:41
  1005.9 36.1 %collective-permute-start.45 = (bf16[320,1152]{1,0:T(8,128)(2,1)S(1)}, bf16[320,1152]{1,0:T(8,128)(2,1)S(1)}, u32[]{:S(2)}, u32[]{:S(2)}) collective-permute-start(bf16[320,1152]{1,0:T(8,128)(2,1)S(1)} %dynamic-slice_bitcast_fusion.2), channel_id=1, source_target_pairs={{0,4},{1,5},{2,6},{3,7},{4,0},{5,1},{6,2},{7,3},{8,12},{9,13},{10,... | collective-permute-start | bytes 2211848 | tf_op jit(solution)/shard_map/ppermute | solution.py:38
  1042.1 45.2 %collective-permute-start.40 = (bf16[640,1536]{0,1:T(8,128)(2,1)}, bf16[640,1536]{0,1:T(8,128)(2,1)}, u32[]{:S(2)}, u32[]{:S(2)}) collective-permute-start(bf16[640,1536]{0,1:T(8,128)(2,1)} %add_convert_fusion.2), channel_id=1, source_target_pairs={{0,8},{1,9},{2,10},{3,11},{4,12},{5,13},{6,14},{7,15},{8,16},{9,17... | collective-permute-start | bytes 5898248 | tf_op jit(solution)/shard_map/ppermute | solution.py:41
  1093.4 24.8 %collective-permute-start.41 = (bf16[320,1536]{1,0:T(8,128)(2,1)S(1)}, bf16[320,1536]{1,0:T(8,128)(2,1)S(1)}, u32[]{:S(2)}, u32[]{:S(2)}) collective-permute-start(bf16[320,1536]{1,0:T(8,128)(2,1)S(1)} %dynamic-slice_bitcast_fusion), channel_id=1, source_target_pairs={{0,4},{1,5},{2,6},{3,7},{4,0},{5,1},{6,2},{7,3},{8,12},{9,13},{10,... | collective-permute-start | bytes 2949128 | tf_op jit(solution)/shard_map/ppermute | solution.py:38
  1096.0 28.6 %collective-permute-start.29 = (bf16[2,128,2560]{2,1,0:T(8,128)(2,1)S(1)}, bf16[2,128,2560]{2,1,0:T(8,128)(2,1)S(1)}, u32[]{:S(2)}, u32[]{:S(2)}) collective-permute-start(bf16[2,128,2560]{2,1,0:T(8,128)(2,1)S(1)} %pad_maximum_fusion.14), channel_id=1, source_target_pairs={{0,2},{1,3},{2,0},{3,1},{4,6},{5,7},{6,4},{7,5},{8,10},{9,11},{10,... | collective-permute-start | bytes 3932168 | tf_op jit(solution)/shard_map/ppermute | solution.py:38
  1097.0 46.0 %collective-permute-start.31 = (bf16[2,128,2560]{2,1,0:T(8,128)(2,1)S(1)}, bf16[2,128,2560]{2,1,0:T(8,128)(2,1)S(1)}, u32[]{:S(2)}, u32[]{:S(2)}) collective-permute-start(bf16[2,128,2560]{2,1,0:T(8,128)(2,1)S(1)} %copy-done.67), channel_id=1, source_target_pairs={{0,4},{1,5},{2,6},{3,7},{4,0},{5,1},{6,2},{7,3},{8,12},{9,13},{10,... | collective-permute-start | bytes 3932168 | tf_op jit(solution)/shard_map/ppermute | solution.py:38
  1124.4 21.0 %collective-permute-start.46 = (f32[2,320]{1,0:T(2,128)S(1)}, f32[2,320]{1,0:T(2,128)S(1)}, u32[]{:S(2)}, u32[]{:S(2)}) collective-permute-start(f32[2,320]{1,0:T(2,128)S(1)} %pad_maximum_fusion.23), channel_id=1, source_target_pairs={{0,1},{1,0},{2,3},{3,2},{4,5},{5,4},{6,7},{7,6},{8,9},{9,8},{10,11... | collective-permute-start | bytes 7688 | tf_op jit(solution)/shard_map/ppermute | solution.py:38
  1143.4 14.8 %collective-permute-start.30 = (bf16[128,2560]{1,0:T(8,128)(2,1)S(1)}, bf16[128,2560]{1,0:T(8,128)(2,1)S(1)}, u32[]{:S(2)}, u32[]{:S(2)}) collective-permute-start(bf16[128,2560]{1,0:T(8,128)(2,1)S(1)} %get-tuple-element.63), channel_id=1, source_target_pairs={{0,4},{1,5},{2,6},{3,7},{4,0},{5,1},{6,2},{7,3},{8,12},{9,13},{10,... | collective-permute-start | bytes 1966088 | tf_op jit(solution)/shard_map/ppermute | solution.py:38
  1144.5 13.7 %collective-permute-start.32 = (bf16[128,2560]{1,0:T(8,128)(2,1)S(1)}, bf16[128,2560]{1,0:T(8,128)(2,1)S(1)}, u32[]{:S(2)}, u32[]{:S(2)}) collective-permute-start(bf16[128,2560]{1,0:T(8,128)(2,1)S(1)} %get-tuple-element.64), channel_id=1, source_target_pairs={{0,2},{1,3},{2,0},{3,1},{4,6},{5,7},{6,4},{7,5},{8,10},{9,11},{10,... | collective-permute-start | bytes 1966088 | tf_op jit(solution)/shard_map/ppermute | solution.py:38
  1145.5 11.5 collective-permute-start.47
  (100 other events, 1180.3 us)

commit v2 on v1

v2 whole, which is shorter than its diff:
```python
import functools

import jax
import jax.numpy as jnp
from jax import lax
from jax.experimental import pallas as pl
from jax.experimental.pallas import tpu as pltpu
from jax.sharding import PartitionSpec as P

HEAD_SIZE = 80
WINDOW_LENGTH = 512
EPS = 1e-05
THETA = 1000000.0
FLOOR = -1e30
AXES = ("tok", "mp")
FF_CHUNKS = (128, 384, 256, 128)


class Grid:
    def __init__(self):
        self.nz = lax.axis_size("tok") // 2
        tok = lax.axis_index("tok")
        mp = lax.axis_index("mp")
        self.z, self.y = tok // 2, tok % 2
        self.x, self.c = mp // 2, mp % 2
        self.me = self.y * 4 + self.x * 2 + self.c

    def pairs(self, move):
        out = []
        for z in range(self.nz):
            for g in range(8):
                target = move(z, g)
                if target is not None:
                    out.append((z * 8 + g, target[0] * 8 + target[1]))
        return out

    def swap(self, value, bit):
        return lax.ppermute(value, AXES, self.pairs(lambda z, g: (z, g ^ bit)))

    def ring(self, value):
        return lax.ppermute(value, AXES, self.pairs(lambda z, g: ((z + 1) % self.nz, g)))

    def step(self, value, d):
        def move(z, g):
            return (z + d, g) if 0 <= z + d < self.nz else None

        return lax.ppermute(value, AXES, self.pairs(move))


Y, X, C = 4, 2, 1


def rotated(grid, value, back=False):
    width = value.shape[-1] // grid.nz
    parts = []
    for s in range(grid.nz):
        block = lax.rem(grid.z - s + grid.nz, grid.nz)
        parts.append(lax.dynamic_slice_in_dim(value, block * width, width, value.ndim - 1))
    return jnp.concatenate(parts, -1)


LANES = 128
SCALE = HEAD_SIZE ** (-0.5)
LOG2E = 1.4426950408889634
MIB = 1024 * 1024
BF16 = jnp.bfloat16
F32 = jnp.float32
HBM = pl.BlockSpec(memory_space=pl.ANY)
WHOLE = pl.BlockSpec(memory_space=pltpu.VMEM)
MESH = pl.DeviceIdType.MESH


def light(**kwargs):
    return dict(
        cost_estimate=pl.CostEstimate(flops=1000000, bytes_accessed=100000, transcendentals=0),
        **kwargs,
    )


def params(mib, **kwargs):
    return pltpu.CompilerParams(vmem_limit_bytes=mib * MIB, **kwargs)


def rope_tables(count, first, width):
    half = width // 2
    places = (first + jnp.arange(count, dtype=jnp.int32)).astype(F32)
    freqs = THETA ** (-(jnp.arange(half, dtype=jnp.int32).astype(F32) * 2.0 / width))
    angles = places[:, None] * freqs[None, :]
    cosine, sine = jnp.cos(angles), jnp.sin(angles)
    blank = jnp.zeros((count, LANES // 2 - half), F32)
    return (
        jnp.concatenate([cosine, blank, cosine, blank], 1),
        jnp.concatenate([-sine, blank, sine, blank], 1),
    )


def spread_matrix(turned, plain):
    half = HEAD_SIZE // 2
    f = jnp.arange((turned + plain) * HEAD_SIZE, dtype=jnp.int32)
    head, place = f // HEAD_SIZE, f % HEAD_SIZE
    gap = jnp.where((head < turned) & (place >= half), LANES // 2 - half, 0)
    target = head * LANES + place + gap
    lanes = jnp.arange((turned + plain) * LANES, dtype=jnp.int32)
    return (target[:, None] == lanes[None, :]).astype(BF16)


def nt(left, right):
    return lax.dot_general(left, right, (((1,), (1,)), ((), ())), preferred_element_type=F32)


def nn(left, right):
    return lax.dot_general(left, right, (((1,), (0,)), ((), ())), preferred_element_type=F32)


def tn(left, right):
    return lax.dot_general(left, right, (((0,), (0,)), ((), ())), preferred_element_type=F32)


def mask_bias(kid, qid, keys, rows):
    kk = lax.broadcasted_iota(jnp.int32, (keys, rows), 0)
    qq = lax.broadcasted_iota(jnp.int32, (keys, rows), 1)
    d = qq + WINDOW_LENGTH - kk
    allowed = (d >= 0) & (d < WINDOW_LENGTH) & (kid == qid)
    return jnp.where(allowed, 0.0, FLOOR)


def only(condition, act):
    if condition is None:
        act()
    else:
        pl.when(condition)(act)


class Copy:
    def __init__(self, copy, when, got):
        self.copy, self.when, self.got = copy, when, got

    def wait_recv(self):
        only(self.got, self.copy.wait_recv)

    def wait_send(self):
        only(self.when, self.copy.wait_send)


SEMAPHORES = 96


def semaphores():
    return [
        pltpu.SemaphoreType.DMA((SEMAPHORES,)),
        pltpu.SemaphoreType.DMA((SEMAPHORES,)),
        pltpu.SemaphoreType.DMA((SEMAPHORES,)),
    ]


class Wires:
    def __init__(self, send, recv, local):
        self.send, self.recv, self.here = send, recv, local
        self.count = self.local_count = 0
        self.copies = []
        tokens = lax.axis_size("tok")
        tok, mp = lax.axis_index("tok"), lax.axis_index("mp")
        self.nz = tokens // 2
        self.at_z, self.at_y = tok // 2, tok % 2
        self.at_x, self.at_c = mp // 2, mp % 2
        self.x = (tok, lax.rem(mp + 2, 4))
        self.y = (tok + 1 - 2 * self.at_y, mp)
        self.c = (tok, mp + 1 - 2 * self.at_c)
        self.up = (lax.rem(tok + 2, tokens), mp)
        self.down = (lax.rem(tok + tokens - 2, tokens), mp)

    def greet(self):
        barrier = pltpu.get_barrier_semaphore()
        peers = (self.x, self.y, self.c, self.up, self.down)
        for peer in peers:
            pl.semaphore_signal(barrier, inc=1, device_id=peer, device_id_type=MESH)
        pl.semaphore_wait(barrier, len(peers))

    def start(self, source, target, peer, when=None, got=None):
        i = self.count
        self.count += 1
        copy = pltpu.make_async_remote_copy(
            src_ref=source,
            dst_ref=target,
            send_sem=self.send.at[i],
            recv_sem=self.recv.at[i],
            device_id=peer,
            device_id_type=MESH,
        )
        only(when, copy.start)
        made = Copy(copy, when, got)
        self.copies.append(made)
        return made

    def choose(self, sources, target, peer, got):
        i = self.count
        for when, source in sources:
            self.count = i
            made = self.start(source, target, peer, when, got)
        return made

    def local(self, source, target):
        copy = pltpu.make_async_copy(source, target, self.here.at[self.local_count])
        self.local_count += 1
        copy.start()
        return copy

    def natural(self, b):
        spots = ((self.at_y, 4), (self.at_x, 2), (self.at_c, 1))
        return sum((1 - at if b & bit else at) * bit for at, bit in spots)

    def finish(self):
        for copy in self.copies:
            copy.wait_send()


def drain(*parts):
    parts = list(parts)
    while parts:
        parts = [part for part in parts if next(part, None) is not None]


def run(part):
    next(part, None)


def exchange_halves(wires, sources, slot):
    n = slot.shape[0] // 2
    rows = pl.ds(pl.multiple_of(wires.at_y * n, n), n)
    waits = []
    for pick, lo, hi in sources:
        waits.append(wires.start(pick(1 - wires.at_y), slot.at[rows, lo:hi], wires.y).wait_recv)
        waits.append(wires.local(pick(wires.at_y), slot.at[rows, lo:hi]).wait)
    yield 1
    for wait in waits:
        wait()


def along_z(wires, first, slot):
    nz, z = wires.nz, wires.at_z
    get = lambda s: first if s == 0 else slot(s)
    for s in range(1, nz):
        up = wires.start(get(s - 1), slot(s), wires.up, (z >= s - 1) & (z < nz - 1), z >= s)
        down = wires.start(
            get((nz - s + 1) % nz), slot(nz - s), wires.down, (z + s <= nz) & (z >= 1), z + s < nz
        )
        yield 1
        up.wait_recv()
        down.wait_recv()


def add_into(target, source):
    @pl.loop(0, target.shape[0] // 32)
    def _(t):
        part = pl.ds(pl.multiple_of(t * 32, 32), 32)
        target[part, :] = (target[part, :].astype(F32) + source[part, :].astype(F32)).astype(BF16)


def sum_along_z(wires, p, above, below, stage, mine, got):
    nz, z = wires.nz, wires.at_z
    ups, downs = [], []
    for s in range(1, nz):
        if s > 1:
            loads = [wires.local(p(s), stage.at[0]), wires.local(p(nz - s), stage.at[1])]
            yield 1
            ups[-1].wait_recv()
            downs[-1].wait_recv()
            for load in loads:
                load.wait()
            only((z >= 1) & (z < s), lambda s=s: add_into(above.at[s - 2], stage.at[0]))
            only(
                (z + s >= nz) & (z < nz - 1), lambda s=s: add_into(below.at[s - 2], stage.at[1])
            )
        up = [(z == 0, p(s))]
        down = [(z == nz - 1, p(nz - s))]
        if s > 1:
            up.append(((z >= 1) & (z < s) & (z < nz - 1), above.at[s - 2]))
            down.append(((z + s >= nz) & (z < nz - 1) & (z >= 1), below.at[s - 2]))
        ups.append(wires.choose(up, above.at[s - 1], wires.up, (z >= 1) & (z <= s)))
        downs.append(
            wires.choose(down, below.at[s - 1], wires.down, (z + s >= nz - 1) & (z < nz - 1))
        )
    load = wires.local(p(0), stage.at[0])
    yield 1
    ups[-1].wait_recv()
    downs[-1].wait_recv()
    load.wait()
    only(z >= 1, lambda: add_into(stage.at[0], above.at[nz - 2]))
    only(z < nz - 1, lambda: add_into(stage.at[0], below.at[nz - 2]))
    n = mine.shape[0]
    own = pl.ds(pl.multiple_of(wires.at_y * n, n), n)
    other = pl.ds(pl.multiple_of((1 - wires.at_y) * n, n), n)
    sent = wires.start(stage.at[0, other], got, wires.y)
    kept = wires.local(stage.at[0, own], mine)
    yield 1
    sent.wait_recv()
    kept.wait()


def sum_scratch(nz, rows, cols):
    return [
        pltpu.VMEM((nz - 1, rows, cols), BF16),
        pltpu.VMEM((nz - 1, rows, cols), BF16),
        pltpu.VMEM((2, rows, cols), BF16),
    ]


def sum_outputs(rows, cols):
    return [jax.ShapeDtypeStruct((rows // 2, cols), BF16)] * 2


def columns(ref, rows, lo, hi):
    return lambda s: ref.at[pl.ds(s * rows, rows), lo:hi]


def gather_weight_rows(wires, sources, out):
    n = out.shape[0] // wires.nz
    slot = lambda s: out.at[pl.ds(s * n, n)]
    yield from exchange_halves(wires, sources, slot(0))
    yield from along_z(wires, slot(0), slot)


def gather_phase(wires, block, out, long_x=False):
    n = block.shape[0]
    half = n // 2
    top, bottom = pl.ds(0, half), pl.ds(half, half)
    mine = wires.local(block, out.at[0])
    xb = wires.start(block.at[bottom], out.at[2, bottom], wires.x)
    yt = wires.start(block.at[top], out.at[4, top], wires.y)
    c = [wires.start(block, out.at[1], wires.c)]
    xt = wires.start(block.at[top], out.at[2, top], wires.x)
    yb = wires.start(block.at[bottom], out.at[4, bottom], wires.y)
    yield 1
    yt.wait_recv()
    dt = wires.start(out.at[4, top], out.at[6, top], wires.x)
    c.append(wires.start(out.at[4, top], out.at[5, top], wires.c))
    xb.wait_recv()
    if not long_x:
        db = wires.start(out.at[2, bottom], out.at[6, bottom], wires.y)
    c.append(wires.start(out.at[2, bottom], out.at[3, bottom], wires.c))
    yield 1
    yb.wait_recv()
    if long_x:
        db = wires.start(out.at[4, bottom], out.at[6, bottom], wires.x)
    c.append(wires.start(out.at[4, bottom], out.at[5, bottom], wires.c))
    xt.wait_recv()
    c.append(wires.start(out.at[2, top], out.at[3, top], wires.c))
    yield 1
    dt.wait_recv()
    c.append(wires.start(out.at[6, top], out.at[7, top], wires.c))
    db.wait_recv()
    c.append(wires.start(out.at[6, bottom], out.at[7, bottom], wires.c))
    yield 1
    for copy in c:
        copy.wait_recv()
    mine.wait()


def start_kernel(x_ref, pack_ref, x_all, w_all, send, recv, local):
    wires = Wires(send, recv, local)
    wires.greet()
    weights = gather_weight_rows(
        wires, [(lambda y: pack_ref.at[y], 0, pack_ref.shape[2])], w_all
    )
    run(weights)
    tokens = gather_phase(wires, x_ref, x_all)
    run(tokens)
    drain(weights, tokens)
    wires.finish()


def gather_start(own, pack):
    n, model = own.shape
    return pl.pallas_call(
        start_kernel,
        in_specs=[WHOLE, HBM],
        out_specs=[HBM, HBM],
        out_shape=[
            jax.ShapeDtypeStruct((8, n, model), BF16),
            jax.ShapeDtypeStruct((model, pack.shape[2]), BF16),
        ],
        scratch_shapes=semaphores(),
        compiler_params=params(16, collective_id=0, has_side_effects=True),
        name="gather_start",
        **light(),
    )(own, pack)


def feed_sources(gate, up, down, cut, hidden):
    a, b = cut
    n = b - a
    step = LANES

    def pick(ref):
        return lambda y: ref.at[:, pl.ds(pl.multiple_of(y * hidden + a, step), n)]

    return [(pick(ref), k * n, (k + 1) * n) for k, ref in enumerate((gate, up, down))]


def attention_kernel(
    hidden, cuts,
    x_ref, w_ref, spread_ref, squeeze_ref, cos_ref, sin_ref, kid_ref, qid_ref, dout_ref,
    opack_ref, gate_ref, up_ref, down_ref,
    a1_ref, q_ref, k_ref, v_ref, o_ref, lse_ref, dout_all, w_out, w_zero, w_next,
    x_all, w_flat, w_pad, send, recv, local,
):
    wires = Wires(send, recv, local)
    nz, z = wires.nz, wires.at_z
    rows = x_all.shape[1]
    model = x_all.shape[2]
    heads = q_ref.shape[1] // LANES
    keys = rows + WINDOW_LENGTH
    length = 8 * rows
    wires.greet()
    load_w = wires.local(w_ref, w_flat)
    order = (6, 7, 0, 1, 2, 3, 4, 5)
    loads = {}
    for b in order:
        at = wires.natural(b)
        loads[b] = wires.local(x_ref.at[at], x_all.at[at])
    out_weights = gather_weight_rows(
        wires, [(lambda y: opack_ref.at[y], 0, opack_ref.shape[2])], w_out
    )
    run(out_weights)
    zero_weights = gather_weight_rows(
        wires, feed_sources(gate_ref, up_ref, down_ref, cuts[0], hidden), w_zero
    )
    run(zero_weights)
    next_weights = exchange_halves(
        wires, feed_sources(gate_ref, up_ref, down_ref, cuts[1], hidden), w_next
    )
    run(next_weights)
    cotangents = gather_phase(wires, dout_ref, dout_all, True)
    run(cotangents)
    load_w.wait()

    @pl.loop(0, model // 512)
    def _(t):
        part = pl.ds(pl.multiple_of(t * 512, 512), 512)
        w_pad[part, :] = nn(w_flat[part, :], spread_ref[...]).astype(BF16)

    place = lax.broadcasted_iota(jnp.int32, (8, w_flat.shape[1]), 1)
    which = (place == (heads + 2) * HEAD_SIZE).astype(BF16)
    gain = nt(which, w_flat[...])[0:1, :]

    @pl.when(z == 0)
    def _():
        k_ref[0:WINDOW_LENGTH, :] = jnp.zeros((WINDOW_LENGTH, LANES), BF16)
        v_ref[0:WINDOW_LENGTH, :] = jnp.zeros((WINDOW_LENGTH, LANES), BF16)

    stores = []
    for b in order:
        at = wires.natural(b)
        loads[b].wait()
        x = x_all[at].astype(F32)
        inverse = lax.rsqrt(jnp.mean(x * x, axis=1, keepdims=True) + EPS)
        a1 = (x * inverse * gain).astype(BF16)
        x_all[at] = a1
        stores.append(wires.local(x_all.at[at], a1_ref.at[at]))
        acc = nn(a1, w_pad[...])
        here = slice(b * rows, (b + 1) * rows)
        there = slice(WINDOW_LENGTH + b * rows, WINDOW_LENGTH + (b + 1) * rows)
        cosine, sine = cos_ref[here, :], sin_ref[here, :]
        for h in range(heads + 1):
            u = acc[:, h * LANES : (h + 1) * LANES]
            turned = (u * cosine + pltpu.roll(u, LANES // 2, 1) * sine).astype(BF16)
            if h < heads:
                q_ref[here, h * LANES : (h + 1) * LANES] = turned
            else:
                k_ref[there, :] = turned
        v_ref[there, :] = acc[:, (heads + 1) * LANES :].astype(BF16)
        if b == 7:
            halo = [
                wires.start(
                    ref.at[pl.ds(length, WINDOW_LENGTH)], ref.at[pl.ds(0, WINDOW_LENGTH)],
                    wires.up, z < nz - 1, z > 0,
                )
                for ref in (k_ref, v_ref)
            ]
            run(out_weights)
        if b == 1:
            run(cotangents)
    for copy in halo:
        copy.wait_recv()

    def block(b, at):
        start = pl.multiple_of(b * rows, rows)
        span = pl.ds(start, keys)
        here = pl.ds(start, rows)
        kb = k_ref[span, :]
        vt = v_ref[span, :].T
        bias = mask_bias(kid_ref[span, :], qid_ref[:, here], keys, rows)
        outs = []
        for h in range(heads):
            lanes = slice(h * LANES, (h + 1) * LANES)
            s = nt(kb, q_ref[here, lanes]) * (SCALE * LOG2E) + bias
            peak = jnp.max(s, axis=0, keepdims=True)
            p = jnp.exp2(s - peak)
            total = jnp.sum(p, axis=0, keepdims=True)
            ot = nn(vt, p.astype(BF16)) / total
            outs.append(ot.T.astype(BF16))
            lse_ref[b, h : h + 1, :] = peak + jnp.log2(total)
        o_ref[at] = nn(jnp.concatenate(outs, 1), squeeze_ref[...]).astype(BF16)

    for b in range(8):
        block(b, wires.natural(b))
        if b in (1, 4, 6):
            run(out_weights)
        if b in (3,):
            run(zero_weights)
        if b in (2, 5):
            run(cotangents)
    for store in stores:
        store.wait()
    drain(out_weights, zero_weights, next_weights, cotangents)
    wires.finish()


def attention(x_all, w_attn, cosine, sine, kid, qid, dout, opack, gate, up, down, heads, cuts):
    _, n, model = x_all.shape
    length = 8 * n
    hidden = gate.shape[1] // 2
    wide = heads * LANES
    spread = spread_matrix(heads + 1, 1)
    spread = jnp.concatenate(
        [spread, jnp.zeros((w_attn.shape[1] - spread.shape[0], spread.shape[1]), BF16)], 0
    )
    squeeze = spread_matrix(0, heads).T
    slot = 2 * gate.shape[0]
    first, second = cuts[0][1] - cuts[0][0], cuts[1][1] - cuts[1][0]
    return pl.pallas_call(
        functools.partial(attention_kernel, hidden, cuts),
        in_specs=[HBM, HBM] + [WHOLE] * 7 + [HBM] * 4,
        out_specs=[HBM] + [WHOLE] * 5 + [HBM] * 4,
        out_shape=[
            jax.ShapeDtypeStruct((8, n, model), BF16),
            jax.ShapeDtypeStruct((length, wide), BF16),
            jax.ShapeDtypeStruct((length + WINDOW_LENGTH, LANES), BF16),
            jax.ShapeDtypeStruct((length + WINDOW_LENGTH, LANES), BF16),
            jax.ShapeDtypeStruct((8, n, heads * HEAD_SIZE), BF16),
            jax.ShapeDtypeStruct((8, heads, n), F32),
            jax.ShapeDtypeStruct((8, n, model), BF16),
            jax.ShapeDtypeStruct((model, opack.shape[2]), BF16),
            jax.ShapeDtypeStruct((model, 3 * first), BF16),
            jax.ShapeDtypeStruct((slot, 3 * second), BF16),
        ],
        scratch_shapes=[
            pltpu.VMEM((8, n, model), BF16),
            pltpu.VMEM(w_attn.shape, BF16),
            pltpu.VMEM((model, spread.shape[1]), BF16),
        ]
        + semaphores(),
        compiler_params=params(56, collective_id=5, has_side_effects=True),
        name="attention",
        **light(),
    )(x_all, w_attn, spread, squeeze, cosine, sine, kid, qid, dout, opack, gate, up, down)


def project_kernel(
    a_ref, w_ref, x_ref, gain_ref, slot_ref, res_ref, inv_ref, out_ref, w_all,
    block, cs, cr, q, xr, yr, tr, br, send, recv, local,
):
    wires = Wires(send, recv, local)
    wires.greet()
    n = slot_ref.shape[0]
    own = wires.local(slot_ref, w_all.at[pl.ds(0, n)])
    weights = along_z(wires, slot_ref, lambda s: w_all.at[pl.ds(s * n, n)])
    run(weights)

    def emit(rows, total):
        residual = x_ref[rows, :].astype(F32) + total
        inverse = lax.rsqrt(jnp.mean(residual * residual, axis=1, keepdims=True) + EPS)
        res_ref[rows, :] = residual
        inv_ref[rows, :] = inverse
        block[rows, :] = (residual * inverse * gain_ref[...]).astype(BF16)

    sums = reduce_phase(wires, [(a_ref, w_ref)], cs, cr, q, xr, yr, tr, br, emit)
    run(sums)
    run(sums)
    run(weights)
    drain(sums)
    tokens = gather_phase(wires, block, out_ref)
    run(tokens)
    run(tokens)
    run(weights)
    drain(tokens, weights)
    own.wait()
    wires.finish()


def project_out(o, w_out, inputs, gain, slot):
    n, model = inputs.shape
    return pl.pallas_call(
        project_kernel,
        in_specs=[WHOLE] * 4 + [HBM],
        out_specs=[WHOLE, WHOLE, HBM, HBM],
        out_shape=[
            jax.ShapeDtypeStruct((n, model), F32),
            jax.ShapeDtypeStruct((n, 1), F32),
            jax.ShapeDtypeStruct((8, n, model), BF16),
            jax.ShapeDtypeStruct((model, slot.shape[1]), BF16),
        ],
        scratch_shapes=[pltpu.VMEM((n, model), BF16)] + reduce_scratch(n, model) + semaphores(),
        compiler_params=params(52, collective_id=2, has_side_effects=True),
        name="project_out",
        **light(),
    )(o, w_out, inputs, gain, slot)


def feed_kernel(
    hidden, cuts,
    a_ref, d_ref, w0_ref, w1_ref, gate_ref, up_ref, down_ref,
    m_ref, g_ref, w_ref, grad0, grad1, grad2, mine, got,
    a, d, w, m, g, stage, above, below, extra, send, recv, local,
):
    wires = Wires(send, recv, local)
    nz = wires.nz
    length, model = a.shape
    slot = model // nz
    wires.greet()
    small, large = cuts[0][1] - cuts[0][0], cuts[1][1] - cuts[1][0]
    loads = []
    for ref, (lo, hi) in ((w0_ref, cuts[0]), (w1_ref, cuts[1])):
        for k in range(3):
            loads.append(
                wires.local(
                    ref.at[:, k * (hi - lo) : (k + 1) * (hi - lo)],
                    w.at[:, k * hidden + lo : k * hidden + hi],
                )
            )
    blocks = 4
    rows = length // blocks
    a_loads, d_loads = [], []
    for b in range(blocks):
        part = pl.ds(b * rows, rows)
        a_loads.append(wires.local(a_ref.at[part], a.at[part]))
        d_loads.append(wires.local(d_ref.at[part], d.at[part]))

    def carried(cut):
        lo, hi = cut
        sources = feed_sources(gate_ref, up_ref, down_ref, cut, hidden)
        picks = [(pick, k * hidden + lo, k * hidden + hi) for k, (pick, _, _) in enumerate(sources)]
        head = exchange_halves(wires, picks, w.at[pl.ds(0, slot)])
        yield from head
        hops = [
            along_z(
                wires,
                w.at[pl.ds(0, slot), k * hidden + lo : k * hidden + hi],
                lambda s, k=k: w.at[pl.ds(s * slot, slot), k * hidden + lo : k * hidden + hi],
            )
            for k in range(3)
        ]
        while hops:
            hops = [hop for hop in hops if next(hop, None) is not None]
            yield 1

    later = [carried(cut) for cut in cuts[2:]]
    for part in later:
        run(part)
    for copy in loads:
        copy.wait()

    def units(lo, hi, waits):
        for b in range(blocks):
            if waits:
                a_loads[b].wait()
                d_loads[b].wait()
            part = pl.ds(b * rows, rows)
            gate = nn(a[part, :], w[:, lo:hi])
            up = nn(a[part, :], w[:, hidden + lo : hidden + hi])
            dmixed = nn(d[part, :], w[:, 2 * hidden + lo : 2 * hidden + hi])
            sigma = jax.nn.sigmoid(gate)
            silu = gate * sigma
            m[part, lo:hi] = (silu * up).astype(BF16)
            g[part, hidden + lo : hidden + hi] = (dmixed * silu).astype(BF16)
            g[part, lo:hi] = (dmixed * up * sigma * (1.0 + gate * (1.0 - sigma))).astype(BF16)
            yield 1

    def weight_grads(lo, hi, out):
        n = hi - lo
        tile = 640
        pending = [None, None]
        for t in range(model // tile):
            cols = slice(t * tile, (t + 1) * tile)
            if pending[t % 2] is not None:
                pending[t % 2].wait()
            here = stage.at[t % 2]
            for k in range(3):
                left = d if k == 2 else a
                right = m[:, lo:hi] if k == 2 else g[:, k * hidden + lo : k * hidden + hi]
                here[:, k * n : (k + 1) * n] = tn(left[:, cols], right).astype(BF16)
            pending[t % 2] = wires.local(
                here.at[:, 0 : 3 * n], out.at[pl.ds(t * tile, tile)]
            )
            yield 1
        for copy in pending:
            copy.wait()

    first = (cuts[0][0], cuts[1][1])
    for i, _ in enumerate(units(*first, True)):
        if i == 0:
            run(later[0])
    run(later[0])
    for _ in weight_grads(*first, grad0):
        pass
    sums = sum_along_z(
        wires, columns(grad0, slot, 0, mine.shape[1]), above, below, extra, mine, got
    )
    run(sums)
    run(later[0])
    run(later[1])
    drain(later[0])
    for _ in units(*cuts[2], False):
        pass
    run(sums)
    run(later[1])
    for i, _ in enumerate(weight_grads(*cuts[2], grad1)):
        if i == 1:
            run(later[1])
    run(sums)
    drain(later[1])
    for _ in units(*cuts[3], False):
        pass
    outs = [wires.local(w, w_ref), wires.local(m, m_ref), wires.local(g, g_ref)]
    for _ in weight_grads(*cuts[3], grad2):
        pass
    drain(sums)
    for copy in outs:
        copy.wait()
    wires.finish()


def feed_forward(a2, dout, w0, w1, gate, up, down, cuts):
    length, model = a2.shape
    hidden = gate.shape[1] // 2
    first = cuts[1][1]
    sizes = [first] + [b - a for a, b in cuts[2:]]
    rows = 2 * gate.shape[0]
    nz = model // rows
    share = 3 * first // 2
    return pl.pallas_call(
        functools.partial(feed_kernel, hidden, cuts),
        in_specs=[HBM] * 7,
        out_specs=[HBM] * 8,
        out_shape=[
            jax.ShapeDtypeStruct((length, hidden), BF16),
            jax.ShapeDtypeStruct((length, 2 * hidden), BF16),
            jax.ShapeDtypeStruct((model, 3 * hidden), BF16),
        ]
        + [jax.ShapeDtypeStruct((model, 3 * n), BF16) for n in sizes]
        + sum_outputs(rows, share),
        scratch_shapes=[
            pltpu.VMEM((length, model), BF16),
            pltpu.VMEM((length, model), BF16),
            pltpu.VMEM((model, 3 * hidden), BF16),
            pltpu.VMEM((length, hidden), BF16),
            pltpu.VMEM((length, 2 * hidden), BF16),
            pltpu.VMEM((2, 640, 3 * first), BF16),
        ]
        + sum_scratch(nz, rows, share)
        + semaphores(),
        compiler_params=params(60, collective_id=1, has_side_effects=True),
        name="feed_forward",
        **light(),
    )(a2, dout, w0, w1, gate, up, down)


def reduce_phase(wires, pairs, cs, cr, q, xr, yr, tr, br, emit):
    n = q.shape[1]
    half = n // 2
    top, bottom = pl.ds(0, half), pl.ds(half, half)
    model = q.shape[2]
    tile = 512

    def product(place, target):
        @pl.loop(0, model // tile)
        def _(t):
            cols = pl.ds(pl.multiple_of(t * tile, tile), tile)
            total = None
            for a, w in pairs:
                part = nt(a[place], w[cols, :])
                total = part if total is None else total + part
            target[:, cols] = total.astype(BF16)

    waits = {}
    for j in (3, 1, 2, 0):
        product(2 * j + 1, cs.at[j])
        got = wires.start(cs.at[j], cr.at[j], wires.c)
        product(2 * j, q.at[j])
        got.wait_recv()
        q[j] = (q[j].astype(F32) + cr[j].astype(F32)).astype(BF16)
        if j == 3:
            waits["x1"] = wires.start(q.at[3, top], xr.at[1], wires.x)
            waits["y1"] = wires.start(q.at[3, bottom], yr.at[1], wires.y)
        if j == 1:
            waits["x0"] = wires.start(q.at[1, top], xr.at[0], wires.x)
        if j == 2:
            waits["y0"] = wires.start(q.at[2, bottom], yr.at[0], wires.y)
    yield 1
    waits["x1"].wait_recv()
    q[2, top] = (q[2, top].astype(F32) + xr[1].astype(F32)).astype(BF16)
    waits["t"] = wires.start(q.at[2, top], tr, wires.y)
    waits["y1"].wait_recv()
    q[1, bottom] = (q[1, bottom].astype(F32) + yr[1].astype(F32)).astype(BF16)
    waits["b"] = wires.start(q.at[1, bottom], br, wires.x)
    waits["x0"].wait_recv()
    yield 1
    waits["t"].wait_recv()
    emit(top, q[0, top].astype(F32) + xr[0].astype(F32) + tr[...].astype(F32))
    waits["y0"].wait_recv()
    waits["b"].wait_recv()
    emit(bottom, q[0, bottom].astype(F32) + yr[0].astype(F32) + br[...].astype(F32))


def reduce_scratch(n, model):
    half = n // 2
    return [
        pltpu.VMEM((4, n, model), BF16),
        pltpu.VMEM((4, n, model), BF16),
        pltpu.VMEM((4, n, model), BF16),
        pltpu.VMEM((2, half, model), BF16),
        pltpu.VMEM((2, half, model), BF16),
        pltpu.VMEM((half, model), BF16),
        pltpu.VMEM((half, model), BF16),
    ]


def middle_kernel(
    a_ref, w_ref, dout_ref, res_ref, inv_ref, gain_ref, grad0, grad2,
    dres_ref, out_ref, mine0, got0, mine2, got2,
    block, cs, cr, q, xr, yr, tr, br,
    above0, below0, stage0, above2, below2, stage2, send, recv, local,
):
    wires = Wires(send, recv, local)
    wires.greet()
    rows = mine0.shape[0] * 2
    wide = grad0.shape[1]
    first = sum_along_z(
        wires, columns(grad0, rows, wide - mine0.shape[1], wide), above0, below0, stage0, mine0, got0
    )
    second = sum_along_z(
        wires, columns(grad2, rows, 0, mine2.shape[1]), above2, below2, stage2, mine2, got2
    )
    run(first)

    def emit(rows, total):
        inverse = inv_ref[rows, :]
        normed = res_ref[rows, :] * inverse
        e = total * gain_ref[...]
        back = inverse * (e - normed * jnp.mean(e * normed, axis=1, keepdims=True))
        dres = dout_ref[rows, :].astype(F32) + back
        dres_ref[rows, :] = dres
        block[rows, :] = dres.astype(BF16)

    sums = reduce_phase(wires, [(a_ref, w_ref)], cs, cr, q, xr, yr, tr, br, emit)
    run(sums)
    run(first)
    run(sums)
    run(first)
    run(second)
    drain(sums)
    tokens = gather_phase(wires, block, out_ref)
    run(tokens)
    run(tokens)
    run(first)
    run(second)
    run(tokens)
    run(second)
    run(tokens)
    run(second)
    drain(tokens, first, second)
    wires.finish()


def feed_back(dgu, w, dout, residual, inverse, gain, grad0, grad2):
    n, model = dout.shape
    k = dgu.shape[1]
    rows = 2 * model // lax.axis_size("tok")
    nz = model // rows
    flat = pl.BlockSpec((n, model), lambda i: (0, 0))
    thin = pl.BlockSpec((n, 1), lambda i: (0, 0))
    half, small = grad0.shape[1] // 2, grad2.shape[1]
    return pl.pallas_call(
        middle_kernel,
        grid=(1,),
        in_specs=[
            pl.BlockSpec((8, n, k), lambda i: (0, 0, 0)),
            pl.BlockSpec((model, k), lambda i: (0, 0)),
            flat, flat, thin, pl.BlockSpec((1, model), lambda i: (0, 0)), HBM, HBM,
        ],
        out_specs=[flat] + [HBM] * 5,
        out_shape=[
            jax.ShapeDtypeStruct((n, model), F32),
            jax.ShapeDtypeStruct((8, n, model), BF16),
        ]
        + sum_outputs(rows, half)
        + sum_outputs(rows, small),
        scratch_shapes=[pltpu.VMEM((n, model), BF16)]
        + reduce_scratch(n, model)
        + sum_scratch(nz, rows, half)
        + sum_scratch(nz, rows, small)
        + semaphores(),
        compiler_params=params(62, collective_id=3, has_side_effects=True),
        name="feed_back",
        **light(),
    )(dgu.reshape(8, n, k), w, dout, residual, inverse, gain, grad0, grad2)


def back_kernel(
    da_ref, w_ref, o_ref, q_ref, k_ref, v_ref, lse_ref, kid_ref, qid_ref, cos_ref, sin_ref,
    spread_ref, squeeze_ref, final_ref, m_ref, down_ref, res_ref, grad1,
    dqkv_ref, grad_out, out_ref, mine, got,
    da, do, dk, dv, halo, fetched, m, w_down, cr, xr, yr, tr, br, gstage,
    above, below, stage, send, recv, local,
):
    wires = Wires(send, recv, local)
    nz, z = wires.nz, wires.at_z
    wires.greet()
    n, model = da.shape[1], da.shape[2]
    heads = q_ref.shape[1] // LANES
    wide = heads * HEAD_SIZE
    keys = n + WINDOW_LENGTH
    length = 8 * n
    loads = [wires.local(da_ref.at[b], da.at[b]) for b in range(8)]
    late = [
        wires.local(m_ref, m),
        wires.local(down_ref.at[:, 2 * m.shape[2] :], w_down),
    ]
    rows = 2 * mine.shape[0]
    carried = sum_along_z(
        wires, columns(grad1, rows, 0, mine.shape[1]), above, below, stage, mine, got
    )
    run(carried)
    dk[...] = jnp.zeros_like(dk)
    dv[...] = jnp.zeros_like(dv)
    for b in range(8):
        loads[b].wait()
        flat = nn(da[b], w_ref[...]).astype(BF16)
        do[b] = nn(flat, spread_ref[...]).astype(BF16)

    tile = 640
    for t in range(model // tile):
        cols = slice(t * tile, (t + 1) * tile)
        total = None
        for b in range(8):
            part = tn(da[b, :, cols], o_ref[b])
            total = part if total is None else total + part
        gstage[cols, :] = total.astype(BF16)
    save = wires.local(gstage, grad_out)
    for load in late:
        load.wait()

    def emit(part, total):
        out_ref[part, :] = (res_ref[part, :] + total).astype(BF16)

    sums = reduce_phase(
        wires, [(m, w_down)], da.at[pl.ds(0, 4)], cr, da.at[pl.ds(4, 4)], xr, yr, tr, br, emit
    )
    run(sums)
    run(carried)

    def block(b, at):
        start = pl.multiple_of(b * n, n)
        span = pl.ds(start, keys)
        here = pl.ds(start, n)
        kb = k_ref[span, :]
        vb = v_ref[span, :]
        kt = kb.T
        bias = mask_bias(kid_ref[span, :], qid_ref[:, here], keys, n)
        cosine, sine = cos_ref[here, :], sin_ref[here, :]
        dqs = []
        dk_sum = dv_sum = None
        for h in range(heads):
            lanes = slice(h * LANES, (h + 1) * LANES)
            qh = q_ref[here, lanes]
            doh = do[at, :, lanes]
            p = jnp.exp2(nt(kb, qh) * (SCALE * LOG2E) + (bias - lse_ref[b, h : h + 1, :]))
            t = p * nt(vb, doh)
            inner = jnp.sum(t, axis=0, keepdims=True)
            ds = (t - p * inner).astype(BF16)
            dq = nn(kt, ds).T * SCALE
            dqs.append((dq * cosine - pltpu.roll(dq, LANES // 2, 1) * sine).astype(BF16))
            dk_h = nn(ds, qh)
            dv_h = nn(p.astype(BF16), doh)
            dk_sum = dk_h if dk_sum is None else dk_sum + dk_h
            dv_sum = dv_h if dv_sum is None else dv_sum + dv_h
        dqkv_ref[at, :, 0:wide] = nn(jnp.concatenate(dqs, 1), squeeze_ref[...]).astype(BF16)
        dk[span, :] += dk_sum
        dv[span, :] += dv_sum

    for b in range(8):
        block(b, wires.natural(b))
        if b == 1:
            halo[:, 0:LANES] = dk[0:WINDOW_LENGTH, :].astype(BF16)
            halo[:, LANES:] = dv[0:WINDOW_LENGTH, :].astype(BF16)
            borrowed = wires.start(halo, fetched, wires.down, z >= 1, z < nz - 1)
        if b in (2, 5):
            run(sums)
        if b == 4:
            run(carried)
    borrowed.wait_recv()

    @pl.when(z < nz - 1)
    def _():
        dk[length:, :] += fetched[:, 0:LANES].astype(F32)
        dv[length:, :] += fetched[:, LANES:].astype(F32)

    for b in range(8):
        here = slice(b * n, (b + 1) * n)
        there = slice(WINDOW_LENGTH + b * n, WINDOW_LENGTH + (b + 1) * n)
        dkb = dk[there, :] * SCALE
        dkb = dkb * cos_ref[here, :] - pltpu.roll(dkb, LANES // 2, 1) * sin_ref[here, :]
        both = jnp.concatenate([dkb.astype(BF16), dv[there, :].astype(BF16)], 1)
        dqkv_ref[wires.natural(b), :, wide:] = nn(both, final_ref[...]).astype(BF16)
    drain(sums, carried)
    save.wait()
    wires.finish()


def attention_back(
    da_all, w_out, o, q, k_all, v_all, lse, kid, qid, cosine, sine, mixed, w_feed, residual, grad1
):
    _, n, model = da_all.shape
    length = 8 * n
    heads = q.shape[1] // LANES
    wide = heads * HEAD_SIZE
    spread = spread_matrix(0, heads)
    squeeze = spread_matrix(heads, 0).T
    final = spread_matrix(1, 1).T
    rows = 2 * model // lax.axis_size("tok")
    nz = model // rows
    hidden = mixed.shape[1]
    half = n // 2
    return pl.pallas_call(
        back_kernel,
        in_specs=[HBM] + [WHOLE] * 13 + [HBM, HBM, WHOLE, HBM],
        out_specs=[WHOLE, HBM, WHOLE, HBM, HBM],
        out_shape=[
            jax.ShapeDtypeStruct((8, n, wide + 2 * HEAD_SIZE), BF16),
            jax.ShapeDtypeStruct((model, wide), BF16),
            jax.ShapeDtypeStruct((n, model), BF16),
        ]
        + sum_outputs(rows, grad1.shape[1]),
        scratch_shapes=[
            pltpu.VMEM((8, n, model), BF16),
            pltpu.VMEM((8, n, heads * LANES), BF16),
            pltpu.VMEM(k_all.shape, F32),
            pltpu.VMEM(k_all.shape, F32),
            pltpu.VMEM((WINDOW_LENGTH, 2 * LANES), BF16),
            pltpu.VMEM((WINDOW_LENGTH, 2 * LANES), BF16),
            pltpu.VMEM((8, n, hidden), BF16),
            pltpu.VMEM((model, hidden), BF16),
            pltpu.VMEM((4, n, model), BF16),
            pltpu.VMEM((2, half, model), BF16),
            pltpu.VMEM((2, half, model), BF16),
            pltpu.VMEM((half, model), BF16),
            pltpu.VMEM((half, model), BF16),
            pltpu.VMEM((model, wide), BF16),
        ]
        + sum_scratch(nz, rows, grad1.shape[1])
        + semaphores(),
        compiler_params=params(62, collective_id=6, has_side_effects=True),
        name="attention_back",
        **light(),
    )(
        da_all, w_out, o, q, k_all, v_all, lse, kid, qid, cosine, sine, spread, squeeze, final,
        mixed.reshape(8, n, hidden), w_feed, residual, grad1,
    )


def last_kernel(
    a_ref, w_ref, x_ref, inv_ref, gain_ref, dres_ref, a1_ref, grad_out,
    out_ref, mine0, got0, mine1, got1,
    cs, cr, q, xr, yr, tr, br, a1, grad,
    above0, below0, stage0, above1, below1, stage1, send, recv, local,
):
    wires = Wires(send, recv, local)
    wires.greet()
    rows = 2 * mine0.shape[0]
    model = a1.shape[2]
    loads = [wires.local(a1_ref.at[b], a1.at[b]) for b in range(8)]
    first = sum_along_z(
        wires, columns(grad_out, rows, 0, mine0.shape[1]), above0, below0, stage0, mine0, got0
    )
    run(first)

    def emit(rows, total):
        inverse = inv_ref[rows, :]
        normed = x_ref[rows, :].astype(F32) * inverse
        e = total * gain_ref[...]
        back = inverse * (e - normed * jnp.mean(e * normed, axis=1, keepdims=True))
        out_ref[rows, :] = dres_ref[rows, :] + back

    sums = reduce_phase(wires, [(a_ref, w_ref)], cs, cr, q, xr, yr, tr, br, emit)
    run(sums)
    run(first)
    for load in loads:
        load.wait()
    tile = 640
    for t in range(model // tile):
        cols = slice(t * tile, (t + 1) * tile)
        total = None
        for b in range(8):
            part = tn(a1[b, :, cols], a_ref[b])
            total = part if total is None else total + part
        grad[cols, :] = total.astype(BF16)
        if t == 1:
            run(first)
    second = sum_along_z(
        wires, columns(grad, rows, 0, mine1.shape[1]), above1, below1, stage1, mine1, got1
    )
    run(second)
    run(first)
    run(sums)
    run(second)
    drain(sums, second, first)
    wires.finish()


def input_back(dqkv, w, inputs, inverse, gain, dres, a1, grad_out):
    n, model = inputs.shape
    rows = 2 * model // lax.axis_size("tok")
    nz = model // rows
    wide = dqkv.shape[2]
    return pl.pallas_call(
        last_kernel,
        in_specs=[WHOLE] * 6 + [HBM] * 2,
        out_specs=[WHOLE] + [HBM] * 4,
        out_shape=[jax.ShapeDtypeStruct((n, model), F32)]
        + sum_outputs(rows, grad_out.shape[1])
        + sum_outputs(rows, wide),
        scratch_shapes=reduce_scratch(n, model)
        + [pltpu.VMEM((8, n, model), BF16), pltpu.VMEM((model, wide), BF16)]
        + sum_scratch(nz, rows, grad_out.shape[1])
        + sum_scratch(nz, rows, wide)
        + semaphores(),
        compiler_params=params(60, collective_id=4, has_side_effects=True),
        name="input_back",
        **light(),
    )(dqkv, w, inputs, inverse, gain, dres, a1, grad_out)


def body(
    inputs,
    grad_output,
    segments,
    attention_gain,
    query_weight,
    key_matrix,
    value_matrix,
    output_weight,
    feedforward_gain,
    gate_weight,
    up_weight,
    down_weight,
):
    grid = Grid()
    bf16 = jnp.bfloat16
    model = inputs.shape[1]
    length = inputs.shape[0] * 8
    hidden = gate_weight.shape[1] // 2
    qdim = query_weight.shape[1] // 2
    kdim = key_matrix.shape[1] // 2
    cuts = []
    at = 0
    for n in FF_CHUNKS:
        cuts.append((at, at + n))
        at += n
    heads = qdim // HEAD_SIZE

    def packed(*arrays):
        cut = [v.reshape(v.shape[0], 2, -1) for v in arrays]
        return jnp.transpose(jnp.concatenate(cut, 2), (1, 0, 2))

    gains = jnp.stack([attention_gain, feedforward_gain], 1)
    blank = jnp.zeros((gains.shape[0], LANES - (qdim + 2 * kdim + 2) % LANES), bf16)
    tail = jnp.concatenate([gains, blank], 1)
    qkv_pack = packed(
        query_weight, key_matrix, value_matrix, jnp.concatenate([tail, tail], 1)
    )
    out_pack = packed(output_weight.T)
    down_t = down_weight.T

    me = jnp.reshape(grid.me, (1,)).astype(jnp.int32)
    own = rotated(grid, inputs)
    x_all, w_attn = gather_start(own, qkv_pack)
    dout = rotated(grid, grad_output)
    cosine, sine = rope_tables(length, grid.z * length, HEAD_SIZE)
    padded_ids = jnp.concatenate([jnp.full((WINDOW_LENGTH,), -1, jnp.int32), segments])
    key_ids = lax.dynamic_slice_in_dim(padded_ids, grid.z * length, length + WINDOW_LENGTH, 0)
    kid, qid = key_ids[:, None], key_ids[None, WINDOW_LENGTH:]
    gain_rows = w_attn[:, qdim + 2 * kdim : qdim + 2 * kdim + 2].astype(F32).T
    gain_one, gain_two = gain_rows[0:1], gain_rows[1:2]
    a1, q, k_all, v_all, o, lse, dout_all, w_out, w_zero, w_next = attention(
        x_all, w_attn, cosine, sine, kid, qid, dout, out_pack, gate_weight, up_weight, down_t,
        heads, cuts,
    )
    flat = lambda v: v.reshape(length, v.shape[-1])
    residual, inverse_two, a2, w_one = project_out(o, w_out, own, gain_two, w_next)

    mixed, dgu, w_feed, grad0, grad1, grad2, mine_a, got_a = feed_forward(
        flat(a2), flat(dout_all), w_zero, w_one, gate_weight, up_weight, down_t, cuts
    )
    dresidual, da_all, mine_b, got_b, mine_d, got_d = feed_back(
        dgu, w_feed, dout, residual, inverse_two, gain_two, grad0, grad2
    )
    dqkv, grad_o, layer, mine_c, got_c = attention_back(
        da_all, w_out, o, q, k_all, v_all, lse, kid, qid, cosine, sine, mixed, w_feed, residual,
        grad1,
    )
    layer_output = rotated(grid, layer)
    own_wide = own.astype(F32)
    inverse_one = lax.rsqrt(jnp.mean(own_wide * own_wide, axis=-1, keepdims=True) + EPS)
    dinput, mine_o, got_o, mine_q, got_q = input_back(
        dqkv, w_attn[:, : qdim + 2 * kdim], own, inverse_one, gain_one, dresidual, a1, grad_o
    )
    input_gradient = rotated(grid, dinput)

    def paired(mine, got):
        first = jnp.where(grid.y == 0, mine, got)
        second = jnp.where(grid.y == 0, got, mine)
        return jnp.stack([first, second], 1).astype(F32)

    both = lambda left, right: jnp.concatenate([left, right], 1)
    ff_grads = [
        paired(both(mine_a, mine_b), both(got_a, got_b)),
        paired(mine_c, got_c),
        paired(mine_d, got_d),
    ]
    attn_grad = paired(mine_q, got_q)
    out_grad = paired(mine_o, got_o)
    groups = [(cuts[0][0], cuts[1][1])] + cuts[2:]

    def whole(part):
        return part.reshape(part.shape[0], -1)

    query_grad = whole(attn_grad[:, :, :qdim])
    key_grad = whole(attn_grad[:, :, qdim : qdim + kdim])
    value_grad = whole(attn_grad[:, :, qdim + kdim :])
    output_grad = whole(out_grad).T
    parts = []
    for k in range(3):
        parts.append(
            whole(
                jnp.concatenate(
                    [g[:, :, k * (b - a) : (k + 1) * (b - a)] for (a, b), g in zip(groups, ff_grads)],
                    2,
                )
            )
        )
    gate_grad, up_grad, down_grad = parts[0], parts[1], parts[2].T

    def row_sum(*both):
        return sum(
            jnp.sum(w.astype(jnp.float32) * g, axis=1) for w, g in both
        )

    sums = jnp.stack(
        [
            row_sum((query_weight, query_grad), (key_matrix, key_grad), (value_matrix, value_grad)),
            row_sum((gate_weight, gate_grad), (up_weight, up_grad)),
        ]
    )
    sums = sums + grid.swap(sums, C)
    sums = sums + grid.swap(sums, X)
    return (
        layer_output,
        input_gradient,
        sums[0] / attention_gain.astype(jnp.float32),
        query_grad,
        key_grad,
        value_grad,
        output_grad,
        sums[1] / feedforward_gain.astype(jnp.float32),
        gate_grad,
        up_grad,
        down_grad,
    )


def solution(mesh):
    in_specs = (
        P(("tok", "mp"), None),
        P(("tok", "mp"), None),
        P(),
        P("tok"),
        P("tok", "mp"),
        P("tok", "mp"),
        P("tok", "mp"),
        P("mp", "tok"),
        P("tok"),
        P("tok", "mp"),
        P("tok", "mp"),
        P("mp", "tok"),
    )
    out_specs = (
        P(("tok", "mp"), None),
        P(("tok", "mp"), None),
        P("tok"),
        P("tok", "mp"),
        P("tok", "mp"),
        P("tok", "mp"),
        P("mp", "tok"),
        P("tok"),
        P("tok", "mp"),
        P("tok", "mp"),
        P("mp", "tok"),
    )
    return jax.shard_map(body, mesh=mesh, in_specs=in_specs, out_specs=out_specs, check_vma=False)
```

time: 1170 us -> 846 us (0.72)
  waiting for transfers between devices: 370 us -> 0.01 us
  Pallas kernels: 421 us -> 771 us
  matrix products: 113 us -> 0 us
  local copies, waits for them, and re-layouts: 127 us -> 39.2 us
  other arithmetic: 84.9 us -> 24.3 us
  starting transfers between devices: 42.9 us -> 1.48 us
    pallas_call x9 -> x7, Pallas kernels: 421 us -> 771 us  [the longest x1 144 us: feed_forward(): pl.pallas_call(functools.partial(feed_kernel, hidden, cuts), in_specs=[HB...]
    ppermute x29 -> x0, waiting for transfers between devices: 304 us -> none  [the longest x27 298 us: ring(): lax.ppermute(value, AXES, self.pairs(lambda z, g: ((z + 1) % self.nz, g)))]
    dot_general x11 -> x0, matrix products: 113 us -> none  [the longest x5 60 us: outer_product(): lax.dot_general(left, right, (((0,), (0,)), ((), ())), preferred_element_...]
    ppermute x23 -> x2, waiting for transfers between devices: 66.7 us -> 0.01 us  [swap(): return lax.ppermute(value, AXES, self.pairs(lambda z, g: (z, g ^ bit)))]
    unnamed x202 -> x84, local copies, waits for them, and re-layouts: 52.6 us -> 11.9 us
    convert_element_type x21 -> x8, other arithmetic: 35.3 us -> 3.8 us  [the longest x4 3.23 us: spread_matrix(): return (target[:, None] == lanes[None, :]).astype(BF16)]
    ppermute x23 -> x2, starting transfers between devices: 23.9 us -> 1.48 us  [swap(): return lax.ppermute(value, AXES, self.pairs(lambda z, g: (z, g ^ bit)))]
    ppermute x29 -> x0, starting transfers between devices: 19.1 us -> none  [the longest x27 16.5 us: ring(): lax.ppermute(value, AXES, self.pairs(lambda z, g: ((z + 1) % self.nz, g)))]
  transfers between devices with their start and end apart: 52 -> 2, of which waited for: 23 -> 0; matrix products, arithmetic and copies ran while one was open for 25% -> 1% of each run, Pallas kernels for 36% -> 0%
where the time goes in v2:
time: 846 us; the launch traced here: 838 us
  Pallas kernels  771 us (91%)
  local copies, waits for them, and re-layouts  39.2 us (5%)
  other arithmetic  24.3 us (3%)
    pallas_call x1, Pallas kernels, feed_forward(): pl.pallas_call(functools.partial(feed_kernel, hidden, cuts), in_specs=[HB...  144 us
    pallas_call x1, Pallas kernels, feed_back(): pl.pallas_call(middle_kernel, grid=(1,), in_specs=[pl.BlockSpec((8, n, k)...  125 us
    pallas_call x1, Pallas kernels, attention(): pl.pallas_call(functools.partial(attention_kernel, hidden, cuts), in_spec...  118 us
    pallas_call x1, Pallas kernels, project_out(): pl.pallas_call(project_kernel, in_specs=[WHOLE] * 4 + [HBM], out_specs=[W...  112 us
    pallas_call x1, Pallas kernels, attention_back(): pl.pallas_call(back_kernel, in_specs=[HBM] + [WHOLE] * 13 + [HBM, HBM, WH...  106 us
    pallas_call x1, Pallas kernels, input_back(): pl.pallas_call(last_kernel, in_specs=[WHOLE] * 6 + [HBM] * 2, out_specs=[...  105 us
    pallas_call x1, Pallas kernels, gather_start(): pl.pallas_call(start_kernel, in_specs=[WHOLE, HBM], out_specs=[HBM, HBM],...  60.4 us
  transfers between devices with their start and end apart: 2, of which 0 were waited for; matrix products, arithmetic and copies ran while one was open for 1% of the time, Pallas kernels for 0%

profile of v2, /device:TPU:0, one launch (start us, length us, event | category | flops | bytes accessed | tf_op | source)
XLA Modules:
  0.0 837.5 jit_solution(15746768263485046487)
XLA Ops:
  0.8 0.9 fusion.2.squeeze_ref
  1.7 0.8 fusion.4.spread_ref
  2.6 1.4 reshape.324
  5.2 2.0 broadcast_in_dim.56.kid_ref
  7.2 0.7 pad_dynamic-slice_fusion
  8.1 0.9 pad_convert_fusion.spread_ref
  9.5 0.8 copy.61
  10.3 2.4 constant_dynamic-slice_fusion.11
  13.4 0.8 copy-done.1
  14.2 60.4 %gather_start.1 = (bf16[8,256,2560]{2,1,0:T(8,128)(2,1)S(1)}, bf16[2560,512]{1,0:T(8,128)(2,1)S(1)}) custom-call(bf16[256,2560]{1,0:T(8,128)(2,1)S(1)} %get-tuple-element.94.x_ref, bf16[2,320,512]{2,1,0:T(8,128)(2,1)S(1)} %maximum_bitcast_fusion.3.pack_ref), custom_call_target="tpu_custom_call" | custom-call | flops 1000000 | bytes 100000 | tf_op jit(solution)/shard_map/gather_start/pallas_call | solution.py:374
  74.6 4.0 copy-done.3
  78.6 3.2 copy.47
  81.8 0.8 convert_bitcast_fusion
  83.2 0.8 fusion.3.squeeze_ref
  84.1 0.7 fusion.6.final_ref
  84.8 0.8 copy.49.inv_ref
  85.6 3.7 fusion.5
  89.4 2.5 pad_maximum_fusion.1
  91.9 1.2 pad_maximum_fusion.6.dout_ref
  93.0 118.4 %attention.1 = (bf16[8,256,2560]{2,1,0:T(8,128)(2,1)}, bf16[2048,512]{1,0:T(8,128)(2,1)}, bf16[2560,128]{1,0:T(8,128)(2,1)}, bf16[2560,128]{1,0:T(8,128)(2,1)}, ...) custom-call(bf16[8,256,2560]{2,1,0:T(8,128)(2,1)} %copy-done.3, ...), custom_call_target="tpu_custom_call" | custom-call | flops 1000000 | bytes 100000 | tf_op jit(solution)/shard_map/attention/pallas_call | solution.py:531
  211.4 112.1 %project_out.1 = (f32[256,2560]{1,0:T(8,128)}, f32[256,1]{1,0:T(8,128)S(1)}, bf16[8,256,2560]{2,1,0:T(8,128)(2,1)}, bf16[2560,1152]{1,0:T(8,128)(2,1)}) custom-call(bf16[8,256,320]{2,1,0:T(8,128)(2,1)} %get-tuple-element.53.a_ref.o_ref, bf16[2560,320]{1,0:T(8,128)(2,1)} %get-tuple-element.54.w_ref, bf16[256,2560]{1,0:T(8,128)(2,1)S(1)} %copy-done.2, ...), custom_call_target="tpu_custom_call" | custom-call | flops 1000000 | bytes 100000 | tf_op jit(solution)/shard_map/project_out/pallas_call | solution.py:593
  323.6 0.6 copy-done.4
  324.2 143.8 %feed_forward.1 = (bf16[2048,896]{1,0:T(8,128)(2,1)}, bf16[2048,1792]{1,0:T(8,128)(2,1)}, bf16[2560,2688]{1,0:T(8,128)(2,1)}, bf16[2560,1536]{1,0:T(8,128)(2,1)}...) custom-call(bf16[2048,2560]{1,0:T(8,128)(2,1)} %bitcast.57, ...), custom_call_target="tpu_custom_call" | custom-call | flops 1000000 | bytes 100000 | tf_op jit(solution)/shard_map/feed_forward/pallas_call | solution.py:741
  468.0 124.5 %feed_back.1 = (f32[256,2560]{1,0:T(8,128)}, bf16[8,256,2560]{2,1,0:T(8,128)(2,1)}, bf16[320,768]{1,0:T(8,128)(2,1)}, bf16[320,768]{1,0:T(8,128)(2,1)}, bf16[320...) custom-call(bf16[8,256,1792]{2,1,0:T(8,128)(2,1)} %bitcast.62, bf16[2560,2688]{1,0:T(8,128)(2,1)} %get-tuple-element.61.w_ref.down_ref, ...), custom_call_target="tpu_custom_call" | custom-call | flops 1000000 | bytes 100000 | tf_op jit(solution)/shard_map/feed_back/pallas_call | solution.py:883
  592.5 106.4 %attention_back.1 = (bf16[8,256,480]{2,1,0:T(8,128)(2,1)}, bf16[2560,320]{1,0:T(8,128)(2,1)}, bf16[256,2560]{1,0:T(8,128)(2,1)}, bf16[320,768]{1,0:T(8,128)(2,1)}, bf16[320,768]{1,0:T(8,128)(2,1)}) custom-call(bf16[8,256,2560]{2,1,0:T(8,128)(2,1)} %get-tuple-element.66.da_ref, bf16[2560,320]{1,0:T(8,128)(2,1)} %get-tuple-element.54.w_ref, ...), custom_call_target="tpu_custom_call" | custom-call | flops 1000000 | bytes 100000 | tf_op jit(solution)/shard_map/attention_back/pallas_call | solution.py:1034
  698.9 105.0 %input_back.1 = (f32[256,2560]{1,0:T(8,128)}, bf16[320,320]{1,0:T(8,128)(2,1)}, bf16[320,320]{1,0:T(8,128)(2,1)}, bf16[320,480]{1,0:T(8,128)(2,1)}, bf16[320,480]{1,0:T(8,128)(2,1)}) custom-call(bf16[8,256,480]{2,1,0:T(8,128)(2,1)} %get-tuple-element.74.a_ref, bf16[2560,480]{1,0:T(8,128)(2,1)} %bitcast.55, bf16[256,2560]{1,0:T(8,128)(2,1)} %copy-done.1, ...), custom_call_target="tpu_custom_call" | custom-call | flops 1000000 | bytes 100000 | tf_op jit(solution)/shard_map/input_back/pallas_call | solution.py:1125
  804.0 1.3 select_bitcast_fusion.3
  805.4 1.0 maximum_convert_fusion.6
  807.0 1.9 fusion.25
  809.2 1.3 fusion.26
  810.7 1.0 fusion.27
  811.8 0.8 copy.50
  812.5 0.7 reshape.333
  813.4 1.5 copy.52
  815.0 1.0 multiply_reduce_fusion.4
  816.0 1.8 copy.51
  817.8 1.1 multiply_reduce_fusion.5
  819.3 1.4 copy-done.6
  822.2 1.4 copy-done.7
  824.1 0.8 copy-done.13
  825.3 1.0 copy-done.23
  826.5 1.8 pad_maximum_fusion
  828.3 1.2 pad_maximum_fusion.7
  829.4 0.6 copy-done.10
  830.5 1.4 collective-permute-start.1
  832.0 1.6 copy.59
  833.6 0.8 copy.55
  834.3 1.6 reshape.339
  (130 shorter events, 9.2 us)
Async XLA Ops:
  0.6 3.4 copy-start.41
  0.7 3.4 copy-start.40
  0.7 4.1 copy-start.33
  0.7 4.3 copy-start.32
  0.7 4.4 copy-start.39
  4.0 5.1 copy-start.34
  5.2 5.1 copy-start.24
  13.1 1.1 copy-start.1
  74.6 4.0 copy-start.3
  78.6 3.2 copy-start
  83.2 128.2 %copy-start.5 = (f32[1,2560]{1,0:T(1,128)}, f32[1,2560]{1,0:T(1,128)S(1)}, u32[]{:S(2)}) copy-start(f32[1,2560]{1,0:T(1,128)S(1)} %get-tuple-element.135.gain_ref) | copy-start | bytes 30724
  89.4 2.5 copy-start.18
  89.4 2.5 copy-start.19
  93.0 118.4 %copy-start.2 = (bf16[256,2560]{1,0:T(8,128)(2,1)S(1)}, bf16[256,2560]{1,0:T(8,128)(2,1)}, u32[]{:S(2)}) copy-start(bf16[256,2560]{1,0:T(8,128)(2,1)} %copy-done.1) | copy-start | bytes 3932164
  323.5 0.7 copy-start.4
  803.9 2.4 copy-start.26
  804.0 2.4 copy-start.27
  804.0 2.4 copy-start.30
  804.0 2.4 copy-start.31
  807.0 1.9 copy-start.28
  807.0 1.9 copy-start.29
  809.2 1.3 copy-start.37
  809.2 1.4 copy-start.38
  811.8 1.4 copy-start.17
  813.2 5.9 copy-start.12
  813.2 5.7 copy-start.16
  813.2 5.7 copy-start.22
  815.0 4.1 copy-start.25
  819.1 1.6 copy-start.6
  819.3 2.7 copy-start.8
  819.3 2.3 copy-start.11
  819.3 2.4 copy-start.15
  819.3 2.5 copy-start.21
  822.0 1.6 copy-start.7
  822.2 1.8 copy-start.9
  822.2 2.7 copy-start.13
  824.0 6.5 collective-permute-start
  824.9 1.3 copy-start.23
  825.3 1.1 copy-start.35
  825.3 1.1 copy-start.36
  828.3 1.8 copy-start.10
  828.3 2.0 copy-start.14
  828.3 2.0 copy-start.20
  830.5 5.4 collective-permute-start.1

commit v3 on v2

v3 whole, which is shorter than its diff:
```python
import functools

import jax
import jax.numpy as jnp
import ml_dtypes
import numpy as np
from jax import lax
from jax.experimental import pallas as pl
from jax.experimental.pallas import tpu as pltpu
from jax.sharding import PartitionSpec as P

HEAD_SIZE = 80
WINDOW_LENGTH = 512
EPS = 1e-05
THETA = 1000000.0
FLOOR = -1e30
AXES = ("tok", "mp")
FF_CHUNKS = (128, 384, 256, 128)
FF_PARTS = (256, 256, 256, 128)


class Grid:
    def __init__(self):
        self.nz = lax.axis_size("tok") // 2
        tok = lax.axis_index("tok")
        mp = lax.axis_index("mp")
        self.z, self.y = tok // 2, tok % 2
        self.x, self.c = mp // 2, mp % 2
        self.me = self.y * 4 + self.x * 2 + self.c

    def pairs(self, move):
        out = []
        for z in range(self.nz):
            for g in range(8):
                target = move(z, g)
                if target is not None:
                    out.append((z * 8 + g, target[0] * 8 + target[1]))
        return out

    def swap(self, value, bit):
        return lax.ppermute(value, AXES, self.pairs(lambda z, g: (z, g ^ bit)))

    def ring(self, value):
        return lax.ppermute(value, AXES, self.pairs(lambda z, g: ((z + 1) % self.nz, g)))

    def step(self, value, d):
        def move(z, g):
            return (z + d, g) if 0 <= z + d < self.nz else None

        return lax.ppermute(value, AXES, self.pairs(move))


Y, X, C = 4, 2, 1


LANES = 128
SCALE = HEAD_SIZE ** (-0.5)
LOG2E = 1.4426950408889634
MIB = 1024 * 1024
BF16 = jnp.bfloat16
F32 = jnp.float32
HBM = pl.BlockSpec(memory_space=pl.ANY)
WHOLE = pl.BlockSpec(memory_space=pltpu.VMEM)
MESH = pl.DeviceIdType.MESH


def light(**kwargs):
    return dict(
        cost_estimate=pl.CostEstimate(flops=1000000, bytes_accessed=100000, transcendentals=0),
        **kwargs,
    )


def params(mib, **kwargs):
    return pltpu.CompilerParams(vmem_limit_bytes=mib * MIB, **kwargs)


ROPE_STEP = 64


def rope_parts(count, first, width):
    half = width // 2
    freqs = THETA ** (-(jnp.arange(half, dtype=jnp.int32).astype(F32) * 2.0 / width))
    high = first + ROPE_STEP * jnp.arange(count // ROPE_STEP, dtype=jnp.int32)
    places = jnp.concatenate([high, jnp.arange(ROPE_STEP, dtype=jnp.int32)]).astype(F32)
    blank = jnp.zeros((LANES // 2 - half,), F32)
    lanes = jnp.concatenate([freqs, blank, freqs, blank])
    angles = places[:, None] * lanes[None, :]
    return jnp.stack([jnp.cos(angles), jnp.sin(angles)])


def spread_matrix(turned, plain, rows=0, columns=0):
    half = HEAD_SIZE // 2
    f = np.arange((turned + plain) * HEAD_SIZE)
    head, place = f // HEAD_SIZE, f % HEAD_SIZE
    target = head * LANES + place
    target = target + np.where((head < turned) & (place >= half), LANES // 2 - half, 0)
    out = np.zeros(
        (max(rows, f.size), max(columns, (turned + plain) * LANES)), ml_dtypes.bfloat16
    )
    out[f, target] = 1
    return out


def nt(left, right):
    return lax.dot_general(left, right, (((1,), (1,)), ((), ())), preferred_element_type=F32)


def nn(left, right):
    return lax.dot_general(left, right, (((1,), (0,)), ((), ())), preferred_element_type=F32)


def tn(left, right):
    return lax.dot_general(left, right, (((0,), (0,)), ((), ())), preferred_element_type=F32)


def mask_bias(first, keys, rows):
    kk = lax.broadcasted_iota(jnp.int32, (keys, rows), 0)
    qq = lax.broadcasted_iota(jnp.int32, (keys, rows), 1)
    return jnp.where((kk >= first) & (kk - qq <= WINDOW_LENGTH), 0.0, FLOOR)


def identity(n):
    i = lax.broadcasted_iota(jnp.int32, (n, n), 0)
    return (i == lax.broadcasted_iota(jnp.int32, (n, n), 1)).astype(BF16)


def rotation(wires, model):
    width = model // wires.nz
    if width % LANES:
        return [(slice(0, model), slice(0, model))]
    out = []
    for s in range(wires.nz):
        block = lax.rem(wires.at_z - s + wires.nz, wires.nz)
        start = pl.multiple_of(block * width, LANES)
        out.append((slice(s * width, (s + 1) * width), pl.ds(start, width)))
    return out


def outside_rotation(grid, value, back=False):
    width = value.shape[-1] // grid.nz
    if width % LANES == 0:
        return value
    parts = []
    for s in range(grid.nz):
        block = lax.rem(grid.z - s + grid.nz, grid.nz)
        parts.append(lax.dynamic_slice_in_dim(value, block * width, width, value.ndim - 1))
    return jnp.concatenate(parts, -1)


def only(condition, act):
    if condition is None:
        act()
    else:
        pl.when(condition)(act)


class Copy:
    def __init__(self, copy, when, got, index):
        self.copy, self.when, self.got, self.index = copy, when, got, index

    def wait_recv(self):
        only(self.got, self.copy.wait_recv)

    def wait_send(self):
        only(self.when, self.copy.wait_send)


SEMAPHORES = 96


def semaphores():
    return [
        pltpu.SemaphoreType.DMA((SEMAPHORES,)),
        pltpu.SemaphoreType.DMA((SEMAPHORES,)),
        pltpu.SemaphoreType.DMA((SEMAPHORES,)),
    ]


class Wires:
    def __init__(self, send, recv, local):
        self.send, self.recv, self.here = send, recv, local
        self.count = self.local_count = 0
        self.copies = []
        tokens = lax.axis_size("tok")
        tok, mp = lax.axis_index("tok"), lax.axis_index("mp")
        self.nz = tokens // 2
        self.at_z, self.at_y = tok // 2, tok % 2
        self.at_x, self.at_c = mp // 2, mp % 2
        self.x = (tok, lax.rem(mp + 2, 4))
        self.y = (tok + 1 - 2 * self.at_y, mp)
        self.c = (tok, mp + 1 - 2 * self.at_c)
        self.up = (lax.rem(tok + 2, tokens), mp)
        self.down = (lax.rem(tok + tokens - 2, tokens), mp)

    def hello(self):
        barrier = pltpu.get_barrier_semaphore()
        for peer in (self.x, self.y, self.c, self.up, self.down):
            pl.semaphore_signal(barrier, inc=1, device_id=peer, device_id_type=MESH)

    def ready(self):
        pl.semaphore_wait(pltpu.get_barrier_semaphore(), 5)

    def greet(self):
        self.hello()
        self.ready()

    def start(self, source, target, peer, when=None, got=None, index=None):
        i = index
        if index is None:
            i = self.count
            self.count += 1
        copy = pltpu.make_async_remote_copy(
            src_ref=source,
            dst_ref=target,
            send_sem=self.send.at[i],
            recv_sem=self.recv.at[i],
            device_id=peer,
            device_id_type=MESH,
        )
        only(when, copy.start)
        made = Copy(copy, when, got, i)
        self.copies.append(made)
        return made

    def local(self, source, target):
        copy = pltpu.make_async_copy(source, target, self.here.at[self.local_count])
        self.local_count += 1
        copy.start()
        return copy

    def natural(self, b):
        spots = ((self.at_y, b // 4), (self.at_x, b // 2 % 2), (self.at_c, b % 2))
        place = 0
        for at, bit in spots:
            place = 2 * place + at + bit - 2 * at * bit
        return place

    def finish(self):
        for copy in self.copies:
            copy.wait_send()


def drain(*parts):
    parts = list(parts)
    while parts:
        parts = [part for part in parts if next(part, None) is not None]


def run(part):
    next(part, None)


def exchange_halves(wires, sources, slot, bounce=None):
    n = slot.shape[0] // 2
    rows = pl.ds(pl.multiple_of(wires.at_y * n, n), n)
    arrivals, copies = [], []
    for pick, lo, hi in sources:
        arrivals.append(wires.start(pick(1 - wires.at_y), slot.at[rows, lo:hi], wires.y))
        to = slot.at[rows, lo:hi] if bounce is None else bounce.at[:, lo:hi]
        copies.append(wires.local(pick(wires.at_y), to))
    yield 1
    for copy in copies:
        copy.wait()
    if bounce is not None:
        wires.local(bounce, slot.at[rows]).wait()
    for arrival in arrivals:
        arrival.wait_recv()


def along_z(wires, first, slot):
    nz, z = wires.nz, wires.at_z
    get = lambda s: first if s == 0 else slot(s)
    for s in range(1, nz):
        up = wires.start(get(s - 1), slot(s), wires.up, (z >= s - 1) & (z < nz - 1), z >= s)
        down = wires.start(
            get((nz - s + 1) % nz), slot(nz - s), wires.down, (z + s <= nz) & (z >= 1), z + s < nz
        )
        yield 1
        up.wait_recv()
        down.wait_recv()


def add_into(target, source):
    @pl.loop(0, target.shape[0] // 32)
    def _(t):
        part = pl.ds(pl.multiple_of(t * 32, 32), 32)
        target[part, :] = (target[part, :].astype(F32) + source[part, :].astype(F32)).astype(BF16)


def sum_along_z(wires, p, above, below, stage, total):
    nz, z = wires.nz, wires.at_z
    ups, downs = {}, {}

    def ends(s):
        ups[s] = wires.start(p(s), above.at[s - 1], wires.up, z == 0, (z >= 1) & (z <= s))
        downs[s] = wires.start(
            p(nz - s), below.at[s - 1], wires.down, z == nz - 1, (z + s >= nz - 1) & (z < nz - 1)
        )

    ends(1)
    for s in range(2, nz):
        loads = [wires.local(p(s), stage.at[0]), wires.local(p(nz - s), stage.at[1])]
        yield 1
        ups[s - 1].wait_recv()
        downs[s - 1].wait_recv()
        for load in loads:
            load.wait()
        ends(s)
        rising = (z >= 1) & (z < s) & (z < nz - 1)
        falling = (z + s >= nz) & (z < nz - 1) & (z >= 1)
        only(rising, lambda s=s: add_into(above.at[s - 2], stage.at[0]))
        wires.start(above.at[s - 2], above.at[s - 1], wires.up, rising, None, ups[s].index)
        only(falling, lambda s=s: add_into(below.at[s - 2], stage.at[1]))
        wires.start(below.at[s - 2], below.at[s - 1], wires.down, falling, None, downs[s].index)
    load = wires.local(p(0), stage.at[0])
    yield 1
    ups[nz - 1].wait_recv()
    downs[nz - 1].wait_recv()
    load.wait()
    only(z >= 1, lambda: add_into(stage.at[0], above.at[nz - 2]))
    only(z < nz - 1, lambda: add_into(stage.at[0], below.at[nz - 2]))
    kept = wires.local(stage.at[0], total)
    yield 1
    kept.wait()


def swap_rows(wires, total, got):
    n = got.shape[0]
    other = pl.ds(pl.multiple_of((1 - wires.at_y) * n, n), n)
    sent = wires.start(total.at[other], got, wires.y)
    yield 1
    sent.wait_recv()


def sum_scratch(nz, rows, cols):
    return [
        pltpu.VMEM((nz - 1, rows, cols), BF16),
        pltpu.VMEM((nz - 1, rows, cols), BF16),
        pltpu.VMEM((2, rows, cols), BF16),
    ]


def swap_outputs(*totals):
    return [jax.ShapeDtypeStruct((t.shape[0] // 2, t.shape[1]), BF16) for t in totals]


def columns(ref, rows, lo, hi):
    return lambda s: ref.at[pl.ds(s * rows, rows), lo:hi]


def gather_weight_rows(wires, sources, out, bounce=None):
    n = out.shape[0] // wires.nz
    slot = lambda s: out.at[pl.ds(s * n, n)]
    yield from exchange_halves(wires, sources, slot(0), bounce)
    yield from along_z(wires, slot(0), slot)


def gather_phase(wires, block, out, parts):
    views = [(pl.ds(lo, hi - lo), link) for lo, hi, link in parts]
    on_y = [v for v in views if v[1] == "x"] + [v for v in views if v[1] == "y"]
    on_x = on_y[::-1]
    mine = wires.local(block, out.at[0])
    from_y, from_x, diagonal = {}, {}, []
    c = [wires.start(block, out.at[1], wires.c)]
    for k, (rows, _) in enumerate(on_x):
        from_x[k] = wires.start(block.at[rows], out.at[2, rows], wires.x)
    yield 1
    for k, (rows, _) in enumerate(on_y):
        from_y[k] = wires.start(block.at[rows], out.at[4, rows], wires.y)
    yield 1
    for k in range(len(views)):
        for place, arrived, (rows, link), via, own in (
            (4, from_y[k], on_y[k], wires.x, "x"), (2, from_x[k], on_x[k], wires.y, "y"),
        ):
            arrived.wait_recv()
            if link == own:
                relay = wires.start(out.at[place, rows], out.at[6, rows], via)
                diagonal.append((relay, rows))
            c.append(wires.start(out.at[place, rows], out.at[place + 1, rows], wires.c))
        yield 1
    for relay, rows in diagonal:
        relay.wait_recv()
        c.append(wires.start(out.at[6, rows], out.at[7, rows], wires.c))
        yield 1
    for copy in c:
        copy.wait_recv()
    mine.wait()


def halved(n, cut=None):
    cut = n // 2 if cut is None else cut
    return [(0, cut, "x"), (cut, n, "y")]


def start_kernel(
    x_ref, dout_ref, gain_ref, qw_ref, kw_ref, vw_ref, ow_ref, ids_ref, rope_ref,
    x_own, dout_own, opack, cos_ref, sin_ref, first_ref, x_all, w_all,
    pack, send, recv, local,
):
    wires = Wires(send, recv, local)
    wires.hello()
    model = x_ref.shape[1]
    turns = rotation(wires, model)
    at = qw_ref.shape[1] // 2
    for h in range(2):
        pack[h, :, 0:at] = qw_ref[:, h * at : (h + 1) * at]
    for ref in (kw_ref, vw_ref):
        n = ref.shape[0] // 2
        eye = identity(n)
        for h in range(2):
            pack[h, :, at : at + n] = tn(ref[h * n : (h + 1) * n, :], eye).astype(BF16)
        at += n
    rest = pack.shape[2] - at
    row = lax.broadcasted_iota(jnp.int32, (2, rest), 0)
    lane = lax.broadcasted_iota(jnp.int32, (2, rest), 1)
    tail = tn(gain_ref[...], (row == lane).astype(BF16)).astype(BF16)
    for h in range(2):
        pack[h, :, at:] = tail
    wires.ready()
    weights = gather_weight_rows(wires, [(lambda y: pack.at[y], 0, pack.shape[2])], w_all)
    run(weights)
    for to, of in turns:
        x_own[:, to] = x_ref[:, of]
    tokens = gather_phase(wires, x_own, x_all, halved(x_own.shape[0], START_CUT))
    run(tokens)
    run(weights)
    run(tokens)
    for to, of in turns:
        dout_own[:, to] = dout_ref[:, of]
    run(tokens)
    n = ow_ref.shape[1] // 2
    for h in range(2):
        opack[h] = ow_ref[:, h * n : (h + 1) * n]
    run(weights)
    run(tokens)
    length = first_ref.shape[1]
    lane = lax.broadcasted_iota(jnp.int32, (1, LANES), 1)
    sign = jnp.where(lane < LANES // 2, -1.0, 1.0)
    steps = length // ROPE_STEP
    cos_low, sin_low = rope_ref[0, steps:, :], rope_ref[1, steps:, :]
    for t in range(steps):
        part = slice(t * ROPE_STEP, (t + 1) * ROPE_STEP)
        cos_high, sin_high = rope_ref[0, t : t + 1, :], rope_ref[1, t : t + 1, :]
        cos_ref[part, :] = cos_high * cos_low - sin_high * sin_low
        sin_ref[part, :] = (sin_high * cos_low + cos_high * sin_low) * sign
    offset = pl.multiple_of(wires.at_z * length, length)
    ids = ids_ref[:, pl.ds(offset, length)]
    begin = jnp.zeros((1, length), jnp.int32)
    for number in range(1, 5):
        count = jnp.sum((ids_ref[...] < number).astype(jnp.int32), axis=1, keepdims=True)
        begin = jnp.where(ids >= number, count, begin)
    window = lax.broadcasted_iota(jnp.int32, (1, length), 1) - (WINDOW_LENGTH - 1)
    first_ref[...] = jnp.maximum(begin - offset, window) + WINDOW_LENGTH
    drain(weights, tokens)
    wires.finish()


START_CUT = 160


def gather_start(inputs, dout, gains, query, key_t, value_t, out_t, ids, rope, width):
    n, model = inputs.shape
    rows = query.shape[0]
    length = 8 * n
    return pl.pallas_call(
        start_kernel,
        in_specs=[WHOLE] * 9,
        out_specs=[WHOLE] * 6 + [HBM] * 2,
        out_shape=[
            jax.ShapeDtypeStruct((n, model), BF16),
            jax.ShapeDtypeStruct((n, model), BF16),
            jax.ShapeDtypeStruct((2, rows, out_t.shape[1] // 2), BF16),
            jax.ShapeDtypeStruct((length, LANES), F32),
            jax.ShapeDtypeStruct((length, LANES), F32),
            jax.ShapeDtypeStruct((1, length), jnp.int32),
            jax.ShapeDtypeStruct((8, n, model), BF16),
            jax.ShapeDtypeStruct((model, width), BF16),
        ],
        scratch_shapes=[pltpu.VMEM((2, rows, width), BF16)] + semaphores(),
        compiler_params=params(62, collective_id=0, has_side_effects=True),
        name="gather_start",
        **light(),
    )(inputs, dout, gains, query, key_t, value_t, out_t, ids, rope)


def feed_sources(gate, up, down, cut, hidden):
    a, b = cut
    n = b - a
    step = LANES

    def pick(ref):
        return lambda y: ref.at[:, pl.ds(pl.multiple_of(y * hidden + a, step), n)]

    return [(pick(ref), k * n, (k + 1) * n) for k, ref in enumerate((gate, up, down))]


def attention_kernel(
    hidden, cuts,
    x_ref, w_ref, spread_ref, squeeze_ref, cos_ref, sin_ref, first_ref, dout_ref,
    opack_ref, gate_ref, up_ref, down_ref,
    q_ref, k_ref, v_ref, o_ref, lse_ref, gain_ref, a1_ref, dout_all, w_out, w_zero, *rest,
):
    slots, rest = rest[: len(cuts) - 1], rest[len(cuts) - 1 :]
    x_all, w_flat, w_pad, bounce_out, *bounces, send, recv, local = rest
    wires = Wires(send, recv, local)
    nz, z = wires.nz, wires.at_z
    rows = x_all.shape[1]
    model = x_all.shape[2]
    heads = q_ref.shape[1] // LANES
    keys = rows + WINDOW_LENGTH
    length = 8 * rows
    wires.greet()
    load_w = wires.local(w_ref, w_flat)
    order = (6, 7, 0, 1, 2, 3, 4, 5)
    loads = {}
    for b in order:
        at = wires.natural(b)
        loads[b] = wires.local(x_ref.at[at], x_all.at[at])
    out_weights = gather_weight_rows(
        wires, [(lambda y: opack_ref.at[y], 0, opack_ref.shape[2])], w_out, bounce_out
    )
    run(out_weights)
    quarter = rows // 4
    cotangents = gather_phase(
        wires, dout_ref, dout_all, [(t * quarter, (t + 1) * quarter, "x") for t in range(4)]
    )
    run(cotangents)
    load_w.wait()

    @pl.loop(0, model // 512)
    def _(t):
        part = pl.ds(pl.multiple_of(t * 512, 512), 512)
        w_pad[part, :] = nn(w_flat[part, :], spread_ref[...]).astype(BF16)

    zero_weights = gather_weight_rows(
        wires, feed_sources(gate_ref, up_ref, down_ref, cuts[0], hidden), w_zero, bounces[0]
    )
    run(zero_weights)
    run(out_weights)
    place = lax.broadcasted_iota(jnp.int32, (8, w_flat.shape[1]), 1)
    row = lax.broadcasted_iota(jnp.int32, (8, w_flat.shape[1]), 0)
    which = (place == (heads + 2) * HEAD_SIZE + row).astype(BF16)
    gain_ref[...] = nt(which, w_flat[...])
    gain = gain_ref[0:1, :]

    @pl.when(z == 0)
    def _():
        k_ref[0:WINDOW_LENGTH, :] = jnp.zeros((WINDOW_LENGTH, LANES), BF16)
        v_ref[0:WINDOW_LENGTH, :] = jnp.zeros((WINDOW_LENGTH, LANES), BF16)

    stores = []
    for b in order:
        at = wires.natural(b)
        loads[b].wait()
        x = x_all[at].astype(F32)
        inverse = lax.rsqrt(jnp.mean(x * x, axis=1, keepdims=True) + EPS)
        a1 = (x * inverse * gain).astype(BF16)
        x_all[at] = a1
        stores.append(wires.local(x_all.at[at], a1_ref.at[at]))
        acc = nn(a1, w_pad[...])
        here = slice(b * rows, (b + 1) * rows)
        there = slice(WINDOW_LENGTH + b * rows, WINDOW_LENGTH + (b + 1) * rows)
        cosine, sine = cos_ref[here, :], sin_ref[here, :]
        for h in range(heads + 1):
            u = acc[:, h * LANES : (h + 1) * LANES]
            turned = (u * cosine + pltpu.roll(u, LANES // 2, 1) * sine).astype(BF16)
            if h < heads:
                q_ref[here, h * LANES : (h + 1) * LANES] = turned
            else:
                k_ref[there, :] = turned
        v_ref[there, :] = acc[:, (heads + 1) * LANES :].astype(BF16)
        if b == 7:
            halo = [
                wires.start(
                    ref.at[pl.ds(length, WINDOW_LENGTH)], ref.at[pl.ds(0, WINDOW_LENGTH)],
                    wires.up, z < nz - 1, z > 0,
                )
                for ref in (k_ref, v_ref)
            ]
        if b == 0:
            run(zero_weights)
            run(cotangents)
        if b == 2:
            run(out_weights)
    for copy in halo:
        copy.wait_recv()

    def block(b, at):
        start = pl.multiple_of(b * rows, rows)
        span = pl.ds(start, keys)
        here = pl.ds(start, rows)
        kb = k_ref[span, :]
        vt = v_ref[span, :].T
        bias = mask_bias(first_ref[:, here] - start, keys, rows)
        outs = []
        for h in range(heads):
            lanes = slice(h * LANES, (h + 1) * LANES)
            s = nt(kb, q_ref[here, lanes]) * (SCALE * LOG2E) + bias
            peak = jnp.max(s, axis=0, keepdims=True)
            p = jnp.exp2(s - peak)
            total = jnp.sum(p, axis=0, keepdims=True)
            ot = nn(vt, p.astype(BF16)) / total
            outs.append(ot.T.astype(BF16))
            lse_ref[b, h : h + 1, :] = peak + jnp.log2(total)
        o_ref[at] = nn(jnp.concatenate(outs, 1), squeeze_ref[...]).astype(BF16)

    def blocks(lo, hi):
        @pl.loop(lo, hi)
        def _(b):
            block(b, wires.natural(b))

    run(zero_weights)
    run(cotangents)
    run(cotangents)
    blocks(0, 2)
    run(out_weights)
    run(cotangents)
    blocks(2, 4)
    run(cotangents)
    run(zero_weights)
    exchanges = [
        exchange_halves(
            wires, feed_sources(gate_ref, up_ref, down_ref, cut, hidden), slot, bounce
        )
        for cut, slot, bounce in zip(cuts[1:], slots, bounces[1:])
    ]
    run(exchanges[0])
    blocks(4, 6)
    for exchange in exchanges[1:]:
        run(exchange)
    blocks(6, 8)
    for store in stores:
        store.wait()
    drain(out_weights, zero_weights, cotangents, *exchanges)
    wires.finish()


def attention(x_all, w_attn, cosine, sine, first_key, dout, opack, gate, up, down, heads, cuts):
    _, n, model = x_all.shape
    length = 8 * n
    hidden = gate.shape[1] // 2
    wide = heads * LANES
    spread = spread_matrix(heads + 1, 1, rows=w_attn.shape[1])
    squeeze = spread_matrix(0, heads).T
    slot = 2 * gate.shape[0]
    sizes = [3 * (b - a) for a, b in cuts]
    return pl.pallas_call(
        functools.partial(attention_kernel, hidden, cuts),
        in_specs=[HBM, HBM] + [WHOLE] * 6 + [HBM] * 4,
        out_specs=[WHOLE] * 6 + [HBM] * (3 + len(cuts)),
        out_shape=[
            jax.ShapeDtypeStruct((length, wide), BF16),
            jax.ShapeDtypeStruct((length + WINDOW_LENGTH, LANES), BF16),
            jax.ShapeDtypeStruct((length + WINDOW_LENGTH, LANES), BF16),
            jax.ShapeDtypeStruct((8, n, heads * HEAD_SIZE), BF16),
            jax.ShapeDtypeStruct((8, heads, n), F32),
            jax.ShapeDtypeStruct((8, model), F32),
            jax.ShapeDtypeStruct((8, n, model), BF16),
            jax.ShapeDtypeStruct((8, n, model), BF16),
            jax.ShapeDtypeStruct((model, opack.shape[2]), BF16),
            jax.ShapeDtypeStruct((model, sizes[0]), BF16),
        ]
        + [jax.ShapeDtypeStruct((slot, size), BF16) for size in sizes[1:]],
        scratch_shapes=[
            pltpu.VMEM((8, n, model), BF16),
            pltpu.VMEM(w_attn.shape, BF16),
            pltpu.VMEM((model, spread.shape[1]), BF16),
            pltpu.VMEM(opack.shape[1:], BF16),
        ]
        + [pltpu.VMEM((gate.shape[0], size), BF16) for size in sizes]
        + semaphores(),
        compiler_params=params(62, collective_id=5, has_side_effects=True),
        name="attention",
        **light(),
    )(x_all, w_attn, spread, squeeze, cosine, sine, first_key, dout, opack, gate, up, down)


def project_kernel(
    a_ref, w_ref, x_ref, gain_ref, slot_ref, res_ref, inv_ref, out_ref, w_all,
    block, cs, cr, q, xr, yr, tr, br, send, recv, local,
):
    wires = Wires(send, recv, local)
    wires.greet()
    n = slot_ref.shape[0]
    own = wires.local(slot_ref, w_all.at[pl.ds(0, n)])
    weights = along_z(wires, slot_ref, lambda s: w_all.at[pl.ds(s * n, n)])
    run(weights)

    def emit(rows, total):
        residual = x_ref[rows, :].astype(F32) + total
        inverse = lax.rsqrt(jnp.mean(residual * residual, axis=1, keepdims=True) + EPS)
        res_ref[rows, :] = residual
        inv_ref[rows, :] = inverse
        block[rows, :] = (residual * inverse * gain_ref[1:2, :]).astype(BF16)

    sums = reduce_phase(wires, a_ref, w_ref, cs, cr, q, xr, yr, tr, br, emit)
    for _ in range(6):
        run(sums)
    run(weights)
    drain(sums)
    tokens = gather_phase(wires, block, out_ref, halved(block.shape[0]))
    run(tokens)
    run(tokens)
    run(tokens)
    run(weights)
    drain(tokens, weights)
    own.wait()
    wires.finish()


def project_out(o, w_out, inputs, gain, slot):
    n, model = inputs.shape
    return pl.pallas_call(
        project_kernel,
        in_specs=[WHOLE] * 5,
        out_specs=[WHOLE, WHOLE, HBM, HBM],
        out_shape=[
            jax.ShapeDtypeStruct((n, model), F32),
            jax.ShapeDtypeStruct((n, 1), F32),
            jax.ShapeDtypeStruct((8, n, model), BF16),
            jax.ShapeDtypeStruct((model, slot.shape[1]), BF16),
        ],
        scratch_shapes=[pltpu.VMEM((n, model), BF16)] + reduce_scratch(n, model) + semaphores(),
        compiler_params=params(62, collective_id=2, has_side_effects=True),
        name="project_out",
        **light(),
    )(o, w_out, inputs, gain, slot)


def feed_kernel(
    hidden, cuts, chunks,
    a_ref, d_ref, w0_ref, w1_ref, w2_ref, w3_ref,
    m_ref, g_ref, w_ref, grad0, grad1, grad2, grad3, total,
    a, d, w, m, g, stage, above, below, extra, send, recv, local,
):
    wires = Wires(send, recv, local)
    nz = wires.nz
    length, model = a.shape
    slot = model // nz
    wires.hello()

    def spots(lo, hi):
        out = []
        for k in range(3):
            for first, last in chunks:
                left, right = max(lo, first), min(hi, last)
                if left < right:
                    base = 2 * hidden if k == 2 else first + k * (last - first)
                    start = base + left
                    out.append((k * (hi - lo) + left - lo, start, right - left, k, left))
        return out

    loads = []
    for ref, (lo, hi) in ((w0_ref, cuts[0]), (w1_ref, cuts[1])):
        for of, to, n, _, _ in spots(lo, hi):
            loads.append(wires.local(ref.at[:, of : of + n], w.at[:, to : to + n]))
    rows = length // 8
    a_loads, d_loads = [], []

    def fetch(half):
        part = pl.ds(half * 4 * rows, 4 * rows)
        a_loads.append(wires.local(a_ref.at[part], a.at[part]))
        d_loads.append(wires.local(d_ref.at[part], d.at[part]))

    fetch(0)

    def carried(ref, cut):
        pieces, copies = [], []
        for of, to, n, _, _ in spots(*cut):
            pieces.append((to, to + n))
            copies.append(wires.local(ref.at[:, of : of + n], w.at[pl.ds(0, slot), to : to + n]))
        yield 1
        for copy in copies:
            copy.wait()
        hops = [
            along_z(
                wires,
                w.at[pl.ds(0, slot), lo:hi],
                lambda s, lo=lo, hi=hi: w.at[pl.ds(s * slot, slot), lo:hi],
            )
            for lo, hi in pieces
        ]
        while hops:
            hops = [hop for hop in hops if next(hop, None) is not None]
            yield 1

    later = [carried(ref, cut) for ref, cut in zip((w2_ref, w3_ref), cuts[2:])]
    for part in later:
        run(part)
    wires.ready()
    run(later[0])
    for copy in loads:
        copy.wait()

    def units(lo, hi, blocks):
        n = hi - lo

        @pl.loop(*blocks)
        def _(b):
            part = pl.ds(pl.multiple_of(b * rows, rows), rows)
            both = nn(a[part, :], w[:, 2 * lo : 2 * hi])
            gate, up = both[:, :n], both[:, n:]
            dmixed = nn(d[part, :], w[:, 2 * hidden + lo : 2 * hidden + hi])
            sigma = jax.nn.sigmoid(gate)
            silu = gate * sigma
            m[part, lo:hi] = (silu * up).astype(BF16)
            g[part, lo + hi : 2 * hi] = (dmixed * silu).astype(BF16)
            g[part, 2 * lo : lo + hi] = (
                dmixed * up * sigma * (1.0 + gate * (1.0 - sigma))
            ).astype(BF16)

    tile = stage.shape[1]
    last = model // tile

    def weight_grads(lo, hi, out, tiles=None):
        n = hi - lo
        tiles = (0, last) if tiles is None else tiles

        def save(t):
            return pltpu.make_async_copy(
                stage.at[t % 2, :, 0 : 3 * n],
                out.at[pl.ds(pl.multiple_of(t * tile, tile), tile)],
                local.at[SEMAPHORES - 1 - t % 2],
            )

        @pl.loop(*tiles)
        def _(t):
            @pl.when(t >= 2)
            def _():
                save(t - 2).wait()

            cols = pl.ds(pl.multiple_of(t * tile, tile), tile)
            stage[t % 2, :, 0 : 2 * n] = tn(a[:, cols], g[:, 2 * lo : 2 * hi]).astype(BF16)
            stage[t % 2, :, 2 * n : 3 * n] = tn(d[:, cols], m[:, lo:hi]).astype(BF16)
            save(t).start()

        if tiles[1] == last:
            save(last - 2).wait()
            save(last - 1).wait()

    a_loads[0].wait()
    d_loads[0].wait()
    fetch(1)
    units(*chunks[0], (0, 4))
    a_loads[1].wait()
    d_loads[1].wait()
    units(*chunks[0], (4, 8))
    weight_grads(*chunks[0], grad0, (0, 2))
    run(later[0])
    weight_grads(*chunks[0], grad0, (2, last))
    sums = sum_along_z(
        wires, columns(grad0, slot, 0, total.shape[1]), above, below, extra, total
    )
    run(sums)
    units(*chunks[1], (0, 8))
    run(later[0])
    weight_grads(*chunks[1], grad1, (0, 4))
    run(sums)
    run(later[1])
    weight_grads(*chunks[1], grad1, (4, last))
    drain(later[0])
    units(*chunks[2], (0, 4))
    run(later[1])
    run(sums)
    units(*chunks[2], (4, 8))
    weight_grads(*chunks[2], grad2, (0, 2))
    run(later[1])
    weight_grads(*chunks[2], grad2, (2, last))
    drain(later[1])
    outs = [wires.local(w, w_ref)]
    units(*chunks[3], (0, 8))
    outs += [wires.local(m, m_ref), wires.local(g, g_ref)]
    run(sums)
    weight_grads(*chunks[3], grad3)
    drain(sums)
    for copy in outs:
        copy.wait()
    wires.finish()


def feed_forward(a2, dout, w0, w1, w2, w3, cuts, chunks):
    length, model = a2.shape
    hidden = cuts[-1][1]
    sizes = [b - a for a, b in chunks]
    rows = w3.shape[0]
    nz = model // rows
    return pl.pallas_call(
        functools.partial(feed_kernel, hidden, cuts, chunks),
        in_specs=[HBM] * 6,
        out_specs=[HBM] * 8,
        out_shape=[
            jax.ShapeDtypeStruct((length, hidden), BF16),
            jax.ShapeDtypeStruct((length, 2 * hidden), BF16),
            jax.ShapeDtypeStruct((model, 3 * hidden), BF16),
        ]
        + [jax.ShapeDtypeStruct((model, 3 * n), BF16) for n in sizes]
        + [jax.ShapeDtypeStruct((rows, 3 * sizes[0]), BF16)],
        scratch_shapes=[
            pltpu.VMEM((length, model), BF16),
            pltpu.VMEM((length, model), BF16),
            pltpu.VMEM((model, 3 * hidden), BF16),
            pltpu.VMEM((length, hidden), BF16),
            pltpu.VMEM((length, 2 * hidden), BF16),
            pltpu.VMEM((2, 512, 3 * max(sizes)), BF16),
        ]
        + sum_scratch(nz, rows, 3 * sizes[0])
        + semaphores(),
        compiler_params=params(62, collective_id=1, has_side_effects=True),
        name="feed_forward",
        **light(),
    )(a2, dout, w0, w1, w2, w3)


def reduce_phase(wires, a, w, cs, cr, q, xr, yr, tr, br, emit, ready=None):
    n = q.shape[1]
    half = n // 2
    top, bottom = pl.ds(0, half), pl.ds(half, half)
    model = q.shape[2]
    tile = 512
    deep = a.shape[2]

    def product(place, target):
        if ready is not None:
            ready(place)

        @pl.loop(0, model // tile)
        def _(t):
            cols = pl.ds(pl.multiple_of(t * tile, tile), tile)
            target[:, cols] = nt(a[place], w[cols, 0:deep]).astype(BF16)

    waits = {}
    for j in (3, 1, 2, 0):
        product(2 * j + 1, cs.at[j])
        got = wires.start(cs.at[j], cr.at[j], wires.c)
        product(2 * j, q.at[j])
        got.wait_recv()
        q[j] = (q[j].astype(F32) + cr[j].astype(F32)).astype(BF16)
        if j == 3:
            waits["x1"] = wires.start(q.at[3, top], xr.at[1], wires.x)
            waits["y1"] = wires.start(q.at[3, bottom], yr.at[1], wires.y)
        if j == 1:
            waits["x0"] = wires.start(q.at[1, top], xr.at[0], wires.x)
        if j == 2:
            waits["y0"] = wires.start(q.at[2, bottom], yr.at[0], wires.y)
        yield 1
    waits["x1"].wait_recv()
    q[2, top] = (q[2, top].astype(F32) + xr[1].astype(F32)).astype(BF16)
    waits["t"] = wires.start(q.at[2, top], tr, wires.y)
    waits["y1"].wait_recv()
    q[1, bottom] = (q[1, bottom].astype(F32) + yr[1].astype(F32)).astype(BF16)
    waits["b"] = wires.start(q.at[1, bottom], br, wires.x)
    yield 1
    waits["x0"].wait_recv()
    yield 1
    waits["t"].wait_recv()
    emit(top, q[0, top].astype(F32) + xr[0].astype(F32) + tr[...].astype(F32))
    waits["y0"].wait_recv()
    waits["b"].wait_recv()
    emit(bottom, q[0, bottom].astype(F32) + yr[0].astype(F32) + br[...].astype(F32))


def reduce_scratch(n, model):
    half = n // 2
    return [
        pltpu.VMEM((4, n, model), BF16),
        pltpu.VMEM((4, n, model), BF16),
        pltpu.VMEM((4, n, model), BF16),
        pltpu.VMEM((2, half, model), BF16),
        pltpu.VMEM((2, half, model), BF16),
        pltpu.VMEM((half, model), BF16),
        pltpu.VMEM((half, model), BF16),
    ]


def middle_kernel(
    a_ref, w_ref, dout_ref, res_ref, inv_ref, gain_ref, grad0, grad2,
    dres_ref, out_ref, total0, total2,
    a, w, block, cs, cr, q, xr, yr, tr, br,
    above0, below0, stage0, above2, below2, stage2, send, recv, local,
):
    wires = Wires(send, recv, local)
    wires.hello()
    load_w = wires.local(w_ref.at[:, 0 : w.shape[1]], w)
    loads = {place: wires.local(a_ref.at[place], a.at[place]) for place in (7, 6, 3, 2, 5, 4, 1, 0)}
    wires.ready()
    rows = total0.shape[0]
    first = sum_along_z(
        wires, columns(grad0, rows, 0, total0.shape[1]), above0, below0, stage0, total0
    )
    second = sum_along_z(
        wires, columns(grad2, rows, 0, total2.shape[1]), above2, below2, stage2, total2
    )
    run(first)

    def emit(rows, total):
        inverse = inv_ref[rows, :]
        normed = res_ref[rows, :] * inverse
        e = total * gain_ref[1:2, :]
        back = inverse * (e - normed * jnp.mean(e * normed, axis=1, keepdims=True))
        dres = dout_ref[rows, :].astype(F32) + back
        dres_ref[rows, :] = dres
        block[rows, :] = dres.astype(BF16)

    load_w.wait()
    sums = reduce_phase(
        wires, a, w, cs, cr, q, xr, yr, tr, br, emit, lambda place: loads[place].wait()
    )
    for _ in range(4):
        run(sums)
    run(first)
    run(sums)
    run(sums)
    run(first)
    drain(sums)
    tokens = gather_phase(wires, block, out_ref, halved(block.shape[0], BACK_CUT))
    run(tokens)
    run(tokens)
    run(first)
    run(second)
    run(tokens)
    run(second)
    run(tokens)
    run(second)
    drain(tokens, second, first)
    wires.finish()


BACK_CUT = 208


def feed_back(dgu, w, dout, residual, inverse, gain, grad0, grad2):
    n, model = dout.shape
    k = dgu.shape[1]
    rows = 2 * model // lax.axis_size("tok")
    nz = model // rows
    half, small = grad0.shape[1], grad2.shape[1]
    return pl.pallas_call(
        middle_kernel,
        in_specs=[HBM] * 2 + [WHOLE] * 4 + [HBM] * 2,
        out_specs=[WHOLE] + [HBM] * 3,
        out_shape=[
            jax.ShapeDtypeStruct((n, model), F32),
            jax.ShapeDtypeStruct((8, n, model), BF16),
            jax.ShapeDtypeStruct((rows, half), BF16),
            jax.ShapeDtypeStruct((rows, small), BF16),
        ],
        scratch_shapes=[
            pltpu.VMEM((8, n, k), BF16),
            pltpu.VMEM((model, k), BF16),
            pltpu.VMEM((n, model), BF16),
        ]
        + reduce_scratch(n, model)
        + sum_scratch(nz, rows, half)
        + sum_scratch(nz, rows, small)
        + semaphores(),
        compiler_params=params(62, collective_id=3, has_side_effects=True),
        name="feed_back",
        **light(),
    )(dgu.reshape(8, n, k), w, dout, residual, inverse, gain, grad0, grad2)


def back_kernel(
    da_ref, w_ref, o_ref, q_ref, k_ref, v_ref, lse_ref, first_ref, cos_ref, sin_ref,
    spread_ref, squeeze_ref, final_ref, m_ref, down_ref, res_ref, grad1, sum0, sum1, sum2,
    dqkv_ref, out_ref, grad_out, total, got0, got1, got2,
    da, do, dk, dv, halo, fetched, m, w_down, cr, xr, yr, tr, br,
    above, below, stage, stage1, res, send, recv, local,
):
    wires = Wires(send, recv, local)
    nz, z = wires.nz, wires.at_z
    wires.hello()
    n, model = da.shape[1], da.shape[2]
    heads = q_ref.shape[1] // LANES
    wide = heads * HEAD_SIZE
    keys = n + WINDOW_LENGTH
    length = 8 * n
    loads = [wires.local(da_ref.at[b], da.at[b]) for b in range(8)]
    late = [
        wires.local(m_ref, m),
        wires.local(down_ref.at[:, 2 * m.shape[2] :], w_down),
    ]
    rows = total.shape[0]
    wires.ready()
    carried = sum_along_z(
        wires, columns(grad1, rows, 0, total.shape[1]), above, below, stage, total
    )
    run(carried)
    swaps = [
        swap_rows(wires, s, got) for s, got in ((sum0, got0), (sum1, got1), (sum2, got2))
    ]
    for swap in swaps:
        run(swap)
    dk[...] = jnp.zeros_like(dk)
    dv[...] = jnp.zeros_like(dv)
    for b in range(8):
        loads[b].wait()
        flat = nn(da[b], w_ref[...]).astype(BF16)
        do[b] = nn(flat, spread_ref[...]).astype(BF16)

    saves = []
    for t in range(nz):
        cols = slice(t * rows, (t + 1) * rows)
        if t >= 2:
            saves[t - 2].wait()
        total = None
        for b in range(8):
            part = tn(da[b, :, cols], o_ref[b])
            total = part if total is None else total + part
        stage1[t % 2] = total.astype(BF16)
        saves.append(wires.local(stage1.at[t % 2], grad_out.at[pl.ds(t * rows, rows)]))
    for save in saves[-2:]:
        save.wait()
    for load in late:
        load.wait()
    turns = rotation(wires, model)

    def emit(part, total):
        load = wires.local(res_ref.at[part], res)
        load.wait()
        layer = (res[...] + total).astype(BF16)
        for of, to in turns:
            out_ref[part, to] = layer[:, of]

    sums = reduce_phase(
        wires, m, w_down, da.at[pl.ds(0, 4)], cr, da.at[pl.ds(4, 4)], xr, yr, tr, br, emit
    )
    run(sums)
    run(sums)
    run(carried)
    run(sums)
    run(sums)

    def block(b, at):
        start = pl.multiple_of(b * n, n)
        span = pl.ds(start, keys)
        here = pl.ds(start, n)
        kb = k_ref[span, :]
        vb = v_ref[span, :]
        kt = kb.T
        bias = mask_bias(first_ref[:, here] - start, keys, n)
        cosine, sine = cos_ref[here, :], sin_ref[here, :]
        dqs = []
        dk_sum = dv_sum = None
        for h in range(heads):
            lanes = slice(h * LANES, (h + 1) * LANES)
            qh = q_ref[here, lanes]
            doh = do[at, :, lanes]
            p = jnp.exp2(nt(kb, qh) * (SCALE * LOG2E) + (bias - lse_ref[b, h : h + 1, :]))
            t = p * nt(vb, doh)
            inner = jnp.sum(t, axis=0, keepdims=True)
            ds = (t - p * inner).astype(BF16)
            dq = nn(kt, ds).T * SCALE
            dqs.append((dq * cosine - pltpu.roll(dq, LANES // 2, 1) * sine).astype(BF16))
            dk_h = nn(ds, qh)
            dv_h = nn(p.astype(BF16), doh)
            dk_sum = dk_h if dk_sum is None else dk_sum + dk_h
            dv_sum = dv_h if dv_sum is None else dv_sum + dv_h
        dqkv_ref[at, :, 0:wide] = nn(jnp.concatenate(dqs, 1), squeeze_ref[...]).astype(BF16)
        dk[span, :] += dk_sum
        dv[span, :] += dv_sum

    def blocks(lo, hi):
        @pl.loop(lo, hi)
        def _(b):
            block(b, wires.natural(b))

    blocks(0, 2)
    halo[:, 0:LANES] = dk[0:WINDOW_LENGTH, :].astype(BF16)
    halo[:, LANES:] = dv[0:WINDOW_LENGTH, :].astype(BF16)
    borrowed = wires.start(halo, fetched, wires.down, z >= 1, z < nz - 1)
    run(sums)
    blocks(2, 4)
    run(carried)
    blocks(4, 8)
    drain(sums)
    borrowed.wait_recv()

    @pl.when(z < nz - 1)
    def _():
        dk[length:, :] += fetched[:, 0:LANES].astype(F32)
        dv[length:, :] += fetched[:, LANES:].astype(F32)

    for b in range(8):
        here = slice(b * n, (b + 1) * n)
        there = slice(WINDOW_LENGTH + b * n, WINDOW_LENGTH + (b + 1) * n)
        dkb = dk[there, :] * SCALE
        dkb = dkb * cos_ref[here, :] - pltpu.roll(dkb, LANES // 2, 1) * sin_ref[here, :]
        both = jnp.concatenate([dkb.astype(BF16), dv[there, :].astype(BF16)], 1)
        dqkv_ref[wires.natural(b), :, wide:] = nn(both, final_ref[...]).astype(BF16)
    drain(carried, *swaps)
    wires.finish()


def attention_back(
    da_all, w_out, o, q, k_all, v_all, lse, first_key, cosine, sine, mixed, w_feed, residual, grad1,
    sums, width,
):
    _, n, model = da_all.shape
    length = 8 * n
    heads = q.shape[1] // LANES
    wide = heads * HEAD_SIZE
    spread = spread_matrix(0, heads)
    squeeze = spread_matrix(heads, 0).T
    final = spread_matrix(1, 1, rows=width - wide).T
    rows = 2 * model // lax.axis_size("tok")
    nz = model // rows
    hidden = mixed.shape[1]
    half = n // 2
    return pl.pallas_call(
        back_kernel,
        in_specs=[HBM] + [WHOLE] * 12 + [HBM] * 7,
        out_specs=[WHOLE, WHOLE] + [HBM] * 5,
        out_shape=[
            jax.ShapeDtypeStruct((8, n, width), BF16),
            jax.ShapeDtypeStruct((n, model), BF16),
            jax.ShapeDtypeStruct((model, wide), BF16),
            jax.ShapeDtypeStruct((rows, grad1.shape[1]), BF16),
        ]
        + swap_outputs(*sums),
        scratch_shapes=[
            pltpu.VMEM((8, n, model), BF16),
            pltpu.VMEM((8, n, heads * LANES), BF16),
            pltpu.VMEM(k_all.shape, F32),
            pltpu.VMEM(k_all.shape, F32),
            pltpu.VMEM((WINDOW_LENGTH, 2 * LANES), BF16),
            pltpu.VMEM((WINDOW_LENGTH, 2 * LANES), BF16),
            pltpu.VMEM((8, n, hidden), BF16),
            pltpu.VMEM((model, hidden), BF16),
            pltpu.VMEM((4, n, model), BF16),
            pltpu.VMEM((2, half, model), BF16),
            pltpu.VMEM((2, half, model), BF16),
            pltpu.VMEM((half, model), BF16),
            pltpu.VMEM((half, model), BF16),
        ]
        + sum_scratch(nz, rows, grad1.shape[1])
        + [pltpu.VMEM((2, rows, wide), BF16), pltpu.VMEM((half, model), F32)]
        + semaphores(),
        compiler_params=params(63, collective_id=6, has_side_effects=True),
        name="attention_back",
        **light(),
    )(
        da_all, w_out, o, q, k_all, v_all, lse, first_key, cosine, sine, spread, squeeze, final,
        mixed.reshape(8, n, hidden), w_feed, residual, grad1, *sums,
    )


def last_kernel(
    a_ref, w_ref, x_ref, gain_ref, dres_ref, a1_ref, grad_out, sum0,
    out_ref, total, total1, got0, got, got1,
    cs, cr, q, xr, yr, tr, br, a1, grad, above, below, stage, above1, below1, stage1,
    send, recv, local,
):
    wires = Wires(send, recv, local)
    wires.hello()
    rows = total.shape[0]
    model = a1.shape[2]
    loads = [wires.local(a1_ref.at[b], a1.at[b]) for b in range(8)]
    turns = rotation(wires, model)

    def emit(rows, total):
        x = x_ref[rows, :].astype(F32)
        inverse = lax.rsqrt(jnp.mean(x * x, axis=1, keepdims=True) + EPS)
        normed = x * inverse
        e = total * gain_ref[0:1, :]
        back = inverse * (e - normed * jnp.mean(e * normed, axis=1, keepdims=True))
        done = dres_ref[rows, :] + back
        for of, to in turns:
            out_ref[rows, to] = done[:, of]

    wires.ready()
    first = sum_along_z(
        wires, columns(grad_out, rows, 0, total1.shape[1]), above1, below1, stage1, total1
    )
    run(first)
    swap = swap_rows(wires, sum0, got0)
    run(swap)
    for load in loads:
        load.wait()
    tile = 640

    def weight_grads(lo, hi):
        @pl.loop(lo, hi)
        def _(t):
            cols = pl.ds(pl.multiple_of(t * tile, tile), tile)
            total = None
            for b in range(8):
                part = tn(a1[b, :, cols], a_ref[b])
                total = part if total is None else total + part
            grad[cols, :] = total.astype(BF16)

    weight_grads(0, 2)
    run(first)
    weight_grads(2, 4)
    carried = sum_along_z(
        wires, columns(grad, rows, 0, total.shape[1]), above, below, stage, total
    )
    run(carried)
    sums = reduce_phase(wires, a_ref, w_ref, cs, cr, q, xr, yr, tr, br, emit)
    run(sums)
    run(sums)
    run(first)
    run(sums)
    run(sums)
    run(sums)
    run(carried)
    run(first)
    run(sums)
    run(carried)
    drain(sums)
    drain(first)
    first = swap_rows(wires, total1, got1)
    run(first)
    drain(carried)
    drain(swap_rows(wires, total, got), first, swap)
    wires.finish()


def input_back(dqkv, w, inputs, gain, dres, a1, grad_out, total):
    n, model = inputs.shape
    rows = 2 * model // lax.axis_size("tok")
    nz = model // rows
    wide = dqkv.shape[2]
    return pl.pallas_call(
        last_kernel,
        in_specs=[WHOLE] * 5 + [HBM] * 3,
        out_specs=[WHOLE] + [HBM] * 5,
        out_shape=[
            jax.ShapeDtypeStruct((n, model), F32),
            jax.ShapeDtypeStruct((rows, wide), BF16),
            jax.ShapeDtypeStruct((rows, grad_out.shape[1]), BF16),
            jax.ShapeDtypeStruct((rows // 2, total.shape[1]), BF16),
            jax.ShapeDtypeStruct((rows // 2, wide), BF16),
            jax.ShapeDtypeStruct((rows // 2, grad_out.shape[1]), BF16),
        ],
        scratch_shapes=reduce_scratch(n, model)
        + [pltpu.VMEM((8, n, model), BF16), pltpu.VMEM((model, wide), BF16)]
        + sum_scratch(nz, rows, wide)
        + sum_scratch(nz, rows, grad_out.shape[1])
        + semaphores(),
        compiler_params=params(62, collective_id=4, has_side_effects=True),
        name="input_back",
        **light(),
    )(dqkv, w, inputs, gain, dres, a1, grad_out, total)


def finish_kernel(
    chunks, y_ref, *refs,
):
    count = len(chunks) + 2
    mine, got = refs[0 : 2 * count : 2], refs[1 : 2 * count : 2]
    qw, kw, vw, gw, uw, layer, dinput = refs[2 * count : 2 * count + 7]
    gate, up, down, out, query, key, value, sums, row_sums, layer_out, dinput_out, local = refs[
        2 * count + 7 :
    ]
    copies = [
        pltpu.make_async_copy(layer, layer_out, local.at[0]),
        pltpu.make_async_copy(dinput, dinput_out, local.at[1]),
    ]
    for copy in copies:
        copy.start()
    rows = gate.shape[0]
    hidden = gate.shape[1] // 2
    eye = identity(rows)
    wide = lambda v: v.astype(F32)

    def place(h, pieces):
        for (lo, hi), piece in zip(chunks, pieces):
            n = hi - lo
            at = slice(h * hidden + lo, h * hidden + hi)
            for k, ref in enumerate((gate, up, down)):
                ref[:, at] = wide(piece[:, k * n : (k + 1) * n])
        o, q = pieces[-2:]
        for ref, piece in ((out, o), (query, q)):
            n = ref.shape[1] // 2
            ref[:, h * n : (h + 1) * n] = wide(piece[:, 0:n])
        start = query.shape[1] // 2
        for ref in (key, value):
            n = ref.shape[0] // 2
            ref[h * n : (h + 1) * n, :] = tn(q[:, start : start + n], eye)
            start += n

    @pl.when(y_ref[0] == 0)
    def _():
        place(0, [ref.at[0:rows] for ref in mine])
        place(1, got)

    @pl.when(y_ref[0] == 1)
    def _():
        place(0, got)
        place(1, [ref.at[rows:] for ref in mine])

    def total(w, g, axis):
        return jnp.sum(w[...].astype(F32) * g[...], axis=axis, keepdims=True)

    sums[:, 0:1] = total(qw, query, 1)
    sums[:, 1:2] = total(gw, gate, 1) + total(uw, up, 1)
    row_sums[...] = total(kw, key, 0) + total(vw, value, 0)
    for copy in copies:
        copy.wait()


def finish(y, pieces, weights, out_columns, chunks, layer, dinput):
    query, key_t, _, gate, _ = weights
    rows, hidden = gate.shape
    f32 = lambda *shape: jax.ShapeDtypeStruct(shape, F32)
    return pl.pallas_call(
        functools.partial(finish_kernel, chunks),
        in_specs=[pl.BlockSpec(memory_space=pltpu.SMEM)]
        + [WHOLE] * (len(pieces) + len(weights) + 2),
        out_specs=[WHOLE] * 9 + [HBM] * 2,
        out_shape=[
            f32(rows, hidden), f32(rows, hidden), f32(rows, hidden), f32(rows, out_columns),
            f32(*query.shape), f32(*key_t.shape), f32(*key_t.shape), f32(rows, 2), f32(1, rows),
            jax.ShapeDtypeStruct(layer.shape, layer.dtype),
            jax.ShapeDtypeStruct(dinput.shape, dinput.dtype),
        ],
        scratch_shapes=[pltpu.SemaphoreType.DMA((2,))],
        compiler_params=params(62),
        name="finish",
        **light(),
    )(y, *pieces, *weights, layer, dinput)


def body(
    inputs,
    grad_output,
    segments,
    attention_gain,
    query_weight,
    key_matrix,
    value_matrix,
    output_weight,
    feedforward_gain,
    gate_weight,
    up_weight,
    down_weight,
):
    grid = Grid()
    bf16 = jnp.bfloat16
    model = inputs.shape[1]
    length = inputs.shape[0] * 8
    hidden = gate_weight.shape[1] // 2
    qdim = query_weight.shape[1] // 2
    kdim = key_matrix.shape[1] // 2
    cuts = []
    at = 0
    for n in FF_CHUNKS:
        cuts.append((at, at + n))
        at += n
    heads = qdim // HEAD_SIZE

    width = -(-(qdim + 2 * kdim + 2) // LANES) * LANES

    down_t = down_weight.T
    own, dout, out_pack, cosine, sine, first_key, x_all, w_attn = gather_start(
        outside_rotation(grid, inputs), outside_rotation(grid, grad_output),
        jnp.stack([attention_gain, feedforward_gain]),
        query_weight, key_matrix.T, value_matrix.T, output_weight.T,
        segments[None, :], rope_parts(length, grid.z * length, HEAD_SIZE), width,
    )
    q, k_all, v_all, o, lse, gains, a1, dout_all, w_out, w_zero, *slots = attention(
        x_all, w_attn, cosine, sine, first_key, dout, out_pack, gate_weight, up_weight, down_t,
        heads, cuts,
    )
    flat = lambda v: v.reshape(length, v.shape[-1])
    residual, inverse_two, a2, w_one = project_out(o, w_out, own, gains, slots[0])

    chunks = []
    at = 0
    for n in FF_PARTS:
        chunks.append((at, at + n))
        at += n
    mixed, dgu, w_feed, grad0, grad1, grad2, grad3, sum_0 = feed_forward(
        flat(a2), flat(dout_all), w_zero, w_one, *slots[1:], cuts, chunks
    )
    dresidual, da_all, sum_1, sum_3 = feed_back(
        dgu, w_feed, dout, residual, inverse_two, gains, grad1, grad3
    )
    dqkv, layer, grad_o, sum_2, got_0, got_1, got_3 = attention_back(
        da_all, w_out, o, q, k_all, v_all, lse, first_key, cosine, sine, mixed, w_feed, residual,
        grad2, (sum_0, sum_1, sum_3), width,
    )
    dinput, sum_q, sum_o, got_2, got_q, got_o = input_back(
        dqkv, w_attn, own, gains, dresidual, a1, grad_o, sum_2
    )
    pieces = (
        sum_0, got_0, sum_1, got_1, sum_2, got_2, sum_3, got_3, sum_o, got_o, sum_q, got_q
    )
    (
        gate_grad, up_grad, down_grad, output_grad, query_grad, key_grad, value_grad, sums,
        row_sums, layer, dinput,
    ) = finish(
        jnp.reshape(grid.y, (1,)).astype(jnp.int32),
        pieces,
        (query_weight, key_matrix.T, value_matrix.T, gate_weight, up_weight),
        output_weight.shape[0],
        chunks,
        layer,
        dinput,
    )
    sums = jnp.stack([sums[:, 0] + row_sums[0], sums[:, 1]])
    sums = sums + grid.swap(sums, C)
    sums = sums + grid.swap(sums, X)
    return (
        outside_rotation(grid, layer),
        outside_rotation(grid, dinput),
        sums[0] / attention_gain.astype(jnp.float32),
        query_grad,
        key_grad.T,
        value_grad.T,
        output_grad.T,
        sums[1] / feedforward_gain.astype(jnp.float32),
        gate_grad,
        up_grad,
        down_grad.T,
    )


def solution(mesh):
    in_specs = (
        P(("tok", "mp"), None),
        P(("tok", "mp"), None),
        P(),
        P("tok"),
        P("tok", "mp"),
        P("tok", "mp"),
        P("tok", "mp"),
        P("mp", "tok"),
        P("tok"),
        P("tok", "mp"),
        P("tok", "mp"),
        P("mp", "tok"),
    )
    out_specs = (
        P(("tok", "mp"), None),
        P(("tok", "mp"), None),
        P("tok"),
        P("tok", "mp"),
        P("tok", "mp"),
        P("tok", "mp"),
        P("mp", "tok"),
        P("tok"),
        P("tok", "mp"),
        P("tok", "mp"),
        P("mp", "tok"),
    )
    return jax.shard_map(body, mesh=mesh, in_specs=in_specs, out_specs=out_specs, check_vma=False)
```

time: 846 us -> 748 us (0.88)
  Pallas kernels: 771 us -> 734 us
  local copies, waits for them, and re-layouts: 39.2 us -> 2.65 us
  other arithmetic: 24.3 us -> 2.95 us
    pallas_call x1, Pallas kernels: 118 us -> 95.2 us  [attention(): pl.pallas_call(functools.partial(attention_kernel, hidden, cuts), in_spec...]
    pallas_call x6 -> x7, Pallas kernels: 652 us -> 639 us  [the longest x1 142 us: feed_forward(): pl.pallas_call(functools.partial(feed_kernel, hidden, cuts, chunks), in_s...]
    unnamed x84 -> x4, local copies, waits for them, and re-layouts: 11.9 us -> 0.01 us
  transfers between devices with their start and end apart: 2 -> 2, of which waited for: 0 -> 2; matrix products, arithmetic and copies ran while one was open for 1% -> 0% of each run, Pallas kernels for 0% -> 0%
where the time goes in v3:
time: 748 us; the launch traced here: 745 us
  Pallas kernels  734 us (98%)
    pallas_call x1, Pallas kernels, feed_forward(): pl.pallas_call(functools.partial(feed_kernel, hidden, cuts, chunks), in_s...  142 us
    pallas_call x1, Pallas kernels, project_out(): pl.pallas_call(project_kernel, in_specs=[WHOLE] * 5, out_specs=[WHOLE, WH...  119 us
    pallas_call x1, Pallas kernels, feed_back(): pl.pallas_call(middle_kernel, in_specs=[HBM] * 2 + [WHOLE] * 4 + [HBM] *...  118 us
    pallas_call x1, Pallas kernels, attention(): pl.pallas_call(functools.partial(attention_kernel, hidden, cuts), in_spec...  95.2 us
    pallas_call x1, Pallas kernels, input_back(): pl.pallas_call(last_kernel, in_specs=[WHOLE] * 5 + [HBM] * 3, out_specs=[...  94.9 us
    pallas_call x1, Pallas kernels, attention_back(): pl.pallas_call(back_kernel, in_specs=[HBM] + [WHOLE] * 12 + [HBM] * 7, ou...  85.9 us
    pallas_call x1, Pallas kernels, gather_start(): pl.pallas_call(start_kernel, in_specs=[WHOLE] * 9, out_specs=[WHOLE] * 6...  68.2 us
  transfers between devices with their start and end apart: 2, of which 2 were waited for; matrix products, arithmetic and copies ran while one was open for 0% of the time, Pallas kernels for 0%

profile of v3, /device:TPU:0, one launch (start us, length us, event | category | flops | bytes accessed | tf_op | source)
XLA Modules:
  0.0 745.3 jit_solution(7110497923917269711)
XLA Ops:
  0.7 0.7 stack.18
  1.4 0.7 stack.19
  2.1 0.1 pad_maximum_fusion.3
  2.2 0.1 add_convert_fusion
  2.2 0.6 pad_maximum_fusion.2.gain_ref
  2.8 0.2 multiply_cosine_fusion
  3.1 0.6 pad_maximum_fusion.rope_ref
  3.7 68.2 %gather_start.1 = (bf16[256,2560]{1,0:T(8,128)(2,1)}, bf16[256,2560]{1,0:T(8,128)(2,1)}, bf16[2,320,320]{2,1,0:T(8,128)(2,1)}, f32[2048,128]{1,0:T(8,128)}, f32[...) custom-call(bf16[256,2560]{1,0:T(8,128)(2,1)} %x_ref.1, ...), custom_call_target="tpu_custom_call" | custom-call | flops 1000000 | bytes 100000 | tf_op jit(solution)/shard_map/gather_start/pallas_call | solution.py:466
  71.9 95.2 %attention.1 = (bf16[2048,512]{1,0:T(8,128)(2,1)}, bf16[2560,128]{1,0:T(8,128)(2,1)}, bf16[2560,128]{1,0:T(8,128)(2,1)}, bf16[8,256,320]{2,1,0:T(8,128)(2,1)}, f...) custom-call(bf16[8,256,2560]{2,1,0:T(8,128)(2,1)} %get-tuple-element, ...), custom_call_target="tpu_custom_call" | custom-call | flops 1000000 | bytes 100000 | tf_op jit(solution)/shard_map/attention/pallas_call | solution.py:648
  167.1 118.7 %project_out.1 = (f32[256,2560]{1,0:T(8,128)}, f32[256,1]{1,0:T(8,128)}, bf16[8,256,2560]{2,1,0:T(8,128)(2,1)}, bf16[2560,1152]{1,0:T(8,128)(2,1)}) custom-call(bf16[8,256,320]{2,1,0:T(8,128)(2,1)} %get-tuple-element.78.a_ref.o_ref, bf16[2560,320]{1,0:T(8,128)(2,1)} %get-tuple-element.79.w_ref, bf16[256,2560]{1,0:T(8,128)(2,1)} %get-tuple-element.80.x_ref, ...), custom_call_target="tpu_custom_call" | custom-call | flops 1000000 | bytes 100000 | tf_op jit(solution)/shard_map/project_out/pallas_call | solution.py:714
  285.9 142.1 %feed_forward.1 = (bf16[2048,896]{1,0:T(8,128)(2,1)}, bf16[2048,1792]{1,0:T(8,128)(2,1)}, bf16[2560,2688]{1,0:T(8,128)(2,1)}, bf16[2560,768]{1,0:T(8,128)(2,1)},...) custom-call(bf16[2048,2560]{1,0:T(8,128)(2,1)} %bitcast.15, ...), custom_call_target="tpu_custom_call" | custom-call | flops 1000000 | bytes 100000 | tf_op jit(solution)/shard_map/feed_forward/pallas_call | solution.py:888
  428.0 118.1 %feed_back.1 = (f32[256,2560]{1,0:T(8,128)}, bf16[8,256,2560]{2,1,0:T(8,128)(2,1)}, bf16[640,768]{1,0:T(8,128)(2,1)}, bf16[640,384]{1,0:T(8,128)(2,1)}) custom-call(bf16[8,256,1792]{2,1,0:T(8,128)(2,1)} %bitcast.16, bf16[2560,2688]{1,0:T(8,128)(2,1)} %get-tuple-element.91.w_ref.down_ref, bf16[256,2560]{1,0:T(8,128)(2,1)} %get-tuple-element.76.dout_ref, ...), custom_call_target="tpu_custom_call" | custom-call | flops 1000000 | bytes 100000 | tf_op jit(solution)/shard_map/feed_back/pallas_call | solution.py:1038
  546.1 85.9 %attention_back.1 = (bf16[8,256,512]{2,1,0:T(8,128)(2,1)}, bf16[256,2560]{1,0:T(8,128)(2,1)}, bf16[2560,320]{1,0:T(8,128)(2,1)}, bf16[640,768]{1,0:T(8,128)(2,1)...) custom-call(bf16[8,256,2560]{2,1,0:T(8,128)(2,1)} %get-tuple-element.96.da_ref, ...), custom_call_target="tpu_custom_call" | custom-call | flops 1000000 | bytes 100000 | tf_op jit(solution)/shard_map/attention_back/pallas_call | solution.py:1210
  632.0 94.9 %input_back.1 = (f32[256,2560]{1,0:T(8,128)}, bf16[640,512]{1,0:T(8,128)(2,1)}, bf16[640,320]{1,0:T(8,128)(2,1)}, bf16[320,768]{1,0:T(8,128)(2,1)}, bf16[320,512]{1,0:T(8,128)(2,1)}, /*index=5*/bf16[320,320]{1,0:T(8,128)(2,1)}) custom-call(bf16[8,256,512]{2,1,0:T(8,128)(2,1)} %get-tuple-element.108.a_ref, bf16[2560,512]{1,0:T(8,128)(2,1)} %get-tuple-element.72.w_ref, ...), custom_call_target="tpu_custom_call" | custom-call | flops 1000000 | bytes 100000 | tf_op jit(solution)/shard_map/input_back/pallas_call | solution.py:1324
  727.0 0.0 copy-start
  727.0 0.0 copy-start.1
  727.0 10.6 %finish.1 = (f32[320,1792]{1,0:T(8,128)}, f32[320,1792]{1,0:T(8,128)}, f32[320,1792]{1,0:T(8,128)}, f32[320,640]{1,0:T(8,128)}, f32[320,640]{1,0:T(8,128)}, /*in...) custom-call(s32[1]{0:T(128)} %bitcast.y_ref, ...), custom_call_target="tpu_custom_call" | custom-call | flops 1000000 | bytes 100000 | tf_op jit(solution)/shard_map/finish/pallas_call | solution.py:1407
  737.6 1.2 slice_reduce_fusion.1
  738.8 0.7 reshape_add_fusion
  739.5 0.1 collective-permute-start
  739.6 1.1 collective-permute-done
  740.8 1.9 collective-permute-start.1
  742.6 1.8 collective-permute-done.1
  744.5 0.0 copy-done
  744.5 0.0 copy-done.1
  744.5 0.6 convert_divide_fusion
  (9 shorter events, 0.1 us)
Async XLA Ops:
  727.0 17.5 %copy-start = (bf16[320]{0:T(512)(128)(2,1)S(1)}, bf16[320]{0:T(512)(128)(2,1)}, u32[]{:S(2)}) copy-start(bf16[320]{0:T(512)(128)(2,1)} %param.25) | copy-start | bytes 1924
  727.0 17.5 %copy-start.1 = (bf16[320]{0:T(512)(128)(2,1)S(1)}, bf16[320]{0:T(512)(128)(2,1)}, u32[]{:S(2)}) copy-start(bf16[320]{0:T(512)(128)(2,1)} %param.20) | copy-start | bytes 1924
  739.5 1.2 collective-permute-start
  740.8 3.7 collective-permute-start.1

commit v4 on v3

--- a/solution.py
+++ b/solution.py
@@ -158,22 +158,23 @@
 class Copy:
     def __init__(self, copy, when, got, index):
         self.copy, self.when, self.got, self.index = copy, when, got, index
+        self.sent = False
 
     def wait_recv(self):
         only(self.got, self.copy.wait_recv)
 
     def wait_send(self):
-        only(self.when, self.copy.wait_send)
-
-
-SEMAPHORES = 96
+        if not self.sent:
+            only(self.when, self.copy.wait_send)
+        self.sent = True
 
 
 def semaphores():
+    nz = lax.axis_size("tok") // 2
     return [
-        pltpu.SemaphoreType.DMA((SEMAPHORES,)),
-        pltpu.SemaphoreType.DMA((SEMAPHORES,)),
-        pltpu.SemaphoreType.DMA((SEMAPHORES,)),
+        pltpu.SemaphoreType.DMA((48 + 16 * nz,)),
+        pltpu.SemaphoreType.DMA((48 + 16 * nz,)),
+        pltpu.SemaphoreType.DMA((24 + 4 * nz,)),
     ]
 
 
@@ -281,6 +282,9 @@
         down.wait_recv()
 
 
+EARLY = True
+
+
 def add_into(target, source):
     @pl.loop(0, target.shape[0] // 32)
     def _(t):
@@ -288,7 +292,7 @@
         target[part, :] = (target[part, :].astype(F32) + source[part, :].astype(F32)).astype(BF16)
 
 
-def sum_along_z(wires, p, above, below, stage, total):
+def sum_along_z(wires, p, above, below, stage, total, early=EARLY):
     nz, z = wires.nz, wires.at_z
     ups, downs = {}, {}
 
@@ -298,7 +302,8 @@
             p(nz - s), below.at[s - 1], wires.down, z == nz - 1, (z + s >= nz - 1) & (z < nz - 1)
         )
 
-    ends(1)
+    for s in range(1, nz if early else 2):
+        ends(s)
     for s in range(2, nz):
         loads = [wires.local(p(s), stage.at[0]), wires.local(p(nz - s), stage.at[1])]
         yield 1
@@ -306,7 +311,8 @@
         downs[s - 1].wait_recv()
         for load in loads:
             load.wait()
-        ends(s)
+        if not early:
+            ends(s)
         rising = (z >= 1) & (z < s) & (z < nz - 1)
         falling = (z + s >= nz) & (z < nz - 1) & (z >= 1)
         only(rising, lambda s=s: add_into(above.at[s - 2], stage.at[0]))
@@ -393,14 +399,34 @@
     return [(0, cut, "x"), (cut, n, "y")]
 
 
-def start_kernel(
-    x_ref, dout_ref, gain_ref, qw_ref, kw_ref, vw_ref, ow_ref, ids_ref, rope_ref,
-    x_own, dout_own, opack, cos_ref, sin_ref, first_ref, x_all, w_all,
-    pack, send, recv, local,
+def feed_sources(gate, up, down, cut, hidden):
+    a, b = cut
+    n = b - a
+    step = LANES
+
+    def pick(ref):
+        return lambda y: ref.at[:, pl.ds(pl.multiple_of(y * hidden + a, step), n)]
+
+    return [(pick(ref), k * n, (k + 1) * n) for k, ref in enumerate((gate, up, down))]
+
+
+def forward_kernel(
+    hidden, cuts,
+    x_ref, dout_ref, gain_in, qw_ref, kw_ref, vw_ref, ow_ref, ids_ref, rope_ref, spread_ref,
+    squeeze_ref, gate_ref, up_ref, down_ref,
+    x_own, dout_own, cos_ref, sin_ref, first_ref, q_ref, k_ref, v_ref, o_ref, lse_ref, gain_ref,
+    res_ref, inv_ref, a1_ref, dout_all, w_attn, w_out, w_zero, w_one, w_two, w_three, a2_ref,
+    pack, opack, x_all, w_flat, w_pad, w_o, bounce_out, bounce_zero, bounce_one, bounce_two,
+    bounce_three, block, cr, xr, yr, tr, br, send, recv, local,
 ):
     wires = Wires(send, recv, local)
     wires.hello()
-    model = x_ref.shape[1]
+    nz, z = wires.nz, wires.at_z
+    rows, model = x_ref.shape
+    length = 8 * rows
+    heads = q_ref.shape[1] // LANES
+    keys = rows + WINDOW_LENGTH
+
     turns = rotation(wires, model)
     at = qw_ref.shape[1] // 2
     for h in range(2):
@@ -414,27 +440,26 @@
     rest = pack.shape[2] - at
     row = lax.broadcasted_iota(jnp.int32, (2, rest), 0)
     lane = lax.broadcasted_iota(jnp.int32, (2, rest), 1)
-    tail = tn(gain_ref[...], (row == lane).astype(BF16)).astype(BF16)
+    tail = tn(gain_in[...], (row == lane).astype(BF16)).astype(BF16)
     for h in range(2):
         pack[h, :, at:] = tail
     wires.ready()
-    weights = gather_weight_rows(wires, [(lambda y: pack.at[y], 0, pack.shape[2])], w_all)
+    weights = gather_weight_rows(wires, [(lambda y: pack.at[y], 0, pack.shape[2])], w_flat)
     run(weights)
     for to, of in turns:
         x_own[:, to] = x_ref[:, of]
-    tokens = gather_phase(wires, x_own, x_all, halved(x_own.shape[0], START_CUT))
+    tokens = gather_phase(wires, x_own, x_all, halved(rows, START_CUT))
     run(tokens)
     run(weights)
     run(tokens)
     for to, of in turns:
         dout_own[:, to] = dout_ref[:, of]
-    run(tokens)
     n = ow_ref.shape[1] // 2
     for h in range(2):
         opack[h] = ow_ref[:, h * n : (h + 1) * n]
+    run(tokens)
     run(weights)
-    run(tokens)
-    length = first_ref.shape[1]
+
     lane = lax.broadcasted_iota(jnp.int32, (1, LANES), 1)
     sign = jnp.where(lane < LANES // 2, -1.0, 1.0)
     steps = length // ROPE_STEP
@@ -444,7 +469,7 @@
         cos_high, sin_high = rope_ref[0, t : t + 1, :], rope_ref[1, t : t + 1, :]
         cos_ref[part, :] = cos_high * cos_low - sin_high * sin_low
         sin_ref[part, :] = (sin_high * cos_low + cos_high * sin_low) * sign
-    offset = pl.multiple_of(wires.at_z * length, length)
+    offset = pl.multiple_of(z * length, length)
     ids = ids_ref[:, pl.ds(offset, length)]
     begin = jnp.zeros((1, length), jnp.int32)
     for number in range(1, 5):
@@ -452,92 +477,45 @@
         begin = jnp.where(ids >= number, count, begin)
     window = lax.broadcasted_iota(jnp.int32, (1, length), 1) - (WINDOW_LENGTH - 1)
     first_ref[...] = jnp.maximum(begin - offset, window) + WINDOW_LENGTH
-    drain(weights, tokens)
-    wires.finish()
-
-
-START_CUT = 160
-
-
-def gather_start(inputs, dout, gains, query, key_t, value_t, out_t, ids, rope, width):
-    n, model = inputs.shape
-    rows = query.shape[0]
-    length = 8 * n
-    return pl.pallas_call(
-        start_kernel,
-        in_specs=[WHOLE] * 9,
-        out_specs=[WHOLE] * 6 + [HBM] * 2,
-        out_shape=[
-            jax.ShapeDtypeStruct((n, model), BF16),
-            jax.ShapeDtypeStruct((n, model), BF16),
-            jax.ShapeDtypeStruct((2, rows, out_t.shape[1] // 2), BF16),
-            jax.ShapeDtypeStruct((length, LANES), F32),
-            jax.ShapeDtypeStruct((length, LANES), F32),
-            jax.ShapeDtypeStruct((1, length), jnp.int32),
-            jax.ShapeDtypeStruct((8, n, model), BF16),
-            jax.ShapeDtypeStruct((model, width), BF16),
-        ],
-        scratch_shapes=[pltpu.VMEM((2, rows, width), BF16)] + semaphores(),
-        compiler_params=params(62, collective_id=0, has_side_effects=True),
-        name="gather_start",
-        **light(),
-    )(inputs, dout, gains, query, key_t, value_t, out_t, ids, rope)
-
-
-def feed_sources(gate, up, down, cut, hidden):
-    a, b = cut
-    n = b - a
-    step = LANES
-
-    def pick(ref):
-        return lambda y: ref.at[:, pl.ds(pl.multiple_of(y * hidden + a, step), n)]
-
-    return [(pick(ref), k * n, (k + 1) * n) for k, ref in enumerate((gate, up, down))]
-
-
-def attention_kernel(
-    hidden, cuts,
-    x_ref, w_ref, spread_ref, squeeze_ref, cos_ref, sin_ref, first_ref, dout_ref,
-    opack_ref, gate_ref, up_ref, down_ref,
-    q_ref, k_ref, v_ref, o_ref, lse_ref, gain_ref, a1_ref, dout_all, w_out, w_zero, *rest,
-):
-    slots, rest = rest[: len(cuts) - 1], rest[len(cuts) - 1 :]
-    x_all, w_flat, w_pad, bounce_out, *bounces, send, recv, local = rest
-    wires = Wires(send, recv, local)
-    nz, z = wires.nz, wires.at_z
-    rows = x_all.shape[1]
-    model = x_all.shape[2]
-    heads = q_ref.shape[1] // LANES
-    keys = rows + WINDOW_LENGTH
-    length = 8 * rows
-    wires.greet()
-    load_w = wires.local(w_ref, w_flat)
-    order = (6, 7, 0, 1, 2, 3, 4, 5)
-    loads = {}
-    for b in order:
-        at = wires.natural(b)
-        loads[b] = wires.local(x_ref.at[at], x_all.at[at])
+
+    run(tokens)
+    run(weights)
     out_weights = gather_weight_rows(
-        wires, [(lambda y: opack_ref.at[y], 0, opack_ref.shape[2])], w_out, bounce_out
-    )
+        wires, [(lambda y: opack.at[y], 0, opack.shape[2])], w_out, bounce_out
+    )
+    zero_weights, one_weights = [
+        gather_weight_rows(
+            wires, feed_sources(gate_ref, up_ref, down_ref, cut, hidden), out, bounce
+        )
+        for cut, out, bounce in zip(cuts, (w_zero, w_one), (bounce_zero, bounce_one))
+    ]
+    exchanges = [
+        exchange_halves(
+            wires, feed_sources(gate_ref, up_ref, down_ref, cut, hidden), slot, bounce
+        )
+        for cut, slot, bounce in zip(cuts[2:], (w_two, w_three), (bounce_two, bounce_three))
+    ]
     run(out_weights)
+    run(zero_weights)
+    drain(tokens)
+    sent = list(wires.copies)
     quarter = rows // 4
     cotangents = gather_phase(
-        wires, dout_ref, dout_all, [(t * quarter, (t + 1) * quarter, "x") for t in range(4)]
+        wires, dout_own, dout_all, [(t * quarter, (t + 1) * quarter, "x") for t in range(4)]
     )
     run(cotangents)
-    load_w.wait()
+    drain(weights)
+    run(out_weights)
+    run(cotangents)
+    for copy in sent:
+        copy.wait_send()
+    saves = [wires.local(w_flat, w_attn)]
 
     @pl.loop(0, model // 512)
     def _(t):
         part = pl.ds(pl.multiple_of(t * 512, 512), 512)
         w_pad[part, :] = nn(w_flat[part, :], spread_ref[...]).astype(BF16)
 
-    zero_weights = gather_weight_rows(
-        wires, feed_sources(gate_ref, up_ref, down_ref, cuts[0], hidden), w_zero, bounces[0]
-    )
-    run(zero_weights)
-    run(out_weights)
     place = lax.broadcasted_iota(jnp.int32, (8, w_flat.shape[1]), 1)
     row = lax.broadcasted_iota(jnp.int32, (8, w_flat.shape[1]), 0)
     which = (place == (heads + 2) * HEAD_SIZE + row).astype(BF16)
@@ -549,18 +527,14 @@
         k_ref[0:WINDOW_LENGTH, :] = jnp.zeros((WINDOW_LENGTH, LANES), BF16)
         v_ref[0:WINDOW_LENGTH, :] = jnp.zeros((WINDOW_LENGTH, LANES), BF16)
 
-    stores = []
-    for b in order:
-        at = wires.natural(b)
-        loads[b].wait()
+    def project(b, at):
         x = x_all[at].astype(F32)
         inverse = lax.rsqrt(jnp.mean(x * x, axis=1, keepdims=True) + EPS)
         a1 = (x * inverse * gain).astype(BF16)
         x_all[at] = a1
-        stores.append(wires.local(x_all.at[at], a1_ref.at[at]))
         acc = nn(a1, w_pad[...])
-        here = slice(b * rows, (b + 1) * rows)
-        there = slice(WINDOW_LENGTH + b * rows, WINDOW_LENGTH + (b + 1) * rows)
+        here = pl.ds(pl.multiple_of(b * rows, rows), rows)
+        there = pl.ds(pl.multiple_of(WINDOW_LENGTH + b * rows, rows), rows)
         cosine, sine = cos_ref[here, :], sin_ref[here, :]
         for h in range(heads + 1):
             u = acc[:, h * LANES : (h + 1) * LANES]
@@ -570,23 +544,36 @@
             else:
                 k_ref[there, :] = turned
         v_ref[there, :] = acc[:, (heads + 1) * LANES :].astype(BF16)
-        if b == 7:
-            halo = [
-                wires.start(
-                    ref.at[pl.ds(length, WINDOW_LENGTH)], ref.at[pl.ds(0, WINDOW_LENGTH)],
-                    wires.up, z < nz - 1, z > 0,
-                )
-                for ref in (k_ref, v_ref)
-            ]
-        if b == 0:
-            run(zero_weights)
-            run(cotangents)
-        if b == 2:
-            run(out_weights)
+
+    def projected(lo, hi):
+        @pl.loop(lo, hi)
+        def _(b):
+            project(b, wires.natural(b))
+
+        for b in range(lo, hi):
+            at = wires.natural(b)
+            saves.append(wires.local(x_all.at[at], a1_ref.at[at]))
+
+    projected(6, 8)
+    halo = [
+        wires.start(
+            ref.at[pl.ds(length, WINDOW_LENGTH)], ref.at[pl.ds(0, WINDOW_LENGTH)],
+            wires.up, z < nz - 1, z > 0,
+        )
+        for ref in (k_ref, v_ref)
+    ]
+    run(zero_weights)
+    projected(0, 2)
+    run(out_weights)
+    projected(2, 6)
+    run(zero_weights)
+    run(cotangents)
+    run(cotangents)
+    run(one_weights)
     for copy in halo:
         copy.wait_recv()
 
-    def block(b, at):
+    def attend(b, at):
         start = pl.multiple_of(b * rows, rows)
         span = pl.ds(start, keys)
         here = pl.ds(start, rows)
@@ -605,127 +592,103 @@
             lse_ref[b, h : h + 1, :] = peak + jnp.log2(total)
         o_ref[at] = nn(jnp.concatenate(outs, 1), squeeze_ref[...]).astype(BF16)
 
-    def blocks(lo, hi):
+    def attended(lo, hi):
         @pl.loop(lo, hi)
         def _(b):
-            block(b, wires.natural(b))
-
-    run(zero_weights)
-    run(cotangents)
-    run(cotangents)
-    blocks(0, 2)
+            attend(b, wires.natural(b))
+
+    attended(0, 2)
     run(out_weights)
     run(cotangents)
-    blocks(2, 4)
+    attended(2, 4)
     run(cotangents)
     run(zero_weights)
-    exchanges = [
-        exchange_halves(
-            wires, feed_sources(gate_ref, up_ref, down_ref, cut, hidden), slot, bounce
-        )
-        for cut, slot, bounce in zip(cuts[1:], slots, bounces[1:])
-    ]
-    run(exchanges[0])
-    blocks(4, 6)
-    for exchange in exchanges[1:]:
+    for exchange in exchanges:
         run(exchange)
-    blocks(6, 8)
-    for store in stores:
-        store.wait()
-    drain(out_weights, zero_weights, cotangents, *exchanges)
+    attended(4, 6)
+    drain(out_weights)
+    load_o = wires.local(w_out, w_o)
+    run(one_weights)
+    attended(6, 8)
+    load_o.wait()
+    for save in saves:
+        save.wait()
+
+    def emit(part, total):
+        residual = x_own[part, :].astype(F32) + total
+        inverse = lax.rsqrt(jnp.mean(residual * residual, axis=1, keepdims=True) + EPS)
+        res_ref[part, :] = residual
+        inv_ref[part, :] = inverse
+        block[part, :] = (residual * inverse * gain_ref[1:2, :]).astype(BF16)
+
+    sums = reduce_phase(
+        wires, o_ref, w_o, x_all.at[pl.ds(0, 4)], cr, x_all.at[pl.ds(4, 4)], xr, yr, tr, br, emit
+    )
+    for _ in range(4):
+        run(sums)
+    drain(zero_weights, cotangents)
+    run(sums)
+    run(one_weights)
+    drain(sums)
+    normed = gather_phase(wires, block, a2_ref, halved(rows))
+    run(normed)
+    run(normed)
+    run(normed)
+    run(one_weights)
+    drain(normed, one_weights, *exchanges)
     wires.finish()
 
 
-def attention(x_all, w_attn, cosine, sine, first_key, dout, opack, gate, up, down, heads, cuts):
-    _, n, model = x_all.shape
+START_CUT = 160
+
+
+def attention_forward(
+    inputs, dout, gains, query, key_t, value_t, out_t, ids, rope, gate, up, down_t, width, cuts
+):
+    n, model = inputs.shape
+    rows = query.shape[0]
     length = 8 * n
+    heads = query.shape[1] // 2 // HEAD_SIZE
     hidden = gate.shape[1] // 2
     wide = heads * LANES
-    spread = spread_matrix(heads + 1, 1, rows=w_attn.shape[1])
+    flat = heads * HEAD_SIZE
+    half = n // 2
+    spread = spread_matrix(heads + 1, 1, rows=width)
     squeeze = spread_matrix(0, heads).T
-    slot = 2 * gate.shape[0]
     sizes = [3 * (b - a) for a, b in cuts]
+    b16 = lambda *shape: jax.ShapeDtypeStruct(shape, BF16)
+    f32 = lambda *shape: jax.ShapeDtypeStruct(shape, F32)
+    v16 = lambda *shape: pltpu.VMEM(shape, BF16)
     return pl.pallas_call(
-        functools.partial(attention_kernel, hidden, cuts),
-        in_specs=[HBM, HBM] + [WHOLE] * 6 + [HBM] * 4,
-        out_specs=[WHOLE] * 6 + [HBM] * (3 + len(cuts)),
+        functools.partial(forward_kernel, hidden, cuts),
+        in_specs=[WHOLE] * 11 + [HBM] * 3,
+        out_specs=[WHOLE] * 13 + [HBM] * 9,
         out_shape=[
-            jax.ShapeDtypeStruct((length, wide), BF16),
-            jax.ShapeDtypeStruct((length + WINDOW_LENGTH, LANES), BF16),
-            jax.ShapeDtypeStruct((length + WINDOW_LENGTH, LANES), BF16),
-            jax.ShapeDtypeStruct((8, n, heads * HEAD_SIZE), BF16),
-            jax.ShapeDtypeStruct((8, heads, n), F32),
-            jax.ShapeDtypeStruct((8, model), F32),
-            jax.ShapeDtypeStruct((8, n, model), BF16),
-            jax.ShapeDtypeStruct((8, n, model), BF16),
-            jax.ShapeDtypeStruct((model, opack.shape[2]), BF16),
-            jax.ShapeDtypeStruct((model, sizes[0]), BF16),
+            b16(n, model), b16(n, model), f32(length, LANES), f32(length, LANES),
+            jax.ShapeDtypeStruct((1, length), jnp.int32), b16(length, wide),
+            b16(length + WINDOW_LENGTH, LANES), b16(length + WINDOW_LENGTH, LANES),
+            b16(8, n, flat), f32(8, heads, n), f32(8, model), f32(n, model), f32(n, 1),
+            b16(8, n, model), b16(8, n, model), b16(model, width), b16(model, flat),
+            b16(model, sizes[0]), b16(model, sizes[1]), b16(2 * rows, sizes[2]),
+            b16(2 * rows, sizes[3]), b16(8, n, model),
+        ],
+        scratch_shapes=[
+            v16(2, rows, width), v16(2, rows, flat), v16(8, n, model), v16(model, width),
+            v16(model, spread.shape[1]), v16(model, flat), v16(rows, flat),
         ]
-        + [jax.ShapeDtypeStruct((slot, size), BF16) for size in sizes[1:]],
-        scratch_shapes=[
-            pltpu.VMEM((8, n, model), BF16),
-            pltpu.VMEM(w_attn.shape, BF16),
-            pltpu.VMEM((model, spread.shape[1]), BF16),
-            pltpu.VMEM(opack.shape[1:], BF16),
+        + [v16(rows, size) for size in sizes]
+        + [
+            v16(n, model), v16(4, n, model), v16(2, half, model), v16(2, half, model),
+            v16(half, model), v16(half, model),
         ]
-        + [pltpu.VMEM((gate.shape[0], size), BF16) for size in sizes]
         + semaphores(),
-        compiler_params=params(62, collective_id=5, has_side_effects=True),
-        name="attention",
+        compiler_params=params(62, collective_id=0, has_side_effects=True),
+        name="attention_forward",
         **light(),
-    )(x_all, w_attn, spread, squeeze, cosine, sine, first_key, dout, opack, gate, up, down)
-
-
-def project_kernel(
-    a_ref, w_ref, x_ref, gain_ref, slot_ref, res_ref, inv_ref, out_ref, w_all,
-    block, cs, cr, q, xr, yr, tr, br, send, recv, local,
-):
-    wires = Wires(send, recv, local)
-    wires.greet()
-    n = slot_ref.shape[0]
-    own = wires.local(slot_ref, w_all.at[pl.ds(0, n)])
-    weights = along_z(wires, slot_ref, lambda s: w_all.at[pl.ds(s * n, n)])
-    run(weights)
-
-    def emit(rows, total):
-        residual = x_ref[rows, :].astype(F32) + total
-        inverse = lax.rsqrt(jnp.mean(residual * residual, axis=1, keepdims=True) + EPS)
-        res_ref[rows, :] = residual
-        inv_ref[rows, :] = inverse
-        block[rows, :] = (residual * inverse * gain_ref[1:2, :]).astype(BF16)
-
-    sums = reduce_phase(wires, a_ref, w_ref, cs, cr, q, xr, yr, tr, br, emit)
-    for _ in range(6):
-        run(sums)
-    run(weights)
-    drain(sums)
-    tokens = gather_phase(wires, block, out_ref, halved(block.shape[0]))
-    run(tokens)
-    run(tokens)
-    run(tokens)
-    run(weights)
-    drain(tokens, weights)
-    own.wait()
-    wires.finish()
-
-
-def project_out(o, w_out, inputs, gain, slot):
-    n, model = inputs.shape
-    return pl.pallas_call(
-        project_kernel,
-        in_specs=[WHOLE] * 5,
-        out_specs=[WHOLE, WHOLE, HBM, HBM],
-        out_shape=[
-            jax.ShapeDtypeStruct((n, model), F32),
-            jax.ShapeDtypeStruct((n, 1), F32),
-            jax.ShapeDtypeStruct((8, n, model), BF16),
-            jax.ShapeDtypeStruct((model, slot.shape[1]), BF16),
-        ],
-        scratch_shapes=[pltpu.VMEM((n, model), BF16)] + reduce_scratch(n, model) + semaphores(),
-        compiler_params=params(62, collective_id=2, has_side_effects=True),
-        name="project_out",
-        **light(),
-    )(o, w_out, inputs, gain, slot)
+    )(
+        inputs, dout, gains, query, key_t, value_t, out_t, ids, rope, spread, squeeze, gate, up,
+        down_t,
+    )
 
 
 def feed_kernel(
@@ -821,7 +784,7 @@
             return pltpu.make_async_copy(
                 stage.at[t % 2, :, 0 : 3 * n],
                 out.at[pl.ds(pl.multiple_of(t * tile, tile), tile)],
-                local.at[SEMAPHORES - 1 - t % 2],
+                local.at[24 + 4 * nz - 1 - t % 2],
             )
 
         @pl.loop(*tiles)
@@ -850,28 +813,27 @@
     run(later[0])
     weight_grads(*chunks[0], grad0, (2, last))
     sums = sum_along_z(
-        wires, columns(grad0, slot, 0, total.shape[1]), above, below, extra, total
+        wires, columns(grad0, slot, 0, total.shape[1]), above, below, extra, total, False
     )
     run(sums)
     units(*chunks[1], (0, 8))
     run(later[0])
     weight_grads(*chunks[1], grad1, (0, 4))
-    run(sums)
     run(later[1])
     weight_grads(*chunks[1], grad1, (4, last))
     drain(later[0])
+    run(sums)
     units(*chunks[2], (0, 4))
     run(later[1])
-    run(sums)
     units(*chunks[2], (4, 8))
     weight_grads(*chunks[2], grad2, (0, 2))
     run(later[1])
     weight_grads(*chunks[2], grad2, (2, last))
     drain(later[1])
+    run(sums)
     outs = [wires.local(w, w_ref)]
     units(*chunks[3], (0, 8))
     outs += [wires.local(m, m_ref), wires.local(g, g_ref)]
-    run(sums)
     weight_grads(*chunks[3], grad3)
     drain(sums)
     for copy in outs:
@@ -989,7 +951,7 @@
         wires, columns(grad0, rows, 0, total0.shape[1]), above0, below0, stage0, total0
     )
     second = sum_along_z(
-        wires, columns(grad2, rows, 0, total2.shape[1]), above2, below2, stage2, total2
+        wires, columns(grad2, rows, 0, total2.shape[1]), above2, below2, stage2, total2, False
     )
     run(first)
 
@@ -1012,8 +974,9 @@
     run(sums)
     run(sums)
     run(first)
+    run(second)
     drain(sums)
-    tokens = gather_phase(wires, block, out_ref, halved(block.shape[0], BACK_CUT))
+    tokens = gather_phase(wires, block, out_ref, halved(block.shape[0]))
     run(tokens)
     run(tokens)
     run(first)
@@ -1021,12 +984,8 @@
     run(tokens)
     run(second)
     run(tokens)
-    run(second)
-    drain(tokens, second, first)
+    drain(second, tokens, first)
     wires.finish()
-
-
-BACK_CUT = 208
 
 
 def feed_back(dgu, w, dout, residual, inverse, gain, grad0, grad2):
@@ -1452,19 +1411,17 @@
 
     width = -(-(qdim + 2 * kdim + 2) // LANES) * LANES
 
-    down_t = down_weight.T
-    own, dout, out_pack, cosine, sine, first_key, x_all, w_attn = gather_start(
+    (
+        own, dout, cosine, sine, first_key, q, k_all, v_all, o, lse, gains, residual, inverse_two,
+        a1, dout_all, w_attn, w_out, w_zero, w_one, w_two, w_three, a2,
+    ) = attention_forward(
         outside_rotation(grid, inputs), outside_rotation(grid, grad_output),
         jnp.stack([attention_gain, feedforward_gain]),
         query_weight, key_matrix.T, value_matrix.T, output_weight.T,
-        segments[None, :], rope_parts(length, grid.z * length, HEAD_SIZE), width,
-    )
-    q, k_all, v_all, o, lse, gains, a1, dout_all, w_out, w_zero, *slots = attention(
-        x_all, w_attn, cosine, sine, first_key, dout, out_pack, gate_weight, up_weight, down_t,
-        heads, cuts,
+        segments[None, :], rope_parts(length, grid.z * length, HEAD_SIZE),
+        gate_weight, up_weight, down_weight.T, width, cuts,
     )
     flat = lambda v: v.reshape(length, v.shape[-1])
-    residual, inverse_two, a2, w_one = project_out(o, w_out, own, gains, slots[0])
 
     chunks = []
     at = 0
@@ -1472,7 +1429,7 @@
         chunks.append((at, at + n))
         at += n
     mixed, dgu, w_feed, grad0, grad1, grad2, grad3, sum_0 = feed_forward(
-        flat(a2), flat(dout_all), w_zero, w_one, *slots[1:], cuts, chunks
+        flat(a2), flat(dout_all), w_zero, w_one, w_two, w_three, cuts, chunks
     )
     dresidual, da_all, sum_1, sum_3 = feed_back(
         dgu, w_feed, dout, residual, inverse_two, gains, grad1, grad3

time: 748 us -> 682 us (0.912)
  Pallas kernels: 734 us -> 668 us
    pallas_call x3 -> x1, Pallas kernels: 282 us -> 232 us  [attention_forward(): pl.pallas_call(functools.partial(forward_kernel, hidden, cuts), in_specs=...]
    pallas_call x1, Pallas kernels: 118 us -> 110 us  [feed_back(): pl.pallas_call(middle_kernel, in_specs=[HBM] * 2 + [WHOLE] * 4 + [HBM] *...]
where the time goes in v4:
time: 682 us; the launch traced here: 680 us
  Pallas kernels  668 us (98%)
    pallas_call x1, Pallas kernels, attention_forward(): pl.pallas_call(functools.partial(forward_kernel, hidden, cuts), in_specs=...  232 us
    pallas_call x1, Pallas kernels, feed_forward(): pl.pallas_call(functools.partial(feed_kernel, hidden, cuts, chunks), in_s...  136 us
    pallas_call x1, Pallas kernels, feed_back(): pl.pallas_call(middle_kernel, in_specs=[HBM] * 2 + [WHOLE] * 4 + [HBM] *...  110 us
    pallas_call x1, Pallas kernels, input_back(): pl.pallas_call(last_kernel, in_specs=[WHOLE] * 5 + [HBM] * 3, out_specs=[...  94.6 us
    pallas_call x1, Pallas kernels, attention_back(): pl.pallas_call(back_kernel, in_specs=[HBM] + [WHOLE] * 12 + [HBM] * 7, ou...  85.6 us
  transfers between devices with their start and end apart: 2, of which 2 were waited for; matrix products, arithmetic and copies ran while one was open for 0% of the time, Pallas kernels for 0%

profile of v4, /device:TPU:0, one launch (start us, length us, event | category | flops | bytes accessed | tf_op | source)
XLA Modules:
  0.0 679.7 jit_solution(10772651918399528270)
XLA Ops:
  0.7 0.7 stack.18
  1.4 0.7 stack.19
  2.1 0.1 pad_maximum_fusion.3
  2.2 0.1 add_convert_fusion
  2.2 0.6 pad_maximum_fusion.2.gain_in
  2.8 0.2 multiply_cosine_fusion
  3.1 0.6 pad_maximum_fusion.rope_ref
  3.7 231.8 %attention_forward.1 = (bf16[256,2560]{1,0:T(8,128)(2,1)}, bf16[256,2560]{1,0:T(8,128)(2,1)}, f32[2048,128]{1,0:T(8,128)}, f32[2048,128]{1,0:T(8,128)}, s32[1,20...) custom-call(bf16[256,2560]{1,0:T(8,128)(2,1)} %x_ref.1, ...), custom_call_target="tpu_custom_call" | custom-call | flops 1000000 | bytes 100000 | tf_op jit(solution)/shard_map/attention_forward/pallas_call | solution.py:662
  235.5 135.9 %feed_forward.1 = (bf16[2048,896]{1,0:T(8,128)(2,1)}, bf16[2048,1792]{1,0:T(8,128)(2,1)}, bf16[2560,2688]{1,0:T(8,128)(2,1)}, bf16[2560,768]{1,0:T(8,128)(2,1)},...) custom-call(bf16[2048,2560]{1,0:T(8,128)(2,1)} %bitcast.15, ...), custom_call_target="tpu_custom_call" | custom-call | flops 1000000 | bytes 100000 | tf_op jit(solution)/shard_map/feed_forward/pallas_call | solution.py:850
  371.4 109.7 %feed_back.1 = (f32[256,2560]{1,0:T(8,128)}, bf16[8,256,2560]{2,1,0:T(8,128)(2,1)}, bf16[640,768]{1,0:T(8,128)(2,1)}, bf16[640,384]{1,0:T(8,128)(2,1)}) custom-call(bf16[8,256,1792]{2,1,0:T(8,128)(2,1)} %bitcast.16, bf16[2560,2688]{1,0:T(8,128)(2,1)} %get-tuple-element.76.w_ref.down_ref, bf16[256,2560]{1,0:T(8,128)(2,1)} %get-tuple-element.77.dout_ref, ...), custom_call_target="tpu_custom_call" | custom-call | flops 1000000 | bytes 100000 | tf_op jit(solution)/shard_map/feed_back/pallas_call | solution.py:997
  481.1 85.6 %attention_back.1 = (bf16[8,256,512]{2,1,0:T(8,128)(2,1)}, bf16[256,2560]{1,0:T(8,128)(2,1)}, bf16[2560,320]{1,0:T(8,128)(2,1)}, bf16[640,768]{1,0:T(8,128)(2,1)...) custom-call(bf16[8,256,2560]{2,1,0:T(8,128)(2,1)} %get-tuple-element.83.da_ref, ...), custom_call_target="tpu_custom_call" | custom-call | flops 1000000 | bytes 100000 | tf_op jit(solution)/shard_map/attention_back/pallas_call | solution.py:1169
  566.7 94.6 %input_back.1 = (f32[256,2560]{1,0:T(8,128)}, bf16[640,512]{1,0:T(8,128)(2,1)}, bf16[640,320]{1,0:T(8,128)(2,1)}, bf16[320,768]{1,0:T(8,128)(2,1)}, bf16[320,512]{1,0:T(8,128)(2,1)}, /*index=5*/bf16[320,320]{1,0:T(8,128)(2,1)}) custom-call(bf16[8,256,512]{2,1,0:T(8,128)(2,1)} %get-tuple-element.100.a_ref, bf16[2560,512]{1,0:T(8,128)(2,1)} %get-tuple-element.101.w_ref, ...), custom_call_target="tpu_custom_call" | custom-call | flops 1000000 | bytes 100000 | tf_op jit(solution)/shard_map/input_back/pallas_call | solution.py:1283
  661.3 0.0 copy-start
  661.3 0.0 copy-start.1
  661.3 10.6 %finish.1 = (f32[320,1792]{1,0:T(8,128)}, f32[320,1792]{1,0:T(8,128)}, f32[320,1792]{1,0:T(8,128)}, f32[320,640]{1,0:T(8,128)}, f32[320,640]{1,0:T(8,128)}, /*in...) custom-call(s32[1]{0:T(128)} %bitcast.y_ref, ...), custom_call_target="tpu_custom_call" | custom-call | flops 1000000 | bytes 100000 | tf_op jit(solution)/shard_map/finish/pallas_call | solution.py:1366
  671.9 1.2 slice_reduce_fusion.1
  673.2 0.7 reshape_add_fusion
  673.9 0.1 collective-permute-start
  673.9 1.1 collective-permute-done
  675.1 1.9 collective-permute-start.1
  677.0 1.8 collective-permute-done.1
  678.8 0.0 copy-done
  678.8 0.0 copy-done.1
  678.8 0.6 convert_divide_fusion
  (9 shorter events, 0.1 us)
Async XLA Ops:
  661.3 17.5 %copy-start = (bf16[320]{0:T(512)(128)(2,1)S(1)}, bf16[320]{0:T(512)(128)(2,1)}, u32[]{:S(2)}) copy-start(bf16[320]{0:T(512)(128)(2,1)} %param.25) | copy-start | bytes 1924
  661.3 17.5 %copy-start.1 = (bf16[320]{0:T(512)(128)(2,1)S(1)}, bf16[320]{0:T(512)(128)(2,1)}, u32[]{:S(2)}) copy-start(bf16[320]{0:T(512)(128)(2,1)} %param.20) | copy-start | bytes 1924
  673.9 1.2 collective-permute-start
  675.1 3.7 collective-permute-start.1

commit v5 on v4

--- a/solution.py
+++ b/solution.py
@@ -286,9 +286,11 @@
 
 
 def add_into(target, source):
-    @pl.loop(0, target.shape[0] // 32)
+    step = 32 if target.shape[0] % 32 == 0 else 16
+
+    @pl.loop(0, target.shape[0] // step)
     def _(t):
-        part = pl.ds(pl.multiple_of(t * 32, 32), 32)
+        part = pl.ds(pl.multiple_of(t * step, step), step)
         target[part, :] = (target[part, :].astype(F32) + source[part, :].astype(F32)).astype(BF16)
 
 
@@ -326,9 +328,10 @@
     load.wait()
     only(z >= 1, lambda: add_into(stage.at[0], above.at[nz - 2]))
     only(z < nz - 1, lambda: add_into(stage.at[0], below.at[nz - 2]))
-    kept = wires.local(stage.at[0], total)
-    yield 1
-    kept.wait()
+    if total is not None:
+        kept = wires.local(stage.at[0], total)
+        yield 1
+        kept.wait()
 
 
 def swap_rows(wires, total, got):
@@ -360,6 +363,31 @@
     slot = lambda s: out.at[pl.ds(s * n, n)]
     yield from exchange_halves(wires, sources, slot(0), bounce)
     yield from along_z(wires, slot(0), slot)
+
+
+def gather_pack_rows(wires, pack, out):
+    n = out.shape[0] // (2 * wires.nz)
+    y = wires.at_y
+
+    def slot(s, side):
+        return out.at[pl.ds(pl.multiple_of((2 * s + side) * n, n), n)]
+
+    mine = pack.at[y]
+    arrival = wires.start(pack.at[1 - y], slot(0, y), wires.y)
+    kept = wires.local(mine, slot(0, y))
+    own = along_z(wires, mine, lambda s: slot(s, y))
+    run(own)
+    yield 1
+    arrival.wait_recv()
+    other = along_z(wires, slot(0, 1 - y), lambda s: slot(s, 1 - y))
+    run(other)
+    yield 1
+    for _ in range(1, wires.nz):
+        run(own)
+        yield 1
+        run(other)
+        yield 1
+    kept.wait()
 
 
 def gather_phase(wires, block, out, parts):
@@ -416,7 +444,7 @@
     squeeze_ref, gate_ref, up_ref, down_ref,
     x_own, dout_own, cos_ref, sin_ref, first_ref, q_ref, k_ref, v_ref, o_ref, lse_ref, gain_ref,
     res_ref, inv_ref, a1_ref, dout_all, w_attn, w_out, w_zero, w_one, w_two, w_three, a2_ref,
-    pack, opack, x_all, w_flat, w_pad, w_o, bounce_out, bounce_zero, bounce_one, bounce_two,
+    pack, opack, x_all, w_flat, w_pad, w_o, o_slots, o_other, bounce_zero, bounce_one, bounce_two,
     bounce_three, block, cr, xr, yr, tr, br, send, recv, local,
 ):
     wires = Wires(send, recv, local)
@@ -444,7 +472,7 @@
     for h in range(2):
         pack[h, :, at:] = tail
     wires.ready()
-    weights = gather_weight_rows(wires, [(lambda y: pack.at[y], 0, pack.shape[2])], w_flat)
+    weights = gather_pack_rows(wires, pack, w_flat)
     run(weights)
     for to, of in turns:
         x_own[:, to] = x_ref[:, of]
@@ -452,11 +480,13 @@
     run(tokens)
     run(weights)
     run(tokens)
+    run(weights)
     for to, of in turns:
         dout_own[:, to] = dout_ref[:, of]
     n = ow_ref.shape[1] // 2
     for h in range(2):
         opack[h] = ow_ref[:, h * n : (h + 1) * n]
+    run(weights)
     run(tokens)
     run(weights)
 
@@ -478,11 +508,24 @@
     window = lax.broadcasted_iota(jnp.int32, (1, length), 1) - (WINDOW_LENGTH - 1)
     first_ref[...] = jnp.maximum(begin - offset, window) + WINDOW_LENGTH
 
+    run(weights)
     run(tokens)
     run(weights)
-    out_weights = gather_weight_rows(
-        wires, [(lambda y: opack.at[y], 0, opack.shape[2])], w_out, bounce_out
-    )
+    def gather_out():
+        y, flat = wires.at_y, opack.shape[2]
+        arrival = wires.start(opack.at[1 - y], o_other, wires.y)
+        yield 1
+        arrival.wait_recv()
+        o_slots[0, :, 0:flat] = opack[y]
+        o_slots[0, :, flat:] = o_other[...]
+        yield from along_z(wires, o_slots.at[0], lambda s: o_slots.at[s])
+        n = opack.shape[1]
+        for s in range(nz):
+            for k, side in enumerate((y, 1 - y)):
+                part = pl.ds(pl.multiple_of((2 * s + side) * n, n), n)
+                w_o[part, :] = o_slots[s, :, k * flat : (k + 1) * flat]
+
+    out_weights = gather_out()
     zero_weights, one_weights = [
         gather_weight_rows(
             wires, feed_sources(gate_ref, up_ref, down_ref, cut, hidden), out, bounce
@@ -497,14 +540,13 @@
     ]
     run(out_weights)
     run(zero_weights)
-    drain(tokens)
+    drain(tokens, weights)
     sent = list(wires.copies)
     quarter = rows // 4
     cotangents = gather_phase(
         wires, dout_own, dout_all, [(t * quarter, (t + 1) * quarter, "x") for t in range(4)]
     )
     run(cotangents)
-    drain(weights)
     run(out_weights)
     run(cotangents)
     for copy in sent:
@@ -607,10 +649,9 @@
         run(exchange)
     attended(4, 6)
     drain(out_weights)
-    load_o = wires.local(w_out, w_o)
+    saves.append(wires.local(w_o, w_out))
     run(one_weights)
     attended(6, 8)
-    load_o.wait()
     for save in saves:
         save.wait()
 
@@ -630,16 +671,17 @@
     run(sums)
     run(one_weights)
     drain(sums)
-    normed = gather_phase(wires, block, a2_ref, halved(rows))
-    run(normed)
+    normed = gather_phase(wires, block, a2_ref, halved(rows, NORMED_CUT))
     run(normed)
     run(normed)
     run(one_weights)
+    run(normed)
     drain(normed, one_weights, *exchanges)
     wires.finish()
 
 
 START_CUT = 160
+NORMED_CUT = 128
 
 
 def attention_forward(
@@ -674,7 +716,8 @@
         ],
         scratch_shapes=[
             v16(2, rows, width), v16(2, rows, flat), v16(8, n, model), v16(model, width),
-            v16(model, spread.shape[1]), v16(model, flat), v16(rows, flat),
+            v16(model, spread.shape[1]), v16(model, flat),
+            v16(model // (2 * rows), rows, 2 * flat), v16(rows, flat),
         ]
         + [v16(rows, size) for size in sizes]
         + [
@@ -828,9 +871,9 @@
     units(*chunks[2], (4, 8))
     weight_grads(*chunks[2], grad2, (0, 2))
     run(later[1])
+    run(sums)
     weight_grads(*chunks[2], grad2, (2, last))
     drain(later[1])
-    run(sums)
     outs = [wires.local(w, w_ref)]
     units(*chunks[3], (0, 8))
     outs += [wires.local(m, m_ref), wires.local(g, g_ref)]
@@ -1066,8 +1109,11 @@
         for b in range(8):
             part = tn(da[b, :, cols], o_ref[b])
             total = part if total is None else total + part
-        stage1[t % 2] = total.astype(BF16)
-        saves.append(wires.local(stage1.at[t % 2], grad_out.at[pl.ds(t * rows, rows)]))
+        half = rows // 2
+        for h in range(2):
+            part = total[h * half : (h + 1) * half].astype(BF16)
+            stage1[t % 2, :, h * wide : (h + 1) * wide] = part
+        saves.append(wires.local(stage1.at[t % 2], grad_out.at[pl.ds(t * half, half)]))
     for save in saves[-2:]:
         save.wait()
     for load in late:
@@ -1173,7 +1219,7 @@
         out_shape=[
             jax.ShapeDtypeStruct((8, n, width), BF16),
             jax.ShapeDtypeStruct((n, model), BF16),
-            jax.ShapeDtypeStruct((model, wide), BF16),
+            jax.ShapeDtypeStruct((model // 2, 2 * wide), BF16),
             jax.ShapeDtypeStruct((rows, grad1.shape[1]), BF16),
         ]
         + swap_outputs(*sums),
@@ -1193,7 +1239,7 @@
             pltpu.VMEM((half, model), BF16),
         ]
         + sum_scratch(nz, rows, grad1.shape[1])
-        + [pltpu.VMEM((2, rows, wide), BF16), pltpu.VMEM((half, model), F32)]
+        + [pltpu.VMEM((2, rows // 2, 2 * wide), BF16), pltpu.VMEM((half, model), F32)]
         + semaphores(),
         compiler_params=params(63, collective_id=6, has_side_effects=True),
         name="attention_back",
@@ -1207,7 +1253,7 @@
 def last_kernel(
     a_ref, w_ref, x_ref, gain_ref, dres_ref, a1_ref, grad_out, sum0,
     out_ref, total, total1, got0, got, got1,
-    cs, cr, q, xr, yr, tr, br, a1, grad, above, below, stage, above1, below1, stage1,
+    cs, cr, q, xr, yr, tr, br, a1, grad, above, below, stage, above1, below1, stage1, o_rows,
     send, recv, local,
 ):
     wires = Wires(send, recv, local)
@@ -1229,7 +1275,7 @@
 
     wires.ready()
     first = sum_along_z(
-        wires, columns(grad_out, rows, 0, total1.shape[1]), above1, below1, stage1, total1
+        wires, columns(grad_out, rows // 2, 0, grad_out.shape[1]), above1, below1, stage1, None
     )
     run(first)
     swap = swap_rows(wires, sum0, got0)
@@ -1268,10 +1314,16 @@
     run(carried)
     drain(sums)
     drain(first)
-    first = swap_rows(wires, total1, got1)
-    run(first)
+    half, wide = o_rows.shape[1:]
+    for h in range(2):
+        o_rows[h] = stage1[0, :, h * wide : (h + 1) * wide]
+    keep = wires.local(o_rows.at[0], total1.at[0:half]), wires.local(o_rows.at[1], total1.at[half:])
+    sent = wires.start(o_rows.at[1 - wires.at_y], got1, wires.y)
     drain(carried)
-    drain(swap_rows(wires, total, got), first, swap)
+    drain(swap_rows(wires, total, got), swap)
+    sent.wait_recv()
+    for copy in keep:
+        copy.wait()
     wires.finish()
 
 
@@ -1287,15 +1339,16 @@
         out_shape=[
             jax.ShapeDtypeStruct((n, model), F32),
             jax.ShapeDtypeStruct((rows, wide), BF16),
-            jax.ShapeDtypeStruct((rows, grad_out.shape[1]), BF16),
+            jax.ShapeDtypeStruct((rows, grad_out.shape[1] // 2), BF16),
             jax.ShapeDtypeStruct((rows // 2, total.shape[1]), BF16),
             jax.ShapeDtypeStruct((rows // 2, wide), BF16),
-            jax.ShapeDtypeStruct((rows // 2, grad_out.shape[1]), BF16),
+            jax.ShapeDtypeStruct((rows // 2, grad_out.shape[1] // 2), BF16),
         ],
         scratch_shapes=reduce_scratch(n, model)
         + [pltpu.VMEM((8, n, model), BF16), pltpu.VMEM((model, wide), BF16)]
         + sum_scratch(nz, rows, wide)
-        + sum_scratch(nz, rows, grad_out.shape[1])
+        + sum_scratch(nz, rows // 2, grad_out.shape[1])
+        + [pltpu.VMEM((2, rows // 2, grad_out.shape[1] // 2), BF16)]
         + semaphores(),
         compiler_params=params(62, collective_id=4, has_side_effects=True),
         name="input_back",
@@ -1457,8 +1510,7 @@
         dinput,
     )
     sums = jnp.stack([sums[:, 0] + row_sums[0], sums[:, 1]])
-    sums = sums + grid.swap(sums, C)
-    sums = sums + grid.swap(sums, X)
+    sums = (sums + grid.swap(sums, C)) + (grid.swap(sums, X) + grid.swap(sums, X | C))
     return (
         outside_rotation(grid, layer),
         outside_rotation(grid, dinput),

time: 682 us -> 667 us (0.978)
  Pallas kernels: 668 us -> 653 us
  transfers between devices with their start and end apart: 2 -> 3, of which waited for: 2 -> 2; matrix products, arithmetic and copies ran while one was open for 0% -> 0% of each run, Pallas kernels for 0% -> 0%
where the time goes in v5:
time: 667 us; the launch traced here: 665 us
  Pallas kernels  653 us (98%)
    pallas_call x1, Pallas kernels, attention_forward(): pl.pallas_call(functools.partial(forward_kernel, hidden, cuts), in_specs=...  228 us
    pallas_call x1, Pallas kernels, feed_forward(): pl.pallas_call(functools.partial(feed_kernel, hidden, cuts, chunks), in_s...  132 us
    pallas_call x1, Pallas kernels, feed_back(): pl.pallas_call(middle_kernel, in_specs=[HBM] * 2 + [WHOLE] * 4 + [HBM] *...  109 us
    pallas_call x1, Pallas kernels, input_back(): pl.pallas_call(last_kernel, in_specs=[WHOLE] * 5 + [HBM] * 3, out_specs=[...  88.7 us
    pallas_call x1, Pallas kernels, attention_back(): pl.pallas_call(back_kernel, in_specs=[HBM] + [WHOLE] * 12 + [HBM] * 7, ou...  85.5 us
  transfers between devices with their start and end apart: 3, of which 2 were waited for; matrix products, arithmetic and copies ran while one was open for 0% of the time, Pallas kernels for 0%

profile of v5, /device:TPU:0, one launch (start us, length us, event | category | flops | bytes accessed | tf_op | source)
XLA Modules:
  0.0 664.6 jit_solution(16309448444219250025)
XLA Ops:
  0.7 0.7 stack.18
  1.4 0.7 stack.19
  2.1 0.1 pad_maximum_fusion.3
  2.2 0.1 add_convert_fusion
  2.2 0.6 pad_maximum_fusion.2.gain_in
  2.8 0.2 multiply_cosine_fusion
  3.1 0.6 pad_maximum_fusion.rope_ref
  3.7 228.3 %attention_forward.1 = (bf16[256,2560]{1,0:T(8,128)(2,1)}, bf16[256,2560]{1,0:T(8,128)(2,1)}, f32[2048,128]{1,0:T(8,128)}, f32[2048,128]{1,0:T(8,128)}, s32[1,20...) custom-call(bf16[256,2560]{1,0:T(8,128)(2,1)} %x_ref.1, ...), custom_call_target="tpu_custom_call" | custom-call | flops 1000000 | bytes 100000 | tf_op jit(solution)/shard_map/attention_forward/pallas_call | solution.py:704
  232.0 131.7 %feed_forward.1 = (bf16[2048,896]{1,0:T(8,128)(2,1)}, bf16[2048,1792]{1,0:T(8,128)(2,1)}, bf16[2560,2688]{1,0:T(8,128)(2,1)}, bf16[2560,768]{1,0:T(8,128)(2,1)},...) custom-call(bf16[2048,2560]{1,0:T(8,128)(2,1)} %bitcast.15, ...), custom_call_target="tpu_custom_call" | custom-call | flops 1000000 | bytes 100000 | tf_op jit(solution)/shard_map/feed_forward/pallas_call | solution.py:893
  363.7 108.5 %feed_back.1 = (f32[256,2560]{1,0:T(8,128)}, bf16[8,256,2560]{2,1,0:T(8,128)(2,1)}, bf16[640,768]{1,0:T(8,128)(2,1)}, bf16[640,384]{1,0:T(8,128)(2,1)}) custom-call(bf16[8,256,1792]{2,1,0:T(8,128)(2,1)} %bitcast.16, bf16[2560,2688]{1,0:T(8,128)(2,1)} %get-tuple-element.76.w_ref.down_ref, bf16[256,2560]{1,0:T(8,128)(2,1)} %get-tuple-element.77.dout_ref, ...), custom_call_target="tpu_custom_call" | custom-call | flops 1000000 | bytes 100000 | tf_op jit(solution)/shard_map/feed_back/pallas_call | solution.py:1040
  472.2 85.5 %attention_back.1 = (bf16[8,256,512]{2,1,0:T(8,128)(2,1)}, bf16[256,2560]{1,0:T(8,128)(2,1)}, bf16[1280,640]{1,0:T(8,128)(2,1)}, bf16[640,768]{1,0:T(8,128)(2,1)...) custom-call(bf16[8,256,2560]{2,1,0:T(8,128)(2,1)} %get-tuple-element.83.da_ref, ...), custom_call_target="tpu_custom_call" | custom-call | flops 1000000 | bytes 100000 | tf_op jit(solution)/shard_map/attention_back/pallas_call | solution.py:1215
  557.7 88.7 %input_back.1 = (f32[256,2560]{1,0:T(8,128)}, bf16[640,512]{1,0:T(8,128)(2,1)}, bf16[640,320]{1,0:T(8,128)(2,1)}, bf16[320,768]{1,0:T(8,128)(2,1)}, bf16[320,512]{1,0:T(8,128)(2,1)}, /*index=5*/bf16[320,320]{1,0:T(8,128)(2,1)}) custom-call(bf16[8,256,512]{2,1,0:T(8,128)(2,1)} %get-tuple-element.100.a_ref, bf16[2560,512]{1,0:T(8,128)(2,1)} %get-tuple-element.101.w_ref, ...), custom_call_target="tpu_custom_call" | custom-call | flops 1000000 | bytes 100000 | tf_op jit(solution)/shard_map/input_back/pallas_call | solution.py:1335
  646.4 0.0 copy-start
  646.4 0.0 copy-start.1
  646.4 10.6 %finish.1 = (f32[320,1792]{1,0:T(8,128)}, f32[320,1792]{1,0:T(8,128)}, f32[320,1792]{1,0:T(8,128)}, f32[320,640]{1,0:T(8,128)}, f32[320,640]{1,0:T(8,128)}, /*in...) custom-call(s32[1]{0:T(128)} %bitcast.y_ref, ...), custom_call_target="tpu_custom_call" | custom-call | flops 1000000 | bytes 100000 | tf_op jit(solution)/shard_map/finish/pallas_call | solution.py:1419
  657.0 1.2 slice_reduce_fusion.1
  658.2 0.7 reshape_add_fusion
  658.9 1.7 collective-permute-start.1
  660.6 0.0 collective-permute-start.2
  660.6 0.5 collective-permute-start
  661.1 1.5 collective-permute-done.1
  662.6 1.1 collective-permute-done.2
  663.7 0.0 collective-permute-done
  663.7 0.0 copy-done
  663.7 0.0 copy-done.1
  663.7 0.6 convert_divide_fusion
  (8 shorter events, 0.1 us)
Async XLA Ops:
  646.4 17.3 %copy-start = (bf16[320]{0:T(512)(128)(2,1)S(1)}, bf16[320]{0:T(512)(128)(2,1)}, u32[]{:S(2)}) copy-start(bf16[320]{0:T(512)(128)(2,1)} %param.25) | copy-start | bytes 1924
  646.4 17.3 %copy-start.1 = (bf16[320]{0:T(512)(128)(2,1)S(1)}, bf16[320]{0:T(512)(128)(2,1)}, u32[]{:S(2)}) copy-start(bf16[320]{0:T(512)(128)(2,1)} %param.20) | copy-start | bytes 1924
  658.9 3.7 collective-permute-start.1
  660.6 3.0 collective-permute-start.2
  660.6 3.0 collective-permute-start

commit v6 on v5

--- a/solution.py
+++ b/solution.py
@@ -987,7 +987,7 @@
     wires = Wires(send, recv, local)
     wires.hello()
     load_w = wires.local(w_ref.at[:, 0 : w.shape[1]], w)
-    loads = {place: wires.local(a_ref.at[place], a.at[place]) for place in (7, 6, 3, 2, 5, 4, 1, 0)}
+    loads = {place: wires.local(a_ref.at[place], a.at[place]) for place in (7, 6)}
     wires.ready()
     rows = total0.shape[0]
     first = sum_along_z(
@@ -1008,6 +1008,8 @@
         block[rows, :] = dres.astype(BF16)
 
     load_w.wait()
+    for place in (3, 2, 5, 4, 1, 0):
+        loads[place] = wires.local(a_ref.at[place], a.at[place])
     sums = reduce_phase(
         wires, a, w, cs, cr, q, xr, yr, tr, br, emit, lambda place: loads[place].wait()
     )

time: 667 us -> 667 us (level)
  no operation moved by 1% of the time
where the time goes in v6:
time: 667 us; the launch traced here: 665 us
  Pallas kernels  653 us (98%)
    pallas_call x1, Pallas kernels, attention_forward(): pl.pallas_call(functools.partial(forward_kernel, hidden, cuts), in_specs=...  228 us
    pallas_call x1, Pallas kernels, feed_forward(): pl.pallas_call(functools.partial(feed_kernel, hidden, cuts, chunks), in_s...  132 us
    pallas_call x1, Pallas kernels, feed_back(): pl.pallas_call(middle_kernel, in_specs=[HBM] * 2 + [WHOLE] * 4 + [HBM] *...  109 us
    pallas_call x1, Pallas kernels, input_back(): pl.pallas_call(last_kernel, in_specs=[WHOLE] * 5 + [HBM] * 3, out_specs=[...  88.6 us
    pallas_call x1, Pallas kernels, attention_back(): pl.pallas_call(back_kernel, in_specs=[HBM] + [WHOLE] * 12 + [HBM] * 7, ou...  85.5 us
  transfers between devices with their start and end apart: 3, of which 2 were waited for; matrix products, arithmetic and copies ran while one was open for 0% of the time, Pallas kernels for 0%

profile of v6, /device:TPU:0, one launch (start us, length us, event | category | flops | bytes accessed | tf_op | source)
XLA Modules:
  0.0 664.5 jit_solution(554588581274494492)
XLA Ops:
  0.7 0.7 stack.18
  1.4 0.7 stack.19
  2.1 0.1 pad_maximum_fusion.3
  2.2 0.1 add_convert_fusion
  2.2 0.6 pad_maximum_fusion.2.gain_in
  2.8 0.2 multiply_cosine_fusion
  3.1 0.6 pad_maximum_fusion.rope_ref
  3.7 228.3 %attention_forward.1 = (bf16[256,2560]{1,0:T(8,128)(2,1)}, bf16[256,2560]{1,0:T(8,128)(2,1)}, f32[2048,128]{1,0:T(8,128)}, f32[2048,128]{1,0:T(8,128)}, s32[1,20...) custom-call(bf16[256,2560]{1,0:T(8,128)(2,1)} %x_ref.1, ...), custom_call_target="tpu_custom_call" | custom-call | flops 1000000 | bytes 100000 | tf_op jit(solution)/shard_map/attention_forward/pallas_call | solution.py:704
  232.0 131.7 %feed_forward.1 = (bf16[2048,896]{1,0:T(8,128)(2,1)}, bf16[2048,1792]{1,0:T(8,128)(2,1)}, bf16[2560,2688]{1,0:T(8,128)(2,1)}, bf16[2560,768]{1,0:T(8,128)(2,1)},...) custom-call(bf16[2048,2560]{1,0:T(8,128)(2,1)} %bitcast.15, ...), custom_call_target="tpu_custom_call" | custom-call | flops 1000000 | bytes 100000 | tf_op jit(solution)/shard_map/feed_forward/pallas_call | solution.py:893
  363.7 108.5 %feed_back.1 = (f32[256,2560]{1,0:T(8,128)}, bf16[8,256,2560]{2,1,0:T(8,128)(2,1)}, bf16[640,768]{1,0:T(8,128)(2,1)}, bf16[640,384]{1,0:T(8,128)(2,1)}) custom-call(bf16[8,256,1792]{2,1,0:T(8,128)(2,1)} %bitcast.16, bf16[2560,2688]{1,0:T(8,128)(2,1)} %get-tuple-element.76.w_ref.down_ref, bf16[256,2560]{1,0:T(8,128)(2,1)} %get-tuple-element.77.dout_ref, ...), custom_call_target="tpu_custom_call" | custom-call | flops 1000000 | bytes 100000 | tf_op jit(solution)/shard_map/feed_back/pallas_call | solution.py:1042
  472.2 85.5 %attention_back.1 = (bf16[8,256,512]{2,1,0:T(8,128)(2,1)}, bf16[256,2560]{1,0:T(8,128)(2,1)}, bf16[1280,640]{1,0:T(8,128)(2,1)}, bf16[640,768]{1,0:T(8,128)(2,1)...) custom-call(bf16[8,256,2560]{2,1,0:T(8,128)(2,1)} %get-tuple-element.83.da_ref, ...), custom_call_target="tpu_custom_call" | custom-call | flops 1000000 | bytes 100000 | tf_op jit(solution)/shard_map/attention_back/pallas_call | solution.py:1217
  557.7 88.6 %input_back.1 = (f32[256,2560]{1,0:T(8,128)}, bf16[640,512]{1,0:T(8,128)(2,1)}, bf16[640,320]{1,0:T(8,128)(2,1)}, bf16[320,768]{1,0:T(8,128)(2,1)}, bf16[320,512]{1,0:T(8,128)(2,1)}, /*index=5*/bf16[320,320]{1,0:T(8,128)(2,1)}) custom-call(bf16[8,256,512]{2,1,0:T(8,128)(2,1)} %get-tuple-element.100.a_ref, bf16[2560,512]{1,0:T(8,128)(2,1)} %get-tuple-element.101.w_ref, ...), custom_call_target="tpu_custom_call" | custom-call | flops 1000000 | bytes 100000 | tf_op jit(solution)/shard_map/input_back/pallas_call | solution.py:1337
  646.4 0.0 copy-start
  646.4 0.0 copy-start.1
  646.4 10.6 %finish.1 = (f32[320,1792]{1,0:T(8,128)}, f32[320,1792]{1,0:T(8,128)}, f32[320,1792]{1,0:T(8,128)}, f32[320,640]{1,0:T(8,128)}, f32[320,640]{1,0:T(8,128)}, /*in...) custom-call(s32[1]{0:T(128)} %bitcast.y_ref, ...), custom_call_target="tpu_custom_call" | custom-call | flops 1000000 | bytes 100000 | tf_op jit(solution)/shard_map/finish/pallas_call | solution.py:1421
  657.0 1.2 slice_reduce_fusion.1
  658.2 0.7 reshape_add_fusion
  658.9 1.7 collective-permute-start.1
  660.6 0.0 collective-permute-start.2
  660.6 0.5 collective-permute-start
  661.1 1.5 collective-permute-done.1
  662.6 1.0 collective-permute-done.2
  663.6 0.0 collective-permute-done
  663.7 0.0 copy-done
  663.7 0.0 copy-done.1
  663.7 0.6 convert_divide_fusion
  (8 shorter events, 0.1 us)
Async XLA Ops:
  646.4 17.3 %copy-start = (bf16[320]{0:T(512)(128)(2,1)S(1)}, bf16[320]{0:T(512)(128)(2,1)}, u32[]{:S(2)}) copy-start(bf16[320]{0:T(512)(128)(2,1)} %param.25) | copy-start | bytes 1924
  646.4 17.3 %copy-start.1 = (bf16[320]{0:T(512)(128)(2,1)S(1)}, bf16[320]{0:T(512)(128)(2,1)}, u32[]{:S(2)}) copy-start(bf16[320]{0:T(512)(128)(2,1)} %param.20) | copy-start | bytes 1924
  658.9 3.7 collective-permute-start.1
  660.6 3.0 collective-permute-start.2
  660.6 3.0 collective-permute-start
